TPU v7x, 512 devices: a whole 4x8x8 slice. The times are simulated.
512 devices in a mesh: seq: 64 (over x, y, core), fsdp: 4 (over z_hi), dp: 2 (over z_lo).
Axes of the slice: x: 4, y: 8, z: 8 (z_hi: 4, z_lo: 2; z = z_hi * 2 + z_lo), core: 2. Of those that a mesh axis runs over, the one named last changes fastest.
Arguments:
- qkv: bfloat16 [16384, 3, 4096], P(('dp', 'seq'), None, 'fsdp'), parts along dimension 0, may hold values from -6 to 6
- short_taps: float32 [3, 3, 4096], P(None, None, 'fsdp'), may hold values from -3 to 3
- lifetime: float32 [256, 16], P('fsdp'), may hold values from 30 to 163840
- residues: float32 [256, 16], P('fsdp'), may hold values from -1.5 to 1.5
- skip_gain: float32 [4096], P('fsdp'), may hold values from -4 to 4
- segment_starts: int32 [16], P('dp'), parts along dimension 0, may hold values from 0 to 8191, as said below
- out_weight: bfloat16 [4096, 4096], P('seq', 'fsdp'), may hold values from -0.09375 to 0.09375
Outputs:
- mixed: bfloat16 [16384, 4096], P(('dp', 'seq'), 'fsdp'), parts along dimension 0
There are 2 independent parts, one for each index of `dp`. A program takes and returns all parts, laid end to end along the dimension named above; an argument that names none is the same for every part. Nothing has to cross between parts.
Inputs may be any that keep to these rules, and one draw needn't show every extreme that they name: segment_starts[0] = 0 and the entries rise strictly; document j holds the positions from segment_starts[j] up to the next start (the last one up to 8191).
All inputs are finite; a program needn't handle non-finite values.
Results may differ from a plain program's by a relative error of at most 0.0049.
Values may be sent and summed in bfloat16 or wider, within the bound.
No kernel may reach another device: no remote copies, remote signals or barrier semaphores. Data moves between devices by JAX's collectives and lax.ppermute only.
A program may use at most 128 MiB of HBM per device.

v0:
```python
import jax
import jax.numpy as jnp
from jax import lax
from jax.sharding import PartitionSpec as P

GROUP = 16
SHORT = 3


def from_behind(x, axis, by):
    count = lax.axis_size(axis)
    pairs = [(i, i + by) for i in range(count) if 0 <= i + by < count]
    return lax.ppermute(x, axis, pairs)


def entering_2(value, axis, join, neutral):
    count, mine = (lax.axis_size(axis), lax.axis_index(axis))
    pieces = jax.tree.map(lambda part: lax.all_gather(part, axis), value)
    running = jax.tree.map(
        lambda part, zero: jnp.full_like(part, 0) + jnp.asarray(zero, part.dtype), value, neutral
    )

    def hop(position, running):
        longer = join(running, jax.tree.map(lambda part: part[position], pieces))
        return jax.tree.map(lambda new, old: jnp.where(position < mine, new, old), longer, running)

    return lax.fori_loop(0, count - 1, hop, running)


def segment_of(positions, starts):
    return jnp.sum((positions[:, None] >= starts[None, 1:]).astype(jnp.int32), axis=1)


def modal_terms(lifetime, residues, block_len):
    decay_rate = 1.0 / lifetime
    weighted = residues * jnp.sqrt(-jnp.expm1(-2.0 * decay_rate))
    offsets = jnp.arange(block_len).astype(jnp.float32)
    falling = jnp.exp(-decay_rate[:, :, None] * offsets[None, None, :])
    rising = jnp.exp(decay_rate[:, :, None] * offsets[None, None, :])
    kernel = jnp.einsum(
        "gmt,gms->gts", weighted[:, :, None] * falling, rising, precision=lax.Precision.HIGHEST
    )
    entering = weighted[:, :, None] * jnp.exp(
        -decay_rate[:, :, None] * (offsets[None, None, :] + 1.0)
    )
    leaving = jnp.exp(-decay_rate[:, :, None] * (block_len - 1.0 - offsets[None, None, :]))
    whole_gate = jnp.exp(-decay_rate * block_len)
    causal = (offsets[:, None] >= offsets[None, :]).astype(jnp.float32)
    return (kernel, entering, leaving, whole_gate, causal)


def block_local(kernel, leaving, whole_gate, causal, block_ids, block_vals, prev_id):
    linked = (block_ids[:, None] == block_ids[None, :]).astype(jnp.float32) * causal
    local = jnp.einsum(
        "gts,gcs->gct", kernel * linked[None], block_vals, precision=lax.Precision.HIGHEST
    )
    closing = (block_ids == block_ids[-1]).astype(jnp.float32)
    fresh = jnp.einsum(
        "gms,gcs->gmc",
        leaving * closing[None, None, :],
        block_vals,
        precision=lax.Precision.HIGHEST,
    )
    gate = whole_gate * (block_ids[-1] == prev_id).astype(jnp.float32)
    return (local, gate, fresh)


def block_carry(entering, block_ids, prev_id, state):
    joined = (block_ids == prev_id).astype(jnp.float32)
    return jnp.einsum(
        "gmt,gmc->gct", entering * joined[None, None, :], state, precision=lax.Precision.HIGHEST
    )


def combine_pairs(earlier, current):
    return (earlier[0] * current[0], current[0][:, :, None] * earlier[1] + current[1])


def on_device(qkv, short_taps, lifetime, residues, skip_gain, segment_starts, out_weight):
    tok_rows = qkv.shape[0]
    chans = qkv.shape[2]
    groups = chans // GROUP
    first_pos = lax.axis_index("seq") * tok_rows
    positions = first_pos + jnp.arange(tok_rows)
    seg_ids = segment_of(positions, segment_starts)
    rim_pos = first_pos - (SHORT - 1) + jnp.arange(SHORT - 1)
    rim_ids = jnp.where(rim_pos >= 0, segment_of(rim_pos, segment_starts), -1)
    rim_rows = from_behind(qkv[tok_rows - (SHORT - 1) :], "seq", 1)
    padded = jnp.concatenate([rim_rows, qkv], axis=0).astype(jnp.float32)
    padded_ids = jnp.concatenate([rim_ids, seg_ids])
    feats = jnp.zeros((tok_rows, 3, chans), jnp.float32)
    for offset in range(SHORT):
        begin = SHORT - 1 - offset
        shifted = padded[begin : begin + tok_rows]
        same_doc = (padded_ids[begin : begin + tok_rows] == seg_ids).astype(jnp.float32)
        feats = feats + short_taps[offset][None] * shifted * same_doc[:, None, None]
    query = feats[:, 0, :]
    product = feats[:, 1, :] * feats[:, 2, :]
    block_len = 128
    count_blocks = tok_rows // block_len
    kernel, entering, leaving, whole_gate, causal = modal_terms(lifetime, residues, block_len)
    blocks_vals = product.reshape(count_blocks, block_len, groups, GROUP).transpose(0, 2, 3, 1)
    prev_id = rim_ids[-1]
    number = 0
    local, gate, fresh = block_local(
        kernel, leaving, whole_gate, causal, seg_ids, blocks_vals[number], prev_id
    )
    local_list = [local]
    prev_list = [prev_id]
    identity = (jnp.ones_like(gate), jnp.zeros_like(fresh))
    scanned = entering_2((gate, fresh), "seq", combine_pairs, identity)
    state_in = scanned[1]
    number = 0
    carried = block_carry(entering, seg_ids, prev_list[number], state_in)
    results = [local_list[number] + carried]
    long_range = jnp.stack(results).transpose(0, 3, 1, 2).reshape(tok_rows, chans)
    gated = (query * (long_range + skip_gain[None, :] * product)).astype(jnp.bfloat16)
    every_channel = lax.all_gather(gated, "fsdp", axis=1, tiled=True)
    mixed = jnp.dot(
        every_channel,
        lax.all_gather(out_weight, "seq", axis=0, tiled=True),
        preferred_element_type=jnp.float32,
    )
    return mixed.astype(jnp.bfloat16)


def solution(mesh):
    return jax.shard_map(
        on_device,
        mesh=mesh,
        in_specs=(
            P(("dp", "seq"), None, "fsdp"),
            P(None, None, "fsdp"),
            P("fsdp", None),
            P("fsdp", None),
            P("fsdp"),
            P("dp"),
            P("seq", "fsdp"),
        ),
        out_specs=P(("dp", "seq"), "fsdp"),
        check_vma=False,
    )
```

profile of v0, /device:TPU:1, one launch (start us, length us, event | category | flops | bytes accessed | tf_op | source)
XLA Modules:
  0.0 412.7 jit_solution(1573999288877150768)
XLA Ops:
  7.4 4.6 %collective-permute-start = (bf16[2,3,1024]{2,0,1:T(2,128)(2,1)S(1)}, bf16[2,3,1024]{2,0,1:T(2,128)(2,1)S(1)}, u32[]{:S(2)}, u32[]{:S(2)}) collective-permute-start(bf16[2,3,1024]{2,0,1:T(2,128)(2,1)S(1)} %slice.48), channel_id=1, source_target_pairs={{0,8},{8,16},{16,24},{24,32},{32,40},{40,48},{48,56},{56,64},{64,7... | collective-permute-start | bytes 36872 | tf_op jit(solution)/shard_map/ppermute | solution.py:13
  15.6 1.3 compare_convert_fusion
  18.4 1.5 copy.30
  21.1 2.3 fusion.5
  23.5 1.9 fusion.18
  25.6 50.6 %all-gather.2 = f32[64,64,16]{1,2,0:T(8,128)S(1)} all-gather(f32[1,64,16]{1,2,0:T(8,128)S(1)} %get-tuple-element.154), channel_id=2, replica_groups=mesh['seq'=64,'fsdp'=4,'dp'=2] {'seq'}, dimensions={0}, use_global_device_ids=true | all-gather | bytes 266240 | tf_op jit(solution)/shard_map/all_gather | solution.py:18
  76.3 8.7 %fusion.22 = f32[64,128,128]{2,1,0:T(8,128)} fusion(f32[64,16]{1,0:T(8,128)S(1)} %copy.33, f32[128]{0:T(128)S(1)} %iota_convert_fusion, f32[64,16]{1,0:T(8,128)S(1)} %copy.32, f32[64,16]{1,0:T(8,128)S(1)} %copy.31), kind=kOutput, calls=%fused_computation.31 | convolution fusion | flops 201719808 | bytes 4207104 | tf_op jit(solution)/shard_map/gmt,gms->gts/dot_general | solution.py:40
  85.0 91.6 %all-gather.11.cloned.1.call-done = f32[4096,16,16]{2,1,0:T(8,128)} async-done(((f32[64,16,16]{2,1,0:T(8,128)}), f32[4096,16,16]{2,1,0:T(8,128)}) %all-gather.11.cloned.1.call-update) | async-done | bytes 4194320 | tf_op jit(solution)/shard_map/all_gather | solution.py:18
  176.6 22.6 %copy.34 = f32[64,64,16,16]{1,3,2,0:T(8,128)} copy(f32[64,64,16,16]{3,2,1,0:T(8,128)} %bitcast.49) | data formatting | bytes 8388608
  199.2 65.3 %while.14 = (s32[]{:T(128)}, f32[64,16,16]{0,2,1:T(8,128)S(1)}, s32[]{:T(128)}, f32[64,64,16]{1,2,0:T(8,128)S(1)}, f32[64,64,16,16]{1,3,2,0:T(8,128)}, /*index=5*/s32[]{:T(128)}, s32[]{:T(128)}) while((s32[]{:T(128)}, f32[64,16,16]{0,2,1:T(8,128)S(1)}, s32[]{:T(128)}, f32[64,64,16]{1,2,0:T(8,128)S(1)}, ...), condition=%wide.region_3.4_spmd.clone, body=%wide.region_2.3_spmd.clone.sunk | while | flops 65540 | bytes 209001 | solution.py:27
  200.2 1.0 fusion.47
  201.2 1.0 fusion.47
  202.3 1.0 fusion.47
  203.3 1.0 fusion.47
  204.4 1.0 fusion.47
  205.4 1.0 fusion.47
  206.4 1.0 fusion.47
  207.5 1.0 fusion.47
  208.5 1.0 fusion.47
  209.5 1.0 fusion.47
  210.6 1.0 fusion.47
  211.6 1.0 fusion.47
  212.7 1.0 fusion.47
  213.7 1.0 fusion.47
  214.7 1.0 fusion.47
  215.8 1.0 fusion.47
  216.8 1.0 fusion.47
  217.8 1.0 fusion.47
  218.9 1.0 fusion.47
  219.9 1.0 fusion.47
  221.0 1.0 fusion.47
  222.0 1.0 fusion.47
  223.0 1.0 fusion.47
  224.1 1.0 fusion.47
  225.1 1.0 fusion.47
  227.2 1.0 fusion.47
  229.3 1.0 fusion.47
  230.3 1.0 fusion.47
  232.4 1.0 fusion.47
  234.4 1.0 fusion.47
  235.5 1.0 fusion.47
  236.5 1.0 fusion.47
  237.6 1.0 fusion.47
  239.6 1.0 fusion.47
  241.7 1.0 fusion.47
  242.7 1.0 fusion.47
  243.8 1.0 fusion.47
  244.8 1.0 fusion.47
  246.9 1.0 fusion.47
  249.0 1.0 fusion.47
  250.0 1.0 fusion.47
  252.1 1.0 fusion.47
  254.2 1.0 fusion.47
  255.2 1.0 fusion.47
  256.2 1.0 fusion.47
  257.3 1.0 fusion.47
  259.3 1.0 fusion.47
  261.4 1.0 fusion.47
  262.4 1.0 fusion.47
  263.5 1.0 fusion.47
  265.6 8.3 %fusion.8 = f32[64,16,128]{2,1,0:T(8,128)S(1)} fusion(f32[64,16,128]{2,1,0:T(8,128)S(1)} %fusion.13, f32[64,16,128]{2,1,0:T(8,128)S(1)} %bitcast.51, f32[64,128,128]{2,1,0:T(8,128)} %fusion.22, f32[128,128]{1,0:T(8,128)S(1)} %convert_select_fusion), kind=kOutput, calls=%fused_computation.14 | convolution fusion | flops 202506240 | bytes 5832704 | tf_op jit(solution)/shard_map/gts,gcs->gct/dot_general | solution.py:54
  275.6 33.4 %all-gather.7.cloned.1.call-done = bf16[128,4096]{0,1:T(8,128)(2,1)} async-done(((bf16[128,1024]{0,1:T(8,128)(2,1)}), bf16[128,4096]{0,1:T(8,128)(2,1)}) %all-gather.7.cloned.1.call-update) | async-done | bytes 1048592 | tf_op jit(solution)/shard_map/all_gather | solution.py:118
  309.0 91.5 %all-gather.9.cloned.1.call-done = bf16[4096,1024]{1,0:T(8,128)(2,1)} async-done(((bf16[64,1024]{1,0:T(8,128)(2,1)}), bf16[4096,1024]{1,0:T(8,128)(2,1)}) %all-gather.9.cloned.1.call-update) | async-done | bytes 8388624 | tf_op jit(solution)/shard_map/all_gather | solution.py:121
  400.5 5.7 %convolution_convert_fusion = bf16[128,1024]{1,0:T(8,128)(2,1)} fusion(bf16[128,4096]{0,1:T(8,128)(2,1)} %all-gather.7.cloned.1.call-done, bf16[4096,1024]{1,0:T(8,128)(2,1)} %all-gather.9.cloned.1.call-done), kind=kOutput, calls=%fused_computation.15 | convolution fusion | flops 1073872896 | bytes 9699328 | tf_op jit(solution)/shard_map/dot_general | solution.py:119
  (111 shorter events, 22.4 us)
Async XLA Ops:
  6.5 170.0 %all-gather.11.cloned.1.call-start = ((), (), s32[]{:S(2)}) async-start(), calls=%async_computation.2 | async-start | bytes 34078720 | tf_op jit(solution)/shard_map/all_gather | solution.py:18
  7.4 12.7 %collective-permute-start = (bf16[2,3,1024]{2,0,1:T(2,128)(2,1)S(1)}, bf16[2,3,1024]{2,0,1:T(2,128)(2,1)S(1)}, u32[]{:S(2)}, u32[]{:S(2)}) collective-permute-start(bf16[2,3,1024]{2,0,1:T(2,128)(2,1)S(1)} %slice.48), channel_id=1, source_target_pairs={{0,8},{8,16},{16,24},{24,32},{32,40},{40,48},{48,56},{56,64},{64,7... | collective-permute-start | bytes 36872 | tf_op jit(solution)/shard_map/ppermute | solution.py:13
  25.4 283.7 %all-gather.7.cloned.1.call-start = ((), (), s32[]{:S(2)}) async-start(), calls=%async_computation | async-start | bytes 1310720 | tf_op jit(solution)/shard_map/all_gather | solution.py:118
  265.6 8.3 %copy-start = (f32[1024]{0:T(1024)S(1)}, f32[1024]{0:T(1024)}, u32[]{:S(2)}) copy-start(f32[1024]{0:T(1024)} %param.13) | copy-start | bytes 12292
  274.9 125.6 %all-gather.9.cloned.1.call-start = ((), (), s32[]{:S(2)}) async-start(), calls=%async_computation.1 | async-start | bytes 8519680 | tf_op jit(solution)/shard_map/all_gather | solution.py:121
Sparse Core Ops, SparseCore 0:
  25.5 151.0 all-gather.10
  275.0 33.9 all-gather.6
  312.4 88.0 all-gather.8
where the time goes:
time: 415 us; the launch traced here: 413 us
  waiting for transfers between devices  217 us (52%)
  other arithmetic  69.4 us (17%)
  blocking collectives  50.6 us (12%)
  local copies, waits for them, and re-layouts  29.1 us (7%)
  matrix products  25.3 us (6%)
  between operations  14.5 us (3%)
  starting transfers between devices  4.68 us (1%)
    all_gather x1, waiting for transfers between devices, entering_2(): pieces = jax.tree.map(lambda part: lax.all_gather(part, axis), value)  91.6 us
    all_gather x1, waiting for transfers between devices, on_device(): lax.all_gather(out_weight, 'seq', axis=0, tiled=True)  91.5 us
    select_n x63, other arithmetic, hop(): jnp.where(position < mine, new, old)  63 us
    all_gather x1, blocking collectives, entering_2(): pieces = jax.tree.map(lambda part: lax.all_gather(part, axis), value)  50.6 us
    all_gather x1, waiting for transfers between devices, on_device(): every_channel = lax.all_gather(gated, 'fsdp', axis=1, tiled=True)  33.4 us
    unnamed x4, local copies, waits for them, and re-layouts  24.1 us
    dot_general x1, matrix products, modal_terms(): jnp.einsum('gmt,gms->gts', weighted[:, :, None] * falling, rising, precis...  8.65 us
    dot_general x1, matrix products, block_local(): jnp.einsum('gts,gcs->gct', kernel * linked[None], block_vals, precision=l...  8.32 us
  transfers between devices with their start and end apart: 4, of which 3 were waited for; matrix products, arithmetic and copies ran while one was open for 4% of the time, Pallas kernels for 0%

commit v1 on v0

v1 whole, which is shorter than its diff:
```python
import jax
import jax.numpy as jnp
from jax import lax
from jax.experimental import pallas as pl
from jax.experimental.pallas import tpu as pltpu
from jax.sharding import PartitionSpec as P

GROUP = 16
MODES = 16
SHORT = 3
LANES = 128
PER_TILE = LANES // GROUP
F32 = jnp.float32
BF16 = jnp.bfloat16
ROOMY = pltpu.CompilerParams(vmem_limit_bytes=48 * 1024 * 1024)
SMEM = pl.BlockSpec(memory_space=pltpu.SMEM)
VMEM = pl.BlockSpec(memory_space=pltpu.VMEM)


def iota(shape, axis):
    return lax.broadcasted_iota(jnp.int32, shape, axis)


def segment_of(starts, positions):
    total = jnp.zeros(positions.shape, jnp.int32)
    for j in range(1, starts.shape[0]):
        total = total + (positions >= starts[j]).astype(jnp.int32)
    return total


def not_start(starts, positions):
    clear = jnp.ones(positions.shape, F32)
    for j in range(starts.shape[0]):
        clear = jnp.where(positions == starts[j], 0.0, clear)
    return clear


def halves(x):
    high = x.astype(BF16)
    return high, (x - high.astype(F32)).astype(BF16)


def split_dot(left, right):
    high, low = halves(right)
    upper = jnp.concatenate([high, low], axis=1)
    lower = jnp.concatenate([high, jnp.zeros_like(low)], axis=1)
    both = jnp.concatenate([upper, lower], axis=0)
    out = jnp.dot(left, both, preferred_element_type=F32)
    return out[:, :LANES] + out[:, LANES:]


def own_group():
    return (iota((PER_TILE, LANES), 0) == iota((PER_TILE, LANES), 1) // GROUP).astype(F32)


def prepare_kernel(starts, lifetime, residues, toeplitz, leaving, entering, decay):
    tile = pl.program_id(0)
    first = lax.axis_index("seq") * LANES
    rows = iota((LANES, LANES), 0)
    cols = iota((LANES, LANES), 1)
    seg_row = segment_of(starts, first + rows)
    seg_col = segment_of(starts, first + cols)
    linked = ((seg_row == seg_col) & (rows >= cols)).astype(F32)
    lane = iota((PER_TILE, LANES), 1)
    seg_lane = segment_of(starts, first + lane)
    last = segment_of(starts, jnp.full((PER_TILE, LANES), first + (LANES - 1)))
    before = jnp.where(first > 0, segment_of(starts, jnp.full((PER_TILE, LANES), first - 1)), -1)
    closing = (seg_lane == last).astype(F32)
    joined = (seg_lane == before).astype(F32)
    offset = lane.astype(F32)
    apart = jnp.where(lane == 0, 0, LANES - lane).astype(F32)
    own = own_group()

    rate = 1.0 / lifetime[...]
    double = 2.0 * rate
    series = double * (
        1.0
        - double
        * (0.5 - double * (1.0 / 6 - double * (1.0 / 24 - double * (1.0 / 120 - double * (1.0 / 720)))))
    )
    weight = residues[...] * jnp.sqrt(jnp.where(double < 0.07, series, 1.0 - jnp.exp(-double)))
    taps = jnp.zeros((PER_TILE, LANES), F32)
    leave_rows = []
    enter_rows = []
    for mode in range(MODES):
        r = jnp.broadcast_to(rate[:, mode : mode + 1], (PER_TILE, LANES))
        w = jnp.broadcast_to(weight[:, mode : mode + 1], (PER_TILE, LANES))
        taps = taps + w * jnp.exp(-r * apart)
        leave_rows.append(jnp.exp(-r * (LANES - 1.0 - offset)) * closing)
        enter_rows.append(w * jnp.exp(-r * (offset + 1.0)) * joined)
        whole = jnp.sum(jnp.exp(-r * LANES) * own, axis=0, keepdims=True)
        decay[4 * mode + tile // 2, pl.ds(tile % 2, 1), :] = whole
    high, low = halves(jnp.concatenate(leave_rows, axis=0))
    leaving[0, :, :LANES] = high
    leaving[0, :, LANES:] = low
    high, low = halves(jnp.concatenate(enter_rows, axis=0).T)
    entering[0, :, :LANES] = high
    entering[0, :, LANES:] = low
    for group in range(PER_TILE):
        spread = jnp.broadcast_to(taps[group : group + 1, :], (LANES, LANES))
        rolled = pltpu.roll(spread, 0, 1, stride=1, stride_axis=0)
        high, low = halves(rolled * linked)
        toeplitz[group, :, :LANES] = high
        toeplitz[group, :, LANES:] = low


def prepare(starts, lifetime, residues):
    tiles = lifetime.shape[0] // PER_TILE
    return pl.pallas_call(
        prepare_kernel,
        grid=(tiles,),
        in_specs=[
            SMEM,
            pl.BlockSpec((PER_TILE, MODES), lambda k: (k, 0)),
            pl.BlockSpec((PER_TILE, MODES), lambda k: (k, 0)),
        ],
        out_specs=[
            pl.BlockSpec((PER_TILE, LANES, 2 * LANES), lambda k: (k, 0, 0)),
            pl.BlockSpec((1, LANES, 2 * LANES), lambda k: (k, 0, 0)),
            pl.BlockSpec((1, LANES, 2 * LANES), lambda k: (k, 0, 0)),
            pl.BlockSpec((8 * tiles, 2, LANES), lambda k: (0, 0, 0)),
        ],
        out_shape=[
            jax.ShapeDtypeStruct((tiles * PER_TILE, LANES, 2 * LANES), BF16),
            jax.ShapeDtypeStruct((tiles, LANES, 2 * LANES), BF16),
            jax.ShapeDtypeStruct((tiles, LANES, 2 * LANES), BF16),
            jax.ShapeDtypeStruct((8 * tiles, 2, LANES), F32),
        ],
        compiler_params=ROOMY,
        name="prepare",
    )(starts, lifetime, residues)


def features_kernel(starts, qkv, rim, taps, leaving, query, product, fresh):
    tile = pl.program_id(0)
    first = lax.axis_index("seq") * LANES
    row = iota((LANES, LANES), 0)
    clear = not_start(starts, first + row)
    clear_before = clear * not_start(starts, first + row - 1)
    feats = []
    for kind in range(3):
        now = qkv[kind].astype(F32)
        edge = rim[kind].astype(F32)
        one = jnp.where(row == 0, edge[1:2, :], pltpu.roll(now, 1, 0))
        two = jnp.where(row == 0, edge[0:1, :], jnp.where(row == 1, edge[1:2, :], pltpu.roll(now, 2, 0)))
        feats.append(
            taps[0, kind : kind + 1, :] * now
            + taps[1, kind : kind + 1, :] * one * clear
            + taps[2, kind : kind + 1, :] * two * clear_before
        )
    query[...] = feats[0]
    values = feats[1] * feats[2]
    product[...] = values
    states = split_dot(leaving[0], values)
    own = own_group()
    for mode in range(MODES):
        some = states[mode * PER_TILE : (mode + 1) * PER_TILE, :] * own
        fresh[4 * mode + tile // 2, pl.ds(tile % 2, 1), :] = jnp.sum(some, axis=0, keepdims=True)


def features(starts, qkv, rim, taps, leaving):
    chans = qkv.shape[2]
    tiles = chans // LANES
    flat = pl.BlockSpec((LANES, LANES), lambda k: (0, k))
    return pl.pallas_call(
        features_kernel,
        grid=(tiles,),
        in_specs=[
            SMEM,
            pl.BlockSpec((3, LANES, LANES), lambda k: (0, 0, k)),
            pl.BlockSpec((3, SHORT - 1, LANES), lambda k: (0, 0, k)),
            pl.BlockSpec((SHORT, 3, LANES), lambda k: (0, 0, k)),
            pl.BlockSpec((1, LANES, 2 * LANES), lambda k: (k, 0, 0)),
        ],
        out_specs=[flat, flat, pl.BlockSpec((8 * tiles, 2, LANES), lambda k: (0, 0, 0))],
        out_shape=[
            jax.ShapeDtypeStruct((LANES, chans), F32),
            jax.ShapeDtypeStruct((LANES, chans), F32),
            jax.ShapeDtypeStruct((8 * tiles, 2, LANES), F32),
        ],
        compiler_params=ROOMY,
        name="features",
    )(starts, qkv, rim, taps, leaving)


def scan_kernel(starts, fresh, decay, entering):
    blocks = fresh.shape[0]
    whole = decay[lax.axis_index("seq")]
    gate = jnp.ones((blocks, 2, LANES), F32)
    number = iota((blocks, 2, LANES), 0)
    for j in range(1, starts.shape[0]):
        gate = jnp.where(number == starts[j] // LANES, 0.0, gate)
    state = jnp.zeros((2, LANES), F32)
    for block in range(blocks):
        entering[block] = state
        state = state * (whole * gate[block]) + fresh[block]


def scan_blocks(starts, fresh, decay):
    return pl.pallas_call(
        scan_kernel,
        in_specs=[SMEM, VMEM, VMEM],
        out_specs=VMEM,
        out_shape=jax.ShapeDtypeStruct(fresh.shape, F32),
        name="scan_blocks",
    )(starts, fresh, decay)


def gate_kernel(toeplitz, entering, query, product, skip, states, gated):
    tile = pl.program_id(0)
    values = product[...]
    lane_group = iota((LANES, LANES), 1) // GROUP
    own = own_group()
    spread = []
    for mode in range(MODES):
        state = states[4 * mode + tile // 2, pl.ds(tile % 2, 1), :]
        spread.append(jnp.broadcast_to(state, (PER_TILE, LANES)) * own)
    total = split_dot(entering[0], jnp.concatenate(spread, axis=0))
    high, low = halves(values)
    upper = jnp.concatenate([high, low], axis=1)
    lower = jnp.concatenate([high, jnp.zeros_like(low)], axis=1)
    both = jnp.concatenate([upper, lower], axis=0)
    local = jnp.zeros((LANES, LANES), F32)
    for group in range(PER_TILE):
        out = jnp.dot(toeplitz[group], both, preferred_element_type=F32)
        local = jnp.where(lane_group == group, out[:, :LANES] + out[:, LANES:], local)
    gated[...] = (query[...] * (local + total + skip[...] * values)).astype(BF16)


def gate(toeplitz, entering, query, product, skip, states):
    chans = query.shape[1]
    flat = pl.BlockSpec((LANES, LANES), lambda k: (0, k))
    return pl.pallas_call(
        gate_kernel,
        grid=(chans // LANES,),
        in_specs=[
            pl.BlockSpec((PER_TILE, LANES, 2 * LANES), lambda k: (k, 0, 0)),
            pl.BlockSpec((1, LANES, 2 * LANES), lambda k: (k, 0, 0)),
            flat,
            flat,
            pl.BlockSpec((1, LANES), lambda k: (0, k)),
            VMEM,
        ],
        out_specs=flat,
        out_shape=jax.ShapeDtypeStruct((LANES, chans), BF16),
        compiler_params=ROOMY,
        name="gate",
    )(toeplitz, entering, query, product, skip, states)


def project_kernel(order, mine, behind, ahead, across_top, across_low, weight, mixed, total):
    step = pl.program_id(0)

    def part(left):
        return jnp.dot(left, weight[...], preferred_element_type=F32)

    @pl.when(step == 0)
    def _():
        total[...] = part(mine[...])

    @pl.when(step == 1)
    def _():
        total[...] += part(behind[...])

    @pl.when(step == 2)
    def _():
        total[...] += part(ahead[...])

    @pl.when(step == 3)
    def _():
        across = jnp.concatenate([across_top[...], across_low[...]], axis=0)
        mixed[...] = (total[...] + part(across)).astype(BF16)


def project(order, pieces, weight):
    tokens, depth = pieces[0].shape
    width = weight.shape[1]
    whole = pl.BlockSpec((tokens, depth), lambda k, order: (0, 0))
    half = pl.BlockSpec((tokens // 2, depth), lambda k, order: (0, 0))
    return pl.pallas_call(
        project_kernel,
        grid_spec=pltpu.PrefetchScalarGridSpec(
            num_scalar_prefetch=1,
            grid=(4,),
            in_specs=[whole, whole, whole, half, half, pl.BlockSpec((depth, width), lambda k, order: (order[k], 0))],
            out_specs=pl.BlockSpec((tokens, width), lambda k, order: (0, 0)),
            scratch_shapes=[pltpu.VMEM((tokens, width), F32)],
        ),
        out_shape=jax.ShapeDtypeStruct((tokens, width), BF16),
        compiler_params=ROOMY,
        name="project",
    )(order, *pieces, weight)


def shifted(x, axis, by):
    count = lax.axis_size(axis)
    return lax.ppermute(x, axis, [(i, (i + by) % count) for i in range(count)])


def on_device(qkv, short_taps, lifetime, residues, skip_gain, segment_starts, out_weight):
    weight = lax.all_gather(out_weight, "seq", axis=0, tiled=True)
    kinds = jnp.transpose(qkv, (1, 0, 2))
    rim = shifted(kinds[:, -(SHORT - 1) :, :], "seq", 1)
    toeplitz, leaving, entering, decay = prepare(segment_starts, lifetime, residues)
    query, product, fresh = features(segment_starts, kinds, rim, short_taps, leaving)
    all_fresh = lax.all_to_all(fresh, "seq", 0, 0, tiled=True)
    all_states = scan_blocks(segment_starts, all_fresh, decay)
    states = lax.all_to_all(all_states, "seq", 0, 0, tiled=True)
    gated = gate(toeplitz, entering, query, product, skip_gain[None, :], states)
    behind = shifted(gated, "fsdp", 1)
    ahead = shifted(gated, "fsdp", -1)
    half = gated.shape[0] // 2
    across_top = shifted(behind[:half], "fsdp", 1)
    across_low = shifted(ahead[half:], "fsdp", -1)
    mine = lax.axis_index("fsdp")
    order = jnp.stack([mine, (mine + 3) % 4, (mine + 1) % 4, (mine + 2) % 4]).astype(jnp.int32)
    return project(order, [gated, behind, ahead, across_top, across_low], weight)


def solution(mesh):
    return jax.shard_map(
        on_device,
        mesh=mesh,
        in_specs=(
            P(("dp", "seq"), None, "fsdp"),
            P(None, None, "fsdp"),
            P("fsdp", None),
            P("fsdp", None),
            P("fsdp"),
            P("dp"),
            P("seq", "fsdp"),
        ),
        out_specs=P(("dp", "seq"), "fsdp"),
        check_vma=False,
    )
```

time: 415 us -> 119 us (0.29)
  waiting for transfers between devices: 217 us -> 14.6 us
  other arithmetic: 69.4 us -> 0.08 us
  matrix products: 25.3 us -> 0 us
  starting transfers between devices: 4.68 us -> 26.7 us
  local copies, waits for them, and re-layouts: 29.1 us -> 9.85 us
  Pallas kernels: 0 us -> 18.2 us
  blocking collectives: 50.6 us -> 35.1 us
    all_gather x3 -> x1, waiting for transfers between devices: 216 us -> 5.18 us  [on_device(): weight = lax.all_gather(out_weight, 'seq', axis=0, tiled=True)]
    select_n x64 -> x0, other arithmetic: 63 us -> none  [the longest x63 63 us: hop(): jnp.where(position < mine, new, old)]
    all_gather x1 -> x0, blocking collectives: 50.6 us -> none  [entering_2(): pieces = jax.tree.map(lambda part: lax.all_gather(part, axis), value)]
    all_to_all x0 -> x2, blocking collectives: none -> 35.1 us  [the longest x1 20.8 us: on_device(): all_fresh = lax.all_to_all(fresh, 'seq', 0, 0, tiled=True)]
    dot_general x5 -> x0, matrix products: 25.3 us -> none  [the longest x1 8.65 us: modal_terms(): jnp.einsum('gmt,gms->gts', weighted[:, :, None] * falling, rising, precis...]
    ppermute x1 -> x5, starting transfers between devices: 4.59 us -> 26.7 us  [shifted(): return lax.ppermute(x, axis, [(i, (i + by) % count) for i in range(count)])]
    pallas_call x0 -> x5, Pallas kernels: none -> 18.2 us  [the longest x1 6.15 us: project(): pl.pallas_call(project_kernel, grid_spec=pltpu.PrefetchScalarGridSpec(num...]
    unnamed x4 -> x16, local copies, waits for them, and re-layouts: 24.1 us -> 9.02 us
  transfers between devices with their start and end apart: 4 -> 6, of which waited for: 3 -> 3; matrix products, arithmetic and copies ran while one was open for 4% -> 2% of each run, Pallas kernels for 0% -> 10%
where the time goes in v1:
time: 119 us; the launch traced here: 118 us
  blocking collectives  35.1 us (29%)
  starting transfers between devices  26.7 us (22%)
  Pallas kernels  18.2 us (15%)
  waiting for transfers between devices  14.6 us (12%)
  between operations  13.5 us (11%)
  local copies, waits for them, and re-layouts  9.85 us (8%)
    ppermute x5, starting transfers between devices, shifted(): return lax.ppermute(x, axis, [(i, (i + by) % count) for i in range(count)])  26.7 us
    all_to_all x1, blocking collectives, on_device(): all_fresh = lax.all_to_all(fresh, 'seq', 0, 0, tiled=True)  20.8 us
    all_to_all x1, blocking collectives, on_device(): states = lax.all_to_all(all_states, 'seq', 0, 0, tiled=True)  14.3 us
    unnamed x16, local copies, waits for them, and re-layouts  9.02 us
    ppermute x5, waiting for transfers between devices, shifted(): return lax.ppermute(x, axis, [(i, (i + by) % count) for i in range(count)])  8.76 us
    pallas_call x1, Pallas kernels, project(): pl.pallas_call(project_kernel, grid_spec=pltpu.PrefetchScalarGridSpec(num...  6.15 us
    all_gather x1, waiting for transfers between devices, on_device(): weight = lax.all_gather(out_weight, 'seq', axis=0, tiled=True)  5.18 us
    pallas_call x1, Pallas kernels, prepare(): pl.pallas_call(prepare_kernel, grid=(tiles,), in_specs=[SMEM, pl.BlockSpe...  3.7 us
  transfers between devices with their start and end apart: 6, of which 3 were waited for; matrix products, arithmetic and copies ran while one was open for 2% of the time, Pallas kernels for 10%

profile of v1, /device:TPU:1, one launch (start us, length us, event | category | flops | bytes accessed | tf_op | source)
XLA Modules:
  0.0 118.1 jit_solution(3633814318181998207)
XLA Ops:
  6.5 0.0 all-gather.2.cloned.1.call-start
  6.5 0.7 all-gather.2.cloned.1.call-update
  7.3 0.8 slice.12
  8.1 4.6 %collective-permute-start = (bf16[3,2,1024]{2,1,0:T(2,128)(2,1)S(1)}, bf16[3,2,1024]{2,1,0:T(2,128)(2,1)S(1)}, u32[]{:S(2)}, u32[]{:S(2)}) collective-permute-start(bf16[3,2,1024]{2,1,0:T(2,128)(2,1)S(1)} %slice.12), channel_id=1, source_target_pairs={{0,8},{8,16},{16,24},{24,32},{32,40},{40,48},{48,56},{56,64},{64,7... | collective-permute-start | bytes 36872 | tf_op jit(solution)/shard_map/ppermute | solution.py:297
  12.7 0.8 copy.8.lifetime
  13.5 0.8 copy.9.residues
  14.2 0.0 copy-start.5
  14.2 0.7 copy-done.5
  14.9 3.7 %prepare.1 = (bf16[64,128,256]{2,1,0:T(8,128)(2,1)S(1)}, bf16[8,128,256]{2,1,0:T(8,128)(2,1)S(1)}, bf16[8,128,256]{2,1,0:T(8,128)(2,1)S(1)}, f32[64,2,128]{2,1,0:T(2,128)S(1)}) custom-call(s32[8]{0:T(128)S(1)} %copy-done.5, f32[64,16]{1,0:T(8,128)S(1)} %copy.8.lifetime, f32[64,16]{1,0:T(8,128)S(1)} %copy.9.residues), custom_call_target="tpu_custom_call" | custom-call | tf_op jit(solution)/shard_map/prepare/pallas_call | solution.py:109
  18.6 0.0 copy-start
  18.6 2.0 %copy-done = bf16[64,128,256]{2,1,0:T(8,128)(2,1)} copy-done((bf16[64,128,256]{2,1,0:T(8,128)(2,1)}, bf16[64,128,256]{2,1,0:T(8,128)(2,1)S(1)}, u32[]{:S(2)}) %copy-start) | copy-done | bytes 4194328
  20.6 0.0 copy-start.3
  20.6 0.0 collective-permute-done.rim
  20.6 0.0 copy-start.2
  20.6 1.2 copy-done.2
  21.7 0.0 copy-start.4
  21.7 0.8 copy-done.4
  22.5 3.7 %features.1 = (f32[128,1024]{1,0:T(8,128)S(1)}, f32[128,1024]{1,0:T(8,128)S(1)}, f32[64,2,128]{2,1,0:T(2,128)S(1)}) custom-call(s32[8]{0:T(128)S(1)} %copy-done.5, bf16[3,128,1024]{2,1,0:T(8,128)(2,1)S(1)} %bitcast.7, bf16[3,2,1024]{2,1,0:T(2,128)(2,1)S(1)} %collective-permute-done.rim, f32[3,3,1024]{2,1,0:T(4,128)S(1)} %copy-done.4, ...), custom_call_target="tpu_custom_call" | custom-call | tf_op jit(solution)/shard_map/features/pallas_call | solution.py:165
  26.2 0.0 copy-done.3
  26.2 20.8 %all_to_all.10.fresh = f32[64,2,128]{2,1,0:T(2,128)} all-to-all(f32[64,2,128]{2,1,0:T(2,128)S(1)} %get-tuple-element.17), channel_id=1, replica_groups=mesh['seq'=64,'fsdp'=4,'dp'=2] {'seq'}, dimensions={0} | all-to-all | bytes 131072 | tf_op jit(solution)/shard_map/all_to_all | solution.py:306
  47.0 1.7 %scan_blocks.1 = f32[64,2,128]{2,1,0:T(2,128)} custom-call(s32[8]{0:T(128)} %starts.5, f32[64,2,128]{2,1,0:T(2,128)} %all_to_all.10.fresh, f32[64,2,128]{2,1,0:T(2,128)} %copy-done.3), custom_call_target="tpu_custom_call" | custom-call | tf_op jit(solution)/shard_map/scan_blocks/pallas_call | solution.py:200
  48.7 14.3 %all_to_all.11.states = f32[64,2,128]{2,1,0:T(2,128)S(1)} all-to-all(f32[64,2,128]{2,1,0:T(2,128)} %scan_blocks.1), channel_id=1, replica_groups=mesh['seq'=64,'fsdp'=4,'dp'=2] {'seq'}, dimensions={0} | all-to-all | bytes 131072 | tf_op jit(solution)/shard_map/all_to_all | solution.py:308
  63.0 0.0 copy-start.1
  63.0 2.2 %copy-done.1 = bf16[64,128,256]{2,1,0:T(8,128)(2,1)S(1)} copy-done((bf16[64,128,256]{2,1,0:T(8,128)(2,1)S(1)}, bf16[64,128,256]{2,1,0:T(8,128)(2,1)}, u32[]{:S(2)}) %copy-start.1) | copy-done | bytes 4194328
  65.2 0.0 copy-start.6
  65.2 0.7 copy-done.6
  65.9 3.0 %gate.1.mine = bf16[128,1024]{1,0:T(8,128)(2,1)S(1)} custom-call(bf16[64,128,256]{2,1,0:T(8,128)(2,1)S(1)} %copy-done.1, bf16[8,128,256]{2,1,0:T(8,128)(2,1)S(1)} %get-tuple-element.13.entering, f32[128,1024]{1,0:T(8,128)S(1)} %get-tuple-element.15.query, f32[128,1024]{1,0:T(8,128)S(1)} %get-tuple-element.16.product, f32[1,1024]{1,0:T(1,128)S(1)} %bitcast.8, ...), custom_call_target="tpu_custom_call" | custom-call | tf_op jit(solution)/shard_map/gate/pallas_call | solution.py:233
  68.9 4.0 %collective-permute-start.1 = (bf16[128,1024]{1,0:T(8,128)(2,1)S(1)}, bf16[128,1024]{1,0:T(8,128)(2,1)S(1)}, u32[]{:S(2)}, u32[]{:S(2)}) collective-permute-start(bf16[128,1024]{1,0:T(8,128)(2,1)S(1)} %gate.1.mine), channel_id=1, source_target_pairs={{0,2},{2,4},{4,6},{6,0},{1,3},{3,5},{5,7},{7,1},{8,10},{10,12},{12... | collective-permute-start | bytes 786440 | tf_op jit(solution)/shard_map/ppermute | solution.py:297
  72.9 7.0 %collective-permute-start.2 = (bf16[128,1024]{1,0:T(8,128)(2,1)S(1)}, bf16[128,1024]{1,0:T(8,128)(2,1)S(1)}, u32[]{:S(2)}, u32[]{:S(2)}) collective-permute-start(bf16[128,1024]{1,0:T(8,128)(2,1)S(1)} %gate.1.mine), channel_id=1, source_target_pairs={{0,6},{2,0},{4,2},{6,4},{1,7},{3,1},{5,3},{7,5},{8,14},{10,8},{12,... | collective-permute-start | bytes 786440 | tf_op jit(solution)/shard_map/ppermute | solution.py:297
  79.9 4.8 %collective-permute-done.1.behind = bf16[128,1024]{1,0:T(8,128)(2,1)S(1)} collective-permute-done((bf16[128,1024]{1,0:T(8,128)(2,1)S(1)}, bf16[128,1024]{1,0:T(8,128)(2,1)S(1)}, u32[]{:S(2)}, u32[]{:S(2)}) %collective-permute-start.1) | collective-permute-done | bytes 262176 | tf_op jit(solution)/shard_map/ppermute | solution.py:297
  84.8 6.1 %collective-permute-start.3 = (bf16[64,1024]{1,0:T(8,128)(2,1)S(1)}, bf16[64,1024]{1,0:T(8,128)(2,1)S(1)}, u32[]{:S(2)}, u32[]{:S(2)}) collective-permute-start(bf16[64,1024]{1,0:T(8,128)(2,1)S(1)} %slice.13), channel_id=1, source_target_pairs={{0,2},{2,4},{4,6},{6,0},{1,3},{3,5},{5,7},{7,1},{8,10},{10,12},{12... | collective-permute-start | bytes 393224 | tf_op jit(solution)/shard_map/ppermute | solution.py:297
  90.9 0.0 collective-permute-done.2.ahead
  90.9 5.0 %collective-permute-start.4 = (bf16[64,1024]{1,0:T(8,128)(2,1)S(1)}, bf16[64,1024]{1,0:T(8,128)(2,1)S(1)}, u32[]{:S(2)}, u32[]{:S(2)}) collective-permute-start(bf16[64,1024]{1,0:T(8,128)(2,1)S(1)} %slice.14), channel_id=1, source_target_pairs={{0,6},{2,0},{4,2},{6,4},{1,7},{3,1},{5,3},{7,5},{8,14},{10,8},{12,... | collective-permute-start | bytes 393224 | tf_op jit(solution)/shard_map/ppermute | solution.py:297
  95.9 0.1 pad_add_fusion.order
  96.0 3.9 %collective-permute-done.3.across_top = bf16[64,1024]{1,0:T(8,128)(2,1)S(1)} collective-permute-done((bf16[64,1024]{1,0:T(8,128)(2,1)S(1)}, bf16[64,1024]{1,0:T(8,128)(2,1)S(1)}, u32[]{:S(2)}, u32[]{:S(2)}) %collective-permute-start.3) | collective-permute-done | bytes 131104 | tf_op jit(solution)/shard_map/ppermute | solution.py:297
  99.9 0.0 collective-permute-done.4.across_low
  99.9 5.2 %all-gather.2.cloned.1.call-done.weight = bf16[4096,1024]{1,0:T(8,128)(2,1)} async-done(((bf16[64,1024]{1,0:T(8,128)(2,1)}), bf16[4096,1024]{1,0:T(8,128)(2,1)}) %all-gather.2.cloned.1.call-update) | async-done | bytes 8388624 | tf_op jit(solution)/shard_map/all_gather | solution.py:301
  105.1 6.2 %project.1 = bf16[128,1024]{1,0:T(8,128)(2,1)} custom-call(s32[4]{0:T(128)S(1)} %pad_add_fusion.order, bf16[128,1024]{1,0:T(8,128)(2,1)S(1)} %gate.1.mine, bf16[128,1024]{1,0:T(8,128)(2,1)S(1)} %collective-permute-done.1.behind, bf16[128,1024]{1,0:T(8,128)(2,1)S(1)} %collective-permute-done.2.ahead, bf16[64,1024]{1,0:T(8,128)(2,1)S(1)} %collective-permute-done.3.across_top, ...), custom_call_target="tpu_custom_call" | custom-call | tf_op jit(solution)/shard_map/project/pallas_call | solution.py:280
  (2 shorter events, 0.0 us)
Async XLA Ops:
  6.5 98.6 %all-gather.2.cloned.1.call-start = ((), (), s32[]{:S(2)}) async-start(), calls=%async_computation.2 | async-start | bytes 8519680 | tf_op jit(solution)/shard_map/all_gather | solution.py:301
  8.1 12.5 %collective-permute-start = (bf16[3,2,1024]{2,1,0:T(2,128)(2,1)S(1)}, bf16[3,2,1024]{2,1,0:T(2,128)(2,1)S(1)}, u32[]{:S(2)}, u32[]{:S(2)}) collective-permute-start(bf16[3,2,1024]{2,1,0:T(2,128)(2,1)S(1)} %slice.12), channel_id=1, source_target_pairs={{0,8},{8,16},{16,24},{24,32},{32,40},{40,48},{48,56},{56,64},{64,7... | collective-permute-start | bytes 36872 | tf_op jit(solution)/shard_map/ppermute | solution.py:297
  14.2 0.7 copy-start.5
  18.6 2.0 %copy-start = (bf16[64,128,256]{2,1,0:T(8,128)(2,1)}, bf16[64,128,256]{2,1,0:T(8,128)(2,1)S(1)}, u32[]{:S(2)}) copy-start(bf16[64,128,256]{2,1,0:T(8,128)(2,1)S(1)} %get-tuple-element.12.toeplitz) | copy-start | bytes 12582916
  20.6 5.6 %copy-start.3 = (f32[64,2,128]{2,1,0:T(2,128)}, f32[64,2,128]{2,1,0:T(2,128)S(1)}, u32[]{:S(2)}) copy-start(f32[64,2,128]{2,1,0:T(2,128)S(1)} %get-tuple-element.18.decay) | copy-start | bytes 196612
  20.6 1.2 copy-start.2
  21.7 0.8 copy-start.4
  63.0 2.2 %copy-start.1 = (bf16[64,128,256]{2,1,0:T(8,128)(2,1)S(1)}, bf16[64,128,256]{2,1,0:T(8,128)(2,1)}, u32[]{:S(2)}) copy-start(bf16[64,128,256]{2,1,0:T(8,128)(2,1)} %copy-done) | copy-start | bytes 12582916
  65.2 0.7 copy-start.6
  68.9 15.9 %collective-permute-start.1 = (bf16[128,1024]{1,0:T(8,128)(2,1)S(1)}, bf16[128,1024]{1,0:T(8,128)(2,1)S(1)}, u32[]{:S(2)}, u32[]{:S(2)}) collective-permute-start(bf16[128,1024]{1,0:T(8,128)(2,1)S(1)} %gate.1.mine), channel_id=1, source_target_pairs={{0,2},{2,4},{4,6},{6,0},{1,3},{3,5},{5,7},{7,1},{8,10},{10,12},{12... | collective-permute-start | bytes 786440 | tf_op jit(solution)/shard_map/ppermute | solution.py:297
  72.9 17.9 %collective-permute-start.2 = (bf16[128,1024]{1,0:T(8,128)(2,1)S(1)}, bf16[128,1024]{1,0:T(8,128)(2,1)S(1)}, u32[]{:S(2)}, u32[]{:S(2)}) collective-permute-start(bf16[128,1024]{1,0:T(8,128)(2,1)S(1)} %gate.1.mine), channel_id=1, source_target_pairs={{0,6},{2,0},{4,2},{6,4},{1,7},{3,1},{5,3},{7,5},{8,14},{10,8},{12,... | collective-permute-start | bytes 786440 | tf_op jit(solution)/shard_map/ppermute | solution.py:297
  84.8 15.1 %collective-permute-start.3 = (bf16[64,1024]{1,0:T(8,128)(2,1)S(1)}, bf16[64,1024]{1,0:T(8,128)(2,1)S(1)}, u32[]{:S(2)}, u32[]{:S(2)}) collective-permute-start(bf16[64,1024]{1,0:T(8,128)(2,1)S(1)} %slice.13), channel_id=1, source_target_pairs={{0,2},{2,4},{4,6},{6,0},{1,3},{3,5},{5,7},{7,1},{8,10},{10,12},{12... | collective-permute-start | bytes 393224 | tf_op jit(solution)/shard_map/ppermute | solution.py:297
  90.9 9.0 %collective-permute-start.4 = (bf16[64,1024]{1,0:T(8,128)(2,1)S(1)}, bf16[64,1024]{1,0:T(8,128)(2,1)S(1)}, u32[]{:S(2)}, u32[]{:S(2)}) collective-permute-start(bf16[64,1024]{1,0:T(8,128)(2,1)S(1)} %slice.14), channel_id=1, source_target_pairs={{0,6},{2,0},{4,2},{6,4},{1,7},{3,1},{5,3},{7,5},{8,14},{10,8},{12,... | collective-permute-start | bytes 393224 | tf_op jit(solution)/shard_map/ppermute | solution.py:297
Sparse Core Ops, SparseCore 0:
  10.7 94.3 all-gather.1

commit v2 on v1

v2 whole, which is shorter than its diff:
```python
import jax
import jax.numpy as jnp
from jax import lax
from jax.experimental import pallas as pl
from jax.experimental.pallas import tpu as pltpu
from jax.sharding import PartitionSpec as P

GROUP = 16
MODES = 16
SHORT = 3
LANES = 128
PER_TILE = LANES // GROUP
F32 = jnp.float32
BF16 = jnp.bfloat16
ROOMY = pltpu.CompilerParams(vmem_limit_bytes=20 * 1024 * 1024)
SMEM = pl.BlockSpec(memory_space=pltpu.SMEM)
VMEM = pl.BlockSpec(memory_space=pltpu.VMEM)


def iota(shape, axis):
    return lax.broadcasted_iota(jnp.int32, shape, axis)


def segment_of(starts, positions):
    total = jnp.zeros(positions.shape, jnp.int32)
    for j in range(1, starts.shape[0]):
        total = total + (positions >= starts[j]).astype(jnp.int32)
    return total


def not_start(starts, positions):
    clear = jnp.ones(positions.shape, F32)
    for j in range(starts.shape[0]):
        clear = jnp.where(positions == starts[j], 0.0, clear)
    return clear


def halves(x):
    high = x.astype(BF16)
    return high, (x - high.astype(F32)).astype(BF16)


def doubled(right):
    high, low = halves(right)
    upper = jnp.concatenate([high, low], axis=1)
    lower = jnp.concatenate([high, jnp.zeros_like(low)], axis=1)
    return jnp.concatenate([upper, lower], axis=0)


def split_dot(left, both):
    out = jnp.dot(left, both, preferred_element_type=F32)
    return out[:, :LANES] + out[:, LANES:]


def own_group():
    return (iota((PER_TILE, LANES), 0) == iota((PER_TILE, LANES), 1) // GROUP).astype(F32)


def local_kernel(
    starts, lifetime, residues, qkv, rim, taps, skip, query, base, fresh, entering, decay
):
    tile = pl.program_id(0)
    first = lax.axis_index("seq") * LANES
    rows = iota((LANES, LANES), 0)
    cols = iota((LANES, LANES), 1)
    own = own_group()

    clear = not_start(starts, first + rows)
    clear_before = clear * not_start(starts, first + rows - 1)
    feats = []
    for kind in range(3):
        now = qkv[kind].astype(F32)
        edge = rim[kind].astype(F32)
        one = jnp.where(rows == 0, edge[1:2, :], pltpu.roll(now, 1, 0))
        two = jnp.where(rows == 0, edge[0:1, :], jnp.where(rows == 1, edge[1:2, :], pltpu.roll(now, 2, 0)))
        feats.append(
            taps[0, kind : kind + 1, :] * now
            + taps[1, kind : kind + 1, :] * one * clear
            + taps[2, kind : kind + 1, :] * two * clear_before
        )
    query[...] = feats[0]
    values = feats[1] * feats[2]

    seg_row = segment_of(starts, first + rows)
    seg_col = segment_of(starts, first + cols)
    linked = ((seg_row == seg_col) & (rows >= cols)).astype(F32)
    lane = iota((PER_TILE, LANES), 1)
    seg_lane = segment_of(starts, first + lane)
    last = segment_of(starts, jnp.full((PER_TILE, LANES), first + (LANES - 1)))
    before = jnp.where(first > 0, segment_of(starts, jnp.full((PER_TILE, LANES), first - 1)), -1)
    closing = (seg_lane == last).astype(F32)
    joined = (seg_lane == before).astype(F32)
    offset = lane.astype(F32)
    apart = jnp.where(lane == 0, 0, LANES - lane).astype(F32)

    rate = 1.0 / lifetime[...]
    double = 2.0 * rate
    series = double * (
        1.0
        - double
        * (0.5 - double * (1.0 / 6 - double * (1.0 / 24 - double * (1.0 / 120 - double * (1.0 / 720)))))
    )
    weight = residues[...] * jnp.sqrt(jnp.where(double < 0.07, series, 1.0 - jnp.exp(-double)))
    lags = jnp.zeros((PER_TILE, LANES), F32)
    leave_rows = []
    enter_rows = []
    for mode in range(MODES):
        r = jnp.broadcast_to(rate[:, mode : mode + 1], (PER_TILE, LANES))
        w = jnp.broadcast_to(weight[:, mode : mode + 1], (PER_TILE, LANES))
        lags = lags + w * jnp.exp(-r * apart)
        leave_rows.append(jnp.exp(-r * (LANES - 1.0 - offset)) * closing)
        enter_rows.append(w * jnp.exp(-r * (offset + 1.0)) * joined)
        whole = jnp.sum(jnp.exp(-r * LANES) * own, axis=0, keepdims=True)
        decay[4 * mode + tile // 2, pl.ds(tile % 2, 1), :] = whole
    both = doubled(values)
    high, low = halves(jnp.concatenate(leave_rows, axis=0))
    states = split_dot(jnp.concatenate([high, low], axis=1), both)
    for mode in range(MODES):
        some = states[mode * PER_TILE : (mode + 1) * PER_TILE, :] * own
        fresh[4 * mode + tile // 2, pl.ds(tile % 2, 1), :] = jnp.sum(some, axis=0, keepdims=True)
    high, low = halves(jnp.concatenate(enter_rows, axis=0).T)
    entering[0, :, :LANES] = high
    entering[0, :, LANES:] = low
    total = skip[...] * values
    for group in range(PER_TILE):
        spread = jnp.broadcast_to(lags[group : group + 1, :], (LANES, LANES))
        rolled = pltpu.roll(spread, 0, 1, stride=1, stride_axis=0)
        high, low = halves(rolled * linked)
        out = split_dot(jnp.concatenate([high, low], axis=1), both)
        total = total + jnp.where(cols // GROUP == group, out, 0.0)
    base[...] = total


def local_work(starts, lifetime, residues, qkv, rim, taps, skip):
    chans = qkv.shape[2]
    tiles = chans // LANES
    flat = pl.BlockSpec((LANES, LANES), lambda k: (0, k))
    small = pl.BlockSpec((PER_TILE, MODES), lambda k: (k, 0))
    whole = pl.BlockSpec((8 * tiles, 2, LANES), lambda k: (0, 0, 0))
    return pl.pallas_call(
        local_kernel,
        grid=(tiles,),
        in_specs=[
            SMEM,
            small,
            small,
            pl.BlockSpec((3, LANES, LANES), lambda k: (0, 0, k)),
            pl.BlockSpec((3, SHORT - 1, LANES), lambda k: (0, 0, k)),
            pl.BlockSpec((SHORT, 3, LANES), lambda k: (0, 0, k)),
            pl.BlockSpec((1, LANES), lambda k: (0, k)),
        ],
        out_specs=[flat, flat, whole, pl.BlockSpec((1, LANES, 2 * LANES), lambda k: (k, 0, 0)), whole],
        out_shape=[
            jax.ShapeDtypeStruct((LANES, chans), F32),
            jax.ShapeDtypeStruct((LANES, chans), F32),
            jax.ShapeDtypeStruct((8 * tiles, 2, LANES), F32),
            jax.ShapeDtypeStruct((tiles, LANES, 2 * LANES), BF16),
            jax.ShapeDtypeStruct((8 * tiles, 2, LANES), F32),
        ],
        compiler_params=ROOMY,
        name="local_work",
    )(starts, lifetime, residues, qkv, rim, taps, skip)


def scan_kernel(starts, fresh, decay, entering):
    blocks = fresh.shape[0]
    whole = decay[lax.axis_index("seq")]
    gate = jnp.ones((blocks, 2, LANES), F32)
    number = iota((blocks, 2, LANES), 0)
    for j in range(1, starts.shape[0]):
        gate = jnp.where(number == starts[j] // LANES, 0.0, gate)
    state = jnp.zeros((2, LANES), F32)
    for block in range(blocks):
        entering[block] = state
        state = state * (whole * gate[block]) + fresh[block]


def scan_blocks(starts, fresh, decay):
    return pl.pallas_call(
        scan_kernel,
        in_specs=[SMEM, VMEM, VMEM],
        out_specs=VMEM,
        out_shape=jax.ShapeDtypeStruct(fresh.shape, F32),
        name="scan_blocks",
    )(starts, fresh, decay)


def gate_kernel(entering, query, base, states, gated):
    tile = pl.program_id(0)
    own = own_group()
    spread = []
    for mode in range(MODES):
        state = states[4 * mode + tile // 2, pl.ds(tile % 2, 1), :]
        spread.append(jnp.broadcast_to(state, (PER_TILE, LANES)) * own)
    carried = split_dot(entering[0], doubled(jnp.concatenate(spread, axis=0)))
    gated[...] = (query[...] * (base[...] + carried)).astype(BF16)


def gate(entering, query, base, states):
    chans = query.shape[1]
    flat = pl.BlockSpec((LANES, LANES), lambda k: (0, k))
    return pl.pallas_call(
        gate_kernel,
        grid=(chans // LANES,),
        in_specs=[pl.BlockSpec((1, LANES, 2 * LANES), lambda k: (k, 0, 0)), flat, flat, VMEM],
        out_specs=flat,
        out_shape=jax.ShapeDtypeStruct((LANES, chans), BF16),
        compiler_params=ROOMY,
        name="gate",
    )(entering, query, base, states)


def project_kernel(order, mine, behind, ahead, across_top, across_low, weight, mixed, total):
    step = pl.program_id(0)

    def part(left):
        block = weight[...].reshape(left.shape[1], weight.shape[3])
        return jnp.dot(left, block, preferred_element_type=F32)

    @pl.when(step == 0)
    def _():
        total[...] = part(mine[...])

    @pl.when(step == 1)
    def _():
        total[...] += part(behind[...])

    @pl.when(step == 2)
    def _():
        total[...] += part(ahead[...])

    @pl.when(step == 3)
    def _():
        across = jnp.concatenate([across_top[...], across_low[...]], axis=0)
        mixed[...] = (total[...] + part(across)).astype(BF16)


def project(order, pieces, weight):
    tokens, depth = pieces[0].shape
    outer, planes, rows, width = weight.shape
    whole = pl.BlockSpec((tokens, depth), lambda k, order: (0, 0))
    half = pl.BlockSpec((tokens // 2, depth), lambda k, order: (0, 0))
    block = pl.BlockSpec((outer, 1, rows, width), lambda k, order: (0, order[k], 0, 0))
    return pl.pallas_call(
        project_kernel,
        grid_spec=pltpu.PrefetchScalarGridSpec(
            num_scalar_prefetch=1,
            grid=(planes,),
            in_specs=[whole, whole, whole, half, half, block],
            out_specs=pl.BlockSpec((tokens, width), lambda k, order: (0, 0)),
            scratch_shapes=[pltpu.VMEM((tokens, width), F32)],
        ),
        out_shape=jax.ShapeDtypeStruct((tokens, width), BF16),
        compiler_params=ROOMY,
        name="project",
    )(order, *pieces, weight)


def shifted(x, axis, by):
    count = lax.axis_size(axis)
    return lax.ppermute(x, axis, [(i, (i + by) % count) for i in range(count)])


PLANES = 4


def gather_weight(out_weight):
    count = lax.axis_size("seq")
    inner = count // PLANES
    rows, width = out_weight.shape
    parts = [out_weight] + [shifted(out_weight, "seq", inner * j) for j in range(1, PLANES)]
    column = jnp.concatenate(parts, axis=0)
    groups = [list(range(x * inner, (x + 1) * inner)) for x in range(PLANES)]
    whole = lax.all_gather(column, "seq", axis=0, tiled=True, axis_index_groups=groups)
    return whole.reshape(inner, PLANES, rows, width)


def on_device(qkv, short_taps, lifetime, residues, skip_gain, segment_starts, out_weight):
    kinds = jnp.transpose(qkv, (1, 0, 2))
    rim = shifted(kinds[:, -(SHORT - 1) :, :], "seq", 1)
    weight = gather_weight(out_weight)
    query, base, fresh, entering, decay = local_work(
        segment_starts, lifetime, residues, kinds, rim, short_taps, skip_gain[None, :]
    )
    all_fresh = lax.all_to_all(fresh, "seq", 0, 0, tiled=True)
    all_states = scan_blocks(segment_starts, all_fresh, decay)
    states = lax.all_to_all(all_states, "seq", 0, 0, tiled=True)
    gated = gate(entering, query, base, states)
    behind = shifted(gated, "fsdp", 1)
    ahead = shifted(gated, "fsdp", -1)
    half = gated.shape[0] // 2
    across_top = shifted(behind[:half], "fsdp", 1)
    across_low = shifted(ahead[half:], "fsdp", -1)
    mine = lax.axis_index("fsdp")
    plane = lax.axis_index("seq") // (lax.axis_size("seq") // PLANES)
    held = jnp.stack([mine, mine - 1, mine + 1, mine + 2])
    order = ((plane - held + 2 * PLANES) % PLANES).astype(jnp.int32)
    return project(order, [gated, behind, ahead, across_top, across_low], weight)


def solution(mesh):
    return jax.shard_map(
        on_device,
        mesh=mesh,
        in_specs=(
            P(("dp", "seq"), None, "fsdp"),
            P(None, None, "fsdp"),
            P("fsdp", None),
            P("fsdp", None),
            P("fsdp"),
            P("dp"),
            P("seq", "fsdp"),
        ),
        out_specs=P(("dp", "seq"), "fsdp"),
        check_vma=False,
    )
```

time: 119 us -> 130 us (1.092)
  the two profiles are of different devices: /device:TPU:1 before, /device:TPU:128 now
where the time goes in v2:
time: 130 us
  blocking collectives  32.8 us (25%)
  starting transfers between devices  31 us (24%)
  waiting for transfers between devices  27.6 us (21%)
  between operations  13.5 us (10%)
  Pallas kernels  13.2 us (10%)
  local copies, waits for them, and re-layouts  9.68 us (7%)
  other arithmetic  1.87 us (1%)
    ppermute x8, starting transfers between devices, shifted(): return lax.ppermute(x, axis, [(i, (i + by) % count) for i in range(count)])  31 us
    ppermute x8, waiting for transfers between devices, shifted(): return lax.ppermute(x, axis, [(i, (i + by) % count) for i in range(count)])  27.6 us
    all_to_all x1, blocking collectives, on_device(): all_fresh = lax.all_to_all(fresh, 'seq', 0, 0, tiled=True)  17.9 us
    all_to_all x1, blocking collectives, on_device(): states = lax.all_to_all(all_states, 'seq', 0, 0, tiled=True)  14.9 us
    unnamed x14, local copies, waits for them, and re-layouts  8.84 us
    pallas_call x1, Pallas kernels, local_work(): pl.pallas_call(local_kernel, grid=(tiles,), in_specs=[SMEM, small, small,...  6.02 us
    pallas_call x1, Pallas kernels, project(): pl.pallas_call(project_kernel, grid_spec=pltpu.PrefetchScalarGridSpec(num...  3.73 us
  transfers between devices with their start and end apart: 9, of which 6 were waited for; matrix products, arithmetic and copies ran while one was open for 2% of the time, Pallas kernels for 7%

profile of v2, /device:TPU:128, one launch (start us, length us, event | category | flops | bytes accessed | tf_op | source)
XLA Modules:
  0.0 129.7 jit_solution(12506401248430751689)
XLA Ops:
  6.5 0.0 all-gather.2.cloned.1.call-start
  6.5 3.4 %collective-permute-start.5 = (bf16[64,1024]{1,0:T(8,128)(2,1)}, bf16[64,1024]{1,0:T(8,128)(2,1)S(1)}, u32[]{:S(2)}, u32[]{:S(2)}) collective-permute-start(bf16[64,1024]{1,0:T(8,128)(2,1)} %param.13), channel_id=1, source_target_pairs={{0,128},{8,136},{16,144},{24,152},{32,160},{40,168},{48,176},{56,1... | collective-permute-start | bytes 393224 | tf_op jit(solution)/shard_map/ppermute | solution.py:261
  9.9 4.6 %collective-permute-start.6 = (bf16[64,1024]{1,0:T(8,128)(2,1)}, bf16[64,1024]{1,0:T(8,128)(2,1)S(1)}, u32[]{:S(2)}, u32[]{:S(2)}) collective-permute-start(bf16[64,1024]{1,0:T(8,128)(2,1)} %param.13), channel_id=1, source_target_pairs={{0,256},{8,264},{16,272},{24,280},{32,288},{40,296},{48,304},{56,3... | collective-permute-start | bytes 393224 | tf_op jit(solution)/shard_map/ppermute | solution.py:261
  14.6 3.3 %collective-permute-start.7 = (bf16[64,1024]{1,0:T(8,128)(2,1)}, bf16[64,1024]{1,0:T(8,128)(2,1)S(1)}, u32[]{:S(2)}, u32[]{:S(2)}) collective-permute-start(bf16[64,1024]{1,0:T(8,128)(2,1)} %param.13), channel_id=1, source_target_pairs={{0,384},{8,392},{16,400},{24,408},{32,416},{40,424},{48,432},{56,4... | collective-permute-start | bytes 393224 | tf_op jit(solution)/shard_map/ppermute | solution.py:261
  17.9 0.0 collective-permute-done.5
  17.9 0.9 collective-permute-done.6
  18.9 2.8 %collective-permute-done.7 = bf16[64,1024]{1,0:T(8,128)(2,1)S(1)} collective-permute-done((bf16[64,1024]{1,0:T(8,128)(2,1)}, bf16[64,1024]{1,0:T(8,128)(2,1)S(1)}, u32[]{:S(2)}, u32[]{:S(2)}) %collective-permute-start.7) | collective-permute-done | bytes 131104 | tf_op jit(solution)/shard_map/ppermute | solution.py:261
  21.6 1.8 %pad_maximum_fusion = bf16[256,1024]{1,0:T(8,128)(2,1)} fusion(bf16[64,1024]{1,0:T(8,128)(2,1)S(1)} %collective-permute-done.7, bf16[64,1024]{1,0:T(8,128)(2,1)S(1)} %collective-permute-done.6, bf16[64,1024]{1,0:T(8,128)(2,1)S(1)} %collective-permute-done.5, bf16[64,1024]{1,0:T(8,128)(2,1)} %param.13), kind=kLoop, calls=%fused_computation | loop fusion | flops 2097152 | bytes 1048576 | tf_op jit(solution)/shard_map/concatenate | solution.py:272
  23.4 0.0 all-gather.2.cloned.1.call-update
  23.5 0.8 slice.12
  24.3 1.9 %collective-permute-start = (bf16[3,2,1024]{2,1,0:T(2,128)(2,1)S(1)}, bf16[3,2,1024]{2,1,0:T(2,128)(2,1)S(1)}, u32[]{:S(2)}, u32[]{:S(2)}) collective-permute-start(bf16[3,2,1024]{2,1,0:T(2,128)(2,1)S(1)} %slice.12), channel_id=1, source_target_pairs={{0,8},{8,16},{16,24},{24,32},{32,40},{40,48},{48,56},{56,64},{64,7... | collective-permute-start | bytes 36872 | tf_op jit(solution)/shard_map/ppermute | solution.py:261
  26.2 0.8 copy.8.lifetime
  27.0 0.8 copy.9.residues
  27.8 4.8 %collective-permute-done.rim = bf16[3,2,1024]{2,1,0:T(2,128)(2,1)S(1)} collective-permute-done((bf16[3,2,1024]{2,1,0:T(2,128)(2,1)S(1)}, bf16[3,2,1024]{2,1,0:T(2,128)(2,1)S(1)}, u32[]{:S(2)}, u32[]{:S(2)}) %collective-permute-start) | collective-permute-done | bytes 12320 | tf_op jit(solution)/shard_map/ppermute | solution.py:261
  32.6 0.0 copy-start.1
  32.6 1.1 copy-done.1
  33.7 0.0 copy-start.3
  33.7 0.8 copy-done.3
  34.5 0.0 copy-start.4
  34.5 0.7 copy-done.4
  35.2 0.0 copy-start.5
  35.2 0.7 copy-done.5
  35.9 6.0 %local_work.1 = (f32[128,1024]{1,0:T(8,128)S(1)}, f32[128,1024]{1,0:T(8,128)S(1)}, f32[64,2,128]{2,1,0:T(2,128)S(1)}, bf16[8,128,256]{2,1,0:T(8,128)(2,1)S(1)}, f32[64,2,128]{2,1,0:T(2,128)S(1)}) custom-call(s32[8]{0:T(128)S(1)} %copy-done.5, f32[64,16]{1,0:T(8,128)S(1)} %copy.8.lifetime, f32[64,16]{1,0:T(8,128)S(1)} %copy.9.residues, ...), custom_call_target="tpu_custom_call" | custom-call | tf_op jit(solution)/shard_map/local_work/pallas_call | solution.py:140
  41.9 0.0 copy-start.2
  41.9 0.6 copy-done.2
  42.5 17.9 %all_to_all.10.fresh = f32[64,2,128]{2,1,0:T(2,128)} all-to-all(f32[64,2,128]{2,1,0:T(2,128)S(1)} %get-tuple-element.13), channel_id=1, replica_groups=mesh['seq'=64,'fsdp'=4,'dp'=2] {'seq'}, dimensions={0} | all-to-all | bytes 131072 | tf_op jit(solution)/shard_map/all_to_all | solution.py:285
  60.4 1.7 %scan_blocks.1 = f32[64,2,128]{2,1,0:T(2,128)} custom-call(s32[8]{0:T(128)} %starts.3, f32[64,2,128]{2,1,0:T(2,128)} %all_to_all.10.fresh, f32[64,2,128]{2,1,0:T(2,128)} %copy-done.2), custom_call_target="tpu_custom_call" | custom-call | tf_op jit(solution)/shard_map/scan_blocks/pallas_call | solution.py:179
  62.1 14.9 %all_to_all.11.states = f32[64,2,128]{2,1,0:T(2,128)S(1)} all-to-all(f32[64,2,128]{2,1,0:T(2,128)} %scan_blocks.1), channel_id=1, replica_groups=mesh['seq'=64,'fsdp'=4,'dp'=2] {'seq'}, dimensions={0} | all-to-all | bytes 131072 | tf_op jit(solution)/shard_map/all_to_all | solution.py:287
  77.0 1.8 %gate.1.mine = bf16[128,1024]{1,0:T(8,128)(2,1)S(1)} custom-call(bf16[8,128,256]{2,1,0:T(8,128)(2,1)S(1)} %get-tuple-element.10.entering, f32[128,1024]{1,0:T(8,128)S(1)} %get-tuple-element.11.query, f32[128,1024]{1,0:T(8,128)S(1)} %get-tuple-element.12.base, f32[64,2,128]{2,1,0:T(2,128)S(1)} %all_to_all.11.states), custom_call_target="tpu_custom_call" | custom-call | tf_op jit(solution)/shard_map/gate/pallas_call | solution.py:202
  78.8 7.3 %collective-permute-start.1 = (bf16[128,1024]{1,0:T(8,128)(2,1)S(1)}, bf16[128,1024]{1,0:T(8,128)(2,1)S(1)}, u32[]{:S(2)}, u32[]{:S(2)}) collective-permute-start(bf16[128,1024]{1,0:T(8,128)(2,1)S(1)} %gate.1.mine), channel_id=1, source_target_pairs={{0,2},{2,4},{4,6},{6,0},{1,3},{3,5},{5,7},{7,1},{8,10},{10,12},{12... | collective-permute-start | bytes 786440 | tf_op jit(solution)/shard_map/ppermute | solution.py:261
  86.1 1.9 %collective-permute-start.2 = (bf16[128,1024]{1,0:T(8,128)(2,1)S(1)}, bf16[128,1024]{1,0:T(8,128)(2,1)S(1)}, u32[]{:S(2)}, u32[]{:S(2)}) collective-permute-start(bf16[128,1024]{1,0:T(8,128)(2,1)S(1)} %gate.1.mine), channel_id=1, source_target_pairs={{0,6},{2,0},{4,2},{6,4},{1,7},{3,1},{5,3},{7,5},{8,14},{10,8},{12,... | collective-permute-start | bytes 786440 | tf_op jit(solution)/shard_map/ppermute | solution.py:261
  88.0 9.5 %collective-permute-done.1.behind = bf16[128,1024]{1,0:T(8,128)(2,1)S(1)} collective-permute-done((bf16[128,1024]{1,0:T(8,128)(2,1)S(1)}, bf16[128,1024]{1,0:T(8,128)(2,1)S(1)}, u32[]{:S(2)}, u32[]{:S(2)}) %collective-permute-start.1) | collective-permute-done | bytes 262176 | tf_op jit(solution)/shard_map/ppermute | solution.py:261
  97.5 6.6 %collective-permute-start.3 = (bf16[64,1024]{1,0:T(8,128)(2,1)S(1)}, bf16[64,1024]{1,0:T(8,128)(2,1)S(1)}, u32[]{:S(2)}, u32[]{:S(2)}) collective-permute-start(bf16[64,1024]{1,0:T(8,128)(2,1)S(1)} %slice.13), channel_id=1, source_target_pairs={{0,2},{2,4},{4,6},{6,0},{1,3},{3,5},{5,7},{7,1},{8,10},{10,12},{12... | collective-permute-start | bytes 393224 | tf_op jit(solution)/shard_map/ppermute | solution.py:261
  104.1 0.0 collective-permute-done.2.ahead
  104.1 1.9 %collective-permute-start.4 = (bf16[64,1024]{1,0:T(8,128)(2,1)S(1)}, bf16[64,1024]{1,0:T(8,128)(2,1)S(1)}, u32[]{:S(2)}, u32[]{:S(2)}) collective-permute-start(bf16[64,1024]{1,0:T(8,128)(2,1)S(1)} %slice.14), channel_id=1, source_target_pairs={{0,6},{2,0},{4,2},{6,4},{1,7},{3,1},{5,3},{7,5},{8,14},{10,8},{12,... | collective-permute-start | bytes 393224 | tf_op jit(solution)/shard_map/ppermute | solution.py:261
  106.1 0.1 and_select_fusion.order
  106.1 2.6 %collective-permute-done.3.across_top = bf16[64,1024]{1,0:T(8,128)(2,1)S(1)} collective-permute-done((bf16[64,1024]{1,0:T(8,128)(2,1)S(1)}, bf16[64,1024]{1,0:T(8,128)(2,1)S(1)}, u32[]{:S(2)}, u32[]{:S(2)}) %collective-permute-start.3) | collective-permute-done | bytes 131104 | tf_op jit(solution)/shard_map/ppermute | solution.py:261
  108.7 7.0 %collective-permute-done.4.across_low = bf16[64,1024]{1,0:T(8,128)(2,1)S(1)} collective-permute-done((bf16[64,1024]{1,0:T(8,128)(2,1)S(1)}, bf16[64,1024]{1,0:T(8,128)(2,1)S(1)}, u32[]{:S(2)}, u32[]{:S(2)}) %collective-permute-start.4) | collective-permute-done | bytes 131104 | tf_op jit(solution)/shard_map/ppermute | solution.py:261
  115.7 0.0 all-gather.2.cloned.1.call-done
  115.7 0.0 copy-start
  115.7 3.4 %copy-done = bf16[4096,1024]{1,0:T(8,128)(2,1)S(1)} copy-done((bf16[4096,1024]{1,0:T(8,128)(2,1)S(1)}, bf16[4096,1024]{1,0:T(8,128)(2,1)}, u32[]{:S(2)}) %copy-start) | copy-done | bytes 8388632
  119.1 3.7 %project.1 = bf16[128,1024]{1,0:T(8,128)(2,1)} custom-call(s32[4]{0:T(128)S(1)} %and_select_fusion.order, bf16[128,1024]{1,0:T(8,128)(2,1)S(1)} %gate.1.mine, bf16[128,1024]{1,0:T(8,128)(2,1)S(1)} %collective-permute-done.1.behind, bf16[128,1024]{1,0:T(8,128)(2,1)S(1)} %collective-permute-done.2.ahead, ...), custom_call_target="tpu_custom_call" | custom-call | tf_op jit(solution)/shard_map/project/pallas_call | solution.py:244
  (2 shorter events, 0.0 us)
Async XLA Ops:
  6.5 109.2 %all-gather.2.cloned.1.call-start = ((), (), s32[]{:S(2)}) async-start(), calls=%async_computation.2 | async-start | bytes 8912896 | tf_op jit(solution)/shard_map/all_gather | solution.py:274
  6.5 11.4 %collective-permute-start.5 = (bf16[64,1024]{1,0:T(8,128)(2,1)}, bf16[64,1024]{1,0:T(8,128)(2,1)S(1)}, u32[]{:S(2)}, u32[]{:S(2)}) collective-permute-start(bf16[64,1024]{1,0:T(8,128)(2,1)} %param.13), channel_id=1, source_target_pairs={{0,128},{8,136},{16,144},{24,152},{32,160},{40,168},{48,176},{56,1... | collective-permute-start | bytes 393224 | tf_op jit(solution)/shard_map/ppermute | solution.py:261
  9.9 8.9 %collective-permute-start.6 = (bf16[64,1024]{1,0:T(8,128)(2,1)}, bf16[64,1024]{1,0:T(8,128)(2,1)S(1)}, u32[]{:S(2)}, u32[]{:S(2)}) collective-permute-start(bf16[64,1024]{1,0:T(8,128)(2,1)} %param.13), channel_id=1, source_target_pairs={{0,256},{8,264},{16,272},{24,280},{32,288},{40,296},{48,304},{56,3... | collective-permute-start | bytes 393224 | tf_op jit(solution)/shard_map/ppermute | solution.py:261
  14.6 7.1 %collective-permute-start.7 = (bf16[64,1024]{1,0:T(8,128)(2,1)}, bf16[64,1024]{1,0:T(8,128)(2,1)S(1)}, u32[]{:S(2)}, u32[]{:S(2)}) collective-permute-start(bf16[64,1024]{1,0:T(8,128)(2,1)} %param.13), channel_id=1, source_target_pairs={{0,384},{8,392},{16,400},{24,408},{32,416},{40,424},{48,432},{56,4... | collective-permute-start | bytes 393224 | tf_op jit(solution)/shard_map/ppermute | solution.py:261
  24.3 8.3 %collective-permute-start = (bf16[3,2,1024]{2,1,0:T(2,128)(2,1)S(1)}, bf16[3,2,1024]{2,1,0:T(2,128)(2,1)S(1)}, u32[]{:S(2)}, u32[]{:S(2)}) collective-permute-start(bf16[3,2,1024]{2,1,0:T(2,128)(2,1)S(1)} %slice.12), channel_id=1, source_target_pairs={{0,8},{8,16},{16,24},{24,32},{32,40},{40,48},{48,56},{56,64},{64,7... | collective-permute-start | bytes 36872 | tf_op jit(solution)/shard_map/ppermute | solution.py:261
  32.6 1.1 copy-start.1
  33.7 0.8 copy-start.3
  34.5 0.7 copy-start.4
  35.2 0.7 copy-start.5
  41.9 0.6 copy-start.2
  78.8 18.7 %collective-permute-start.1 = (bf16[128,1024]{1,0:T(8,128)(2,1)S(1)}, bf16[128,1024]{1,0:T(8,128)(2,1)S(1)}, u32[]{:S(2)}, u32[]{:S(2)}) collective-permute-start(bf16[128,1024]{1,0:T(8,128)(2,1)S(1)} %gate.1.mine), channel_id=1, source_target_pairs={{0,2},{2,4},{4,6},{6,0},{1,3},{3,5},{5,7},{7,1},{8,10},{10,12},{12... | collective-permute-start | bytes 786440 | tf_op jit(solution)/shard_map/ppermute | solution.py:261
  86.1 18.0 %collective-permute-start.2 = (bf16[128,1024]{1,0:T(8,128)(2,1)S(1)}, bf16[128,1024]{1,0:T(8,128)(2,1)S(1)}, u32[]{:S(2)}, u32[]{:S(2)}) collective-permute-start(bf16[128,1024]{1,0:T(8,128)(2,1)S(1)} %gate.1.mine), channel_id=1, source_target_pairs={{0,6},{2,0},{4,2},{6,4},{1,7},{3,1},{5,3},{7,5},{8,14},{10,8},{12,... | collective-permute-start | bytes 786440 | tf_op jit(solution)/shard_map/ppermute | solution.py:261
  97.5 11.2 %collective-permute-start.3 = (bf16[64,1024]{1,0:T(8,128)(2,1)S(1)}, bf16[64,1024]{1,0:T(8,128)(2,1)S(1)}, u32[]{:S(2)}, u32[]{:S(2)}) collective-permute-start(bf16[64,1024]{1,0:T(8,128)(2,1)S(1)} %slice.13), channel_id=1, source_target_pairs={{0,2},{2,4},{4,6},{6,0},{1,3},{3,5},{5,7},{7,1},{8,10},{10,12},{12... | collective-permute-start | bytes 393224 | tf_op jit(solution)/shard_map/ppermute | solution.py:261
  104.1 11.6 %collective-permute-start.4 = (bf16[64,1024]{1,0:T(8,128)(2,1)S(1)}, bf16[64,1024]{1,0:T(8,128)(2,1)S(1)}, u32[]{:S(2)}, u32[]{:S(2)}) collective-permute-start(bf16[64,1024]{1,0:T(8,128)(2,1)S(1)} %slice.14), channel_id=1, source_target_pairs={{0,6},{2,0},{4,2},{6,4},{1,7},{3,1},{5,3},{7,5},{8,14},{10,8},{12,... | collective-permute-start | bytes 393224 | tf_op jit(solution)/shard_map/ppermute | solution.py:261
  115.7 3.4 %copy-start = (bf16[4096,1024]{1,0:T(8,128)(2,1)S(1)}, bf16[4096,1024]{1,0:T(8,128)(2,1)}, u32[]{:S(2)}) copy-start(bf16[4096,1024]{1,0:T(8,128)(2,1)} %all-gather.2.cloned.1.call-done) | copy-start | bytes 25165828
Sparse Core Ops, SparseCore 0:
  23.6 63.8 all-gather.1

commit v3 on v2

--- a/solution.py
+++ b/solution.py
@@ -12,7 +12,7 @@
 PER_TILE = LANES // GROUP
 F32 = jnp.float32
 BF16 = jnp.bfloat16
-ROOMY = pltpu.CompilerParams(vmem_limit_bytes=20 * 1024 * 1024)
+ROOMY = pltpu.CompilerParams(vmem_limit_bytes=60 * 1024 * 1024)
 SMEM = pl.BlockSpec(memory_space=pltpu.SMEM)
 VMEM = pl.BlockSpec(memory_space=pltpu.VMEM)
 
@@ -185,7 +185,7 @@
     )(starts, fresh, decay)
 
 
-def gate_kernel(entering, query, base, states, gated):
+def gate_kernel(entering, query, base, states, copies):
     tile = pl.program_id(0)
     own = own_group()
     spread = []
@@ -193,67 +193,59 @@
         state = states[4 * mode + tile // 2, pl.ds(tile % 2, 1), :]
         spread.append(jnp.broadcast_to(state, (PER_TILE, LANES)) * own)
     carried = split_dot(entering[0], doubled(jnp.concatenate(spread, axis=0)))
-    gated[...] = (query[...] * (base[...] + carried)).astype(BF16)
-
-
-def gate(entering, query, base, states):
+    gated = (query[...] * (base[...] + carried)).astype(BF16)
+    for copy in range(copies.shape[0]):
+        copies[copy] = gated
+
+
+def gate(entering, query, base, states, count):
     chans = query.shape[1]
     flat = pl.BlockSpec((LANES, LANES), lambda k: (0, k))
     return pl.pallas_call(
         gate_kernel,
         grid=(chans // LANES,),
         in_specs=[pl.BlockSpec((1, LANES, 2 * LANES), lambda k: (k, 0, 0)), flat, flat, VMEM],
-        out_specs=flat,
-        out_shape=jax.ShapeDtypeStruct((LANES, chans), BF16),
+        out_specs=pl.BlockSpec((count, LANES, LANES), lambda k: (0, 0, k)),
+        out_shape=jax.ShapeDtypeStruct((count, LANES, chans), BF16),
         compiler_params=ROOMY,
         name="gate",
     )(entering, query, base, states)
 
 
-def project_kernel(order, mine, behind, ahead, across_top, across_low, weight, mixed, total):
+def project_kernel(gated, weight, mixed, total):
     step = pl.program_id(0)
-
-    def part(left):
-        block = weight[...].reshape(left.shape[1], weight.shape[3])
-        return jnp.dot(left, block, preferred_element_type=F32)
+    block = weight[...].reshape(gated.shape[2], weight.shape[3])
+    part = jnp.dot(gated[0], block, preferred_element_type=F32)
 
     @pl.when(step == 0)
     def _():
-        total[...] = part(mine[...])
-
-    @pl.when(step == 1)
+        total[...] = part
+
+    @pl.when(step > 0)
     def _():
-        total[...] += part(behind[...])
-
-    @pl.when(step == 2)
+        total[...] += part
+
+    @pl.when(step == pl.num_programs(0) - 1)
     def _():
-        total[...] += part(ahead[...])
-
-    @pl.when(step == 3)
-    def _():
-        across = jnp.concatenate([across_top[...], across_low[...]], axis=0)
-        mixed[...] = (total[...] + part(across)).astype(BF16)
-
-
-def project(order, pieces, weight):
-    tokens, depth = pieces[0].shape
-    outer, planes, rows, width = weight.shape
-    whole = pl.BlockSpec((tokens, depth), lambda k, order: (0, 0))
-    half = pl.BlockSpec((tokens // 2, depth), lambda k, order: (0, 0))
-    block = pl.BlockSpec((outer, 1, rows, width), lambda k, order: (0, order[k], 0, 0))
+        mixed[...] = total[...].astype(BF16)
+
+
+def project(gated, weight):
+    planes, tokens, depth = gated.shape
+    outer, _, rows, width = weight.shape
     return pl.pallas_call(
         project_kernel,
-        grid_spec=pltpu.PrefetchScalarGridSpec(
-            num_scalar_prefetch=1,
-            grid=(planes,),
-            in_specs=[whole, whole, whole, half, half, block],
-            out_specs=pl.BlockSpec((tokens, width), lambda k, order: (0, 0)),
-            scratch_shapes=[pltpu.VMEM((tokens, width), F32)],
-        ),
+        grid=(planes,),
+        in_specs=[
+            pl.BlockSpec((1, tokens, depth), lambda k: (k, 0, 0)),
+            pl.BlockSpec((outer, 1, rows, width), lambda k: (0, k, 0, 0)),
+        ],
+        out_specs=pl.BlockSpec((tokens, width), lambda k: (0, 0)),
         out_shape=jax.ShapeDtypeStruct((tokens, width), BF16),
+        scratch_shapes=[pltpu.VMEM((tokens, width), F32)],
         compiler_params=ROOMY,
         name="project",
-    )(order, *pieces, weight)
+    )(gated, weight)
 
 
 def shifted(x, axis, by):
@@ -268,11 +260,11 @@
     count = lax.axis_size("seq")
     inner = count // PLANES
     rows, width = out_weight.shape
-    parts = [out_weight] + [shifted(out_weight, "seq", inner * j) for j in range(1, PLANES)]
-    column = jnp.concatenate(parts, axis=0)
-    groups = [list(range(x * inner, (x + 1) * inner)) for x in range(PLANES)]
-    whole = lax.all_gather(column, "seq", axis=0, tiled=True, axis_index_groups=groups)
-    return whole.reshape(inner, PLANES, rows, width)
+    lines = [list(range(j, count, inner)) for j in range(inner)]
+    copies = jnp.broadcast_to(out_weight[None], (PLANES, rows, width))
+    column = lax.all_to_all(copies, "seq", 0, 0, tiled=True, axis_index_groups=lines)
+    planes = [list(range(x * inner, (x + 1) * inner)) for x in range(PLANES)]
+    return lax.all_gather(column, "seq", axis=0, tiled=False, axis_index_groups=planes)
 
 
 def on_device(qkv, short_taps, lifetime, residues, skip_gain, segment_starts, out_weight):
@@ -285,17 +277,9 @@
     all_fresh = lax.all_to_all(fresh, "seq", 0, 0, tiled=True)
     all_states = scan_blocks(segment_starts, all_fresh, decay)
     states = lax.all_to_all(all_states, "seq", 0, 0, tiled=True)
-    gated = gate(entering, query, base, states)
-    behind = shifted(gated, "fsdp", 1)
-    ahead = shifted(gated, "fsdp", -1)
-    half = gated.shape[0] // 2
-    across_top = shifted(behind[:half], "fsdp", 1)
-    across_low = shifted(ahead[half:], "fsdp", -1)
-    mine = lax.axis_index("fsdp")
-    plane = lax.axis_index("seq") // (lax.axis_size("seq") // PLANES)
-    held = jnp.stack([mine, mine - 1, mine + 1, mine + 2])
-    order = ((plane - held + 2 * PLANES) % PLANES).astype(jnp.int32)
-    return project(order, [gated, behind, ahead, across_top, across_low], weight)
+    copies = gate(entering, query, base, states, PLANES)
+    gated = lax.all_to_all(copies, "fsdp", 0, 0, tiled=True)
+    return project(gated, weight)
 
 
 def solution(mesh):

time: 130 us -> 130 us (level)
  the two profiles are of different devices: /device:TPU:128 before, /device:TPU:64 now
where the time goes in v3:
time: 130 us; the launch traced here: 129 us
  blocking collectives  83.5 us (64%)
  Pallas kernels  21.3 us (16%)
  between operations  13.4 us (10%)
  local copies, waits for them, and re-layouts  5.12 us (4%)
  waiting for transfers between devices  3.67 us (3%)
  starting transfers between devices  1.92 us (1%)
    all_to_all x1, blocking collectives, on_device(): gated = lax.all_to_all(copies, 'fsdp', 0, 0, tiled=True)  37.6 us
    all_to_all x1, blocking collectives, on_device(): all_fresh = lax.all_to_all(fresh, 'seq', 0, 0, tiled=True)  16.8 us
    all_to_all x1, blocking collectives, on_device(): states = lax.all_to_all(all_states, 'seq', 0, 0, tiled=True)  15.4 us
    all_to_all x1, blocking collectives, gather_weight(): lax.all_to_all(copies, 'seq', 0, 0, tiled=True, axis_index_groups=lines)  13.7 us
    pallas_call x1, Pallas kernels, local_work(): pl.pallas_call(local_kernel, grid=(tiles,), in_specs=[SMEM, small, small,...  7.69 us
    pallas_call x1, Pallas kernels, project(): pl.pallas_call(project_kernel, grid=(planes,), in_specs=[pl.BlockSpec((1,...  5.98 us
    pallas_call x1, Pallas kernels, gate(): pl.pallas_call(gate_kernel, grid=(chans // LANES,), in_specs=[pl.BlockSpe...  5.98 us
    ppermute x1, waiting for transfers between devices, shifted(): return lax.ppermute(x, axis, [(i, (i + by) % count) for i in range(count)])  3.65 us
  transfers between devices with their start and end apart: 2, of which 1 were waited for; matrix products, arithmetic and copies ran while one was open for 3% of the time, Pallas kernels for 12%

profile of v3, /device:TPU:64, one launch (start us, length us, event | category | flops | bytes accessed | tf_op | source)
XLA Modules:
  0.0 128.9 jit_solution(16543804328478243470)
XLA Ops:
  6.5 0.0 all-gather.3.cloned.1.call-start
  6.5 1.0 broadcast_in_dim.10
  7.5 13.7 %all_to_all.20 = bf16[4,64,1024]{2,1,0:T(8,128)(2,1)} all-to-all(bf16[4,64,1024]{2,1,0:T(8,128)(2,1)S(1)} %broadcast_in_dim.10), channel_id=1, replica_groups={{0,128,256,384},{8,136,264,392},{16,144,272,400},{24,152,280,408},{32,1..., dimensions={0} | all-to-all | bytes 1048576 | tf_op jit(solution)/shard_map/all_to_all | solution.py:265
  21.2 0.0 all-gather.3.cloned.1.call-update
  21.2 0.8 slice.4
  22.0 1.9 %collective-permute-start = (bf16[3,2,1024]{2,1,0:T(2,128)(2,1)S(1)}, bf16[3,2,1024]{2,1,0:T(2,128)(2,1)S(1)}, u32[]{:S(2)}, u32[]{:S(2)}) collective-permute-start(bf16[3,2,1024]{2,1,0:T(2,128)(2,1)S(1)} %slice.4), channel_id=1, source_target_pairs={{0,8},{8,16},{16,24},{24,32},{32,40},{40,48},{48,56},{56,64},{64,7... | collective-permute-start | bytes 36872 | tf_op jit(solution)/shard_map/ppermute | solution.py:253
  23.9 1.4 %copy.10.lifetime = f32[64,16]{1,0:T(8,128)} copy(f32[64,16]{0,1:T(8,128)} %param.9) | data formatting | bytes 8192 | tf_op args[2]
  25.3 1.4 %copy.11.residues = f32[64,16]{1,0:T(8,128)} copy(f32[64,16]{0,1:T(8,128)} %param.10) | data formatting | bytes 8192 | tf_op args[3]
  26.7 3.6 %collective-permute-done.rim = bf16[3,2,1024]{2,1,0:T(2,128)(2,1)S(1)} collective-permute-done((bf16[3,2,1024]{2,1,0:T(2,128)(2,1)S(1)}, bf16[3,2,1024]{2,1,0:T(2,128)(2,1)S(1)}, u32[]{:S(2)}, u32[]{:S(2)}) %collective-permute-start) | collective-permute-done | bytes 12320 | tf_op jit(solution)/shard_map/ppermute | solution.py:253
  30.4 0.0 copy-start
  30.4 0.6 copy-done
  31.0 7.7 %local_work.1 = (f32[128,1024]{1,0:T(8,128)}, f32[128,1024]{1,0:T(8,128)}, f32[64,2,128]{2,1,0:T(2,128)}, bf16[8,128,256]{2,1,0:T(8,128)(2,1)}, f32[64,2,128]{2,1,0:T(2,128)}) custom-call(s32[8]{0:T(128)} %starts.3, f32[64,16]{1,0:T(8,128)} %copy.10.lifetime, f32[64,16]{1,0:T(8,128)} %copy.11.residues, bf16[3,128,1024]{2,1,0:T(8,128)(2,1)} %bitcast.5, ...), custom_call_target="tpu_custom_call" | custom-call | tf_op jit(solution)/shard_map/local_work/pallas_call | solution.py:140
  38.6 16.8 %all_to_all.21.fresh = f32[64,2,128]{2,1,0:T(2,128)} all-to-all(f32[64,2,128]{2,1,0:T(2,128)} %get-tuple-element.13), channel_id=1, replica_groups=mesh['seq'=64,'fsdp'=4,'dp'=2] {'seq'}, dimensions={0} | all-to-all | bytes 131072 | tf_op jit(solution)/shard_map/all_to_all | solution.py:277
  55.4 1.7 %scan_blocks.1 = f32[64,2,128]{2,1,0:T(2,128)} custom-call(s32[8]{0:T(128)} %starts.3, f32[64,2,128]{2,1,0:T(2,128)} %all_to_all.21.fresh, f32[64,2,128]{2,1,0:T(2,128)} %get-tuple-element.14.decay), custom_call_target="tpu_custom_call" | custom-call | tf_op jit(solution)/shard_map/scan_blocks/pallas_call | solution.py:179
  57.1 15.4 %all_to_all.22.states = f32[64,2,128]{2,1,0:T(2,128)} all-to-all(f32[64,2,128]{2,1,0:T(2,128)} %scan_blocks.1), channel_id=1, replica_groups=mesh['seq'=64,'fsdp'=4,'dp'=2] {'seq'}, dimensions={0} | all-to-all | bytes 131072 | tf_op jit(solution)/shard_map/all_to_all | solution.py:279
  72.5 6.0 %gate.1 = bf16[4,128,1024]{2,1,0:T(8,128)(2,1)} custom-call(bf16[8,128,256]{2,1,0:T(8,128)(2,1)} %get-tuple-element.10.entering, f32[128,1024]{1,0:T(8,128)} %get-tuple-element.11.query, f32[128,1024]{1,0:T(8,128)} %get-tuple-element.12.base, f32[64,2,128]{2,1,0:T(2,128)} %all_to_all.22.states), custom_call_target="tpu_custom_call" | custom-call | tf_op jit(solution)/shard_map/gate/pallas_call | solution.py:204
  78.5 37.6 %all_to_all.23.gated = bf16[4,128,1024]{2,1,0:T(8,128)(2,1)} all-to-all(bf16[4,128,1024]{2,1,0:T(8,128)(2,1)} %gate.1), channel_id=1, replica_groups=mesh['seq'=64,'fsdp'=4,'dp'=2] {'fsdp'}, dimensions={0} | all-to-all | bytes 2097152 | tf_op jit(solution)/shard_map/all_to_all | solution.py:281
  116.1 0.0 all-gather.3.cloned.1.call-done
  116.1 6.0 %project.1 = bf16[128,1024]{1,0:T(8,128)(2,1)} custom-call(bf16[4,128,1024]{2,1,0:T(8,128)(2,1)} %all_to_all.23.gated, bf16[16,4,64,1024]{3,2,1,0:T(8,128)(2,1)} %bitcast.3), custom_call_target="tpu_custom_call" | custom-call | tf_op jit(solution)/shard_map/project/pallas_call | solution.py:236
Async XLA Ops:
  6.5 109.6 %all-gather.3.cloned.1.call-start = ((), (), s32[]{:S(2)}) async-start(), calls=%async_computation.4 | async-start | bytes 8912896 | tf_op jit(solution)/shard_map/all_gather | solution.py:267
  22.0 8.3 %collective-permute-start = (bf16[3,2,1024]{2,1,0:T(2,128)(2,1)S(1)}, bf16[3,2,1024]{2,1,0:T(2,128)(2,1)S(1)}, u32[]{:S(2)}, u32[]{:S(2)}) collective-permute-start(bf16[3,2,1024]{2,1,0:T(2,128)(2,1)S(1)} %slice.4), channel_id=1, source_target_pairs={{0,8},{8,16},{16,24},{24,32},{32,40},{40,48},{48,56},{56,64},{64,7... | collective-permute-start | bytes 36872 | tf_op jit(solution)/shard_map/ppermute | solution.py:253
  30.4 0.6 copy-start
Sparse Core Ops, SparseCore 0:
  21.3 63.0 all-gather.2

commit v4 on v3

v4 whole, which is shorter than its diff:
```python
import jax
import jax.numpy as jnp
from jax import lax
from jax.experimental import pallas as pl
from jax.experimental.pallas import tpu as pltpu
from jax.sharding import PartitionSpec as P

GROUP = 16
MODES = 16
SHORT = 3
LANES = 128
PER_TILE = LANES // GROUP
F32 = jnp.float32
BF16 = jnp.bfloat16
ROOMY = pltpu.CompilerParams(vmem_limit_bytes=60 * 1024 * 1024)
SMEM = pl.BlockSpec(memory_space=pltpu.SMEM)
VMEM = pl.BlockSpec(memory_space=pltpu.VMEM)


def iota(shape, axis):
    return lax.broadcasted_iota(jnp.int32, shape, axis)


def segment_of(starts, positions):
    total = jnp.zeros(positions.shape, jnp.int32)
    for j in range(1, starts.shape[0]):
        total = total + (positions >= starts[j]).astype(jnp.int32)
    return total


def not_start(starts, positions):
    clear = jnp.ones(positions.shape, F32)
    for j in range(starts.shape[0]):
        clear = jnp.where(positions == starts[j], 0.0, clear)
    return clear


def halves(x):
    high = x.astype(BF16)
    return high, (x - high.astype(F32)).astype(BF16)


def doubled(right):
    high, low = halves(right)
    upper = jnp.concatenate([high, low], axis=1)
    lower = jnp.concatenate([high, jnp.zeros_like(low)], axis=1)
    return jnp.concatenate([upper, lower], axis=0)


def split_dot(left, both):
    out = jnp.dot(left, both, preferred_element_type=F32)
    return out[:, :LANES] + out[:, LANES:]


def own_group():
    return (iota((PER_TILE, LANES), 0) == iota((PER_TILE, LANES), 1) // GROUP).astype(F32)


def turned(x):
    wide = jnp.concatenate([x, jnp.zeros((x.shape[0], LANES - x.shape[1]), F32)], axis=1)
    return jnp.concatenate([wide, jnp.zeros((LANES - x.shape[0], LANES), F32)], axis=0).T


LOCAL_TILES = 2


def local_kernel(
    starts, lifetime, residues, qkv, rim, taps, skip, query, base, fresh, entering, decay, rates, weights
):
    step = pl.program_id(0)
    first = lax.axis_index("seq") * LANES
    rows = iota((LANES, LANES), 0)
    cols = iota((LANES, LANES), 1)
    own = own_group()

    @pl.when(step == 0)
    def _():
        rate = 1.0 / lifetime[...]
        double = 2.0 * rate
        series = double * (
            1.0
            - double
            * (0.5 - double * (1.0 / 6 - double * (1.0 / 24 - double * (1.0 / 120 - double * (1.0 / 720)))))
        )
        rates[...] = turned(rate)
        weights[...] = turned(residues[...] * jnp.sqrt(jnp.where(double < 0.07, series, 1.0 - jnp.exp(-double))))

    clear = not_start(starts, first + rows)
    clear_before = clear * not_start(starts, first + rows - 1)
    seg_row = segment_of(starts, first + rows)
    seg_col = segment_of(starts, first + cols)
    linked = ((seg_row == seg_col) & (rows >= cols)).astype(F32)
    lane = iota((PER_TILE, LANES), 1)
    seg_lane = seg_col[:PER_TILE]
    last = segment_of(starts, jnp.full((PER_TILE, LANES), first + (LANES - 1)))
    before = jnp.where(first > 0, segment_of(starts, jnp.full((PER_TILE, LANES), first - 1)), -1)
    closing = (seg_lane == last).astype(F32)
    joined = (seg_lane == before).astype(F32)
    offset = lane.astype(F32)
    apart = jnp.where(lane == 0, 0, LANES - lane).astype(F32)

    for part in range(LOCAL_TILES):
        tile = step * LOCAL_TILES + part
        span = slice(part * LANES, (part + 1) * LANES)
        feats = []
        for kind in range(3):
            now = qkv[kind, :, span].astype(F32)
            edge = rim[kind, :, span].astype(F32)
            one = jnp.where(rows == 0, edge[1:2, :], pltpu.roll(now, 1, 0))
            two = jnp.where(rows == 0, edge[0:1, :], jnp.where(rows == 1, edge[1:2, :], pltpu.roll(now, 2, 0)))
            feats.append(
                taps[0, kind : kind + 1, span] * now
                + taps[1, kind : kind + 1, span] * one * clear
                + taps[2, kind : kind + 1, span] * two * clear_before
            )
        query[:, span] = feats[0]
        values = feats[1] * feats[2]

        group_rows = pl.ds(pl.multiple_of(tile * PER_TILE, PER_TILE), PER_TILE)
        rate = rates[group_rows, :]
        weight = weights[group_rows, :]
        lags = jnp.zeros((PER_TILE, LANES), F32)
        leave_rows = []
        enter_rows = []
        for mode in range(MODES):
            r = jnp.broadcast_to(rate[:, mode : mode + 1], (PER_TILE, LANES))
            w = jnp.broadcast_to(weight[:, mode : mode + 1], (PER_TILE, LANES))
            lags = lags + w * jnp.exp(-r * apart)
            leave_rows.append(jnp.exp(-r * (LANES - 1.0 - offset)) * closing)
            enter_rows.append(w * jnp.exp(-r * (offset + 1.0)) * joined)
            whole = jnp.sum(jnp.exp(-r * LANES) * own, axis=0, keepdims=True)
            decay[4 * mode + tile // 2, pl.ds(tile % 2, 1), :] = whole
        both = doubled(values)
        high, low = halves(jnp.concatenate(leave_rows, axis=0))
        states = split_dot(jnp.concatenate([high, low], axis=1), both)
        for mode in range(MODES):
            some = states[mode * PER_TILE : (mode + 1) * PER_TILE, :] * own
            fresh[4 * mode + tile // 2, pl.ds(tile % 2, 1), :] = jnp.sum(some, axis=0, keepdims=True)
        high, low = halves(jnp.concatenate(enter_rows, axis=0).T)
        entering[part, :, :LANES] = high
        entering[part, :, LANES:] = low
        total = skip[:, span] * values
        for group in range(PER_TILE):
            spread = jnp.broadcast_to(lags[group : group + 1, :], (LANES, LANES))
            rolled = pltpu.roll(spread, 0, 1, stride=1, stride_axis=0)
            high, low = halves(rolled * linked)
            out = split_dot(jnp.concatenate([high, low], axis=1), both)
            total = total + jnp.where(cols // GROUP == group, out, 0.0)
        base[:, span] = total


def local_work(starts, lifetime, residues, qkv, rim, taps, skip):
    chans = qkv.shape[2]
    tiles = chans // LANES
    width = LOCAL_TILES * LANES
    flat = pl.BlockSpec((LANES, width), lambda k: (0, k))
    small = pl.BlockSpec(lifetime.shape, lambda k: (0, 0))
    whole = pl.BlockSpec((8 * tiles, 2, LANES), lambda k: (0, 0, 0))
    return pl.pallas_call(
        local_kernel,
        grid=(tiles // LOCAL_TILES,),
        in_specs=[
            SMEM,
            small,
            small,
            pl.BlockSpec((3, LANES, width), lambda k: (0, 0, k)),
            pl.BlockSpec((3, SHORT - 1, width), lambda k: (0, 0, k)),
            pl.BlockSpec((SHORT, 3, width), lambda k: (0, 0, k)),
            pl.BlockSpec((1, width), lambda k: (0, k)),
        ],
        out_specs=[
            flat,
            flat,
            whole,
            pl.BlockSpec((LOCAL_TILES, LANES, 2 * LANES), lambda k: (k, 0, 0)),
            whole,
        ],
        out_shape=[
            jax.ShapeDtypeStruct((LANES, chans), F32),
            jax.ShapeDtypeStruct((LANES, chans), F32),
            jax.ShapeDtypeStruct((8 * tiles, 2, LANES), F32),
            jax.ShapeDtypeStruct((tiles, LANES, 2 * LANES), BF16),
            jax.ShapeDtypeStruct((8 * tiles, 2, LANES), F32),
        ],
        scratch_shapes=[pltpu.VMEM((LANES, LANES), F32), pltpu.VMEM((LANES, LANES), F32)],
        compiler_params=ROOMY,
        name="local_work",
    )(starts, lifetime, residues, qkv, rim, taps, skip)


def scan_kernel(starts, fresh, decay, entering):
    blocks = fresh.shape[0]
    whole = decay[lax.axis_index("seq")]
    gate = jnp.ones((blocks, 2, LANES), F32)
    number = iota((blocks, 2, LANES), 0)
    for j in range(1, starts.shape[0]):
        gate = jnp.where(number == starts[j] // LANES, 0.0, gate)
    state = jnp.zeros((2, LANES), F32)
    for block in range(blocks):
        entering[block] = state
        state = state * (whole * gate[block]) + fresh[block]


def scan_blocks(starts, fresh, decay):
    return pl.pallas_call(
        scan_kernel,
        in_specs=[SMEM, VMEM, VMEM],
        out_specs=VMEM,
        out_shape=jax.ShapeDtypeStruct(fresh.shape, F32),
        name="scan_blocks",
    )(starts, fresh, decay)


GATE_TILES = 4


def gate_kernel(entering, query, base, states, copies):
    own = own_group()
    for part in range(GATE_TILES):
        tile = pl.program_id(0) * GATE_TILES + part
        span = slice(part * LANES, (part + 1) * LANES)
        spread = []
        for mode in range(MODES):
            state = states[4 * mode + tile // 2, pl.ds(tile % 2, 1), :]
            spread.append(jnp.broadcast_to(state, (PER_TILE, LANES)) * own)
        carried = split_dot(entering[part], doubled(jnp.concatenate(spread, axis=0)))
        gated = (query[:, span] * (base[:, span] + carried)).astype(BF16)
        for copy in range(copies.shape[0]):
            copies[copy, :, span] = gated


def gate(entering, query, base, states, count):
    chans = query.shape[1]
    width = GATE_TILES * LANES
    flat = pl.BlockSpec((LANES, width), lambda k: (0, k))
    return pl.pallas_call(
        gate_kernel,
        grid=(chans // width,),
        in_specs=[pl.BlockSpec((GATE_TILES, LANES, 2 * LANES), lambda k: (k, 0, 0)), flat, flat, VMEM],
        out_specs=pl.BlockSpec((count, LANES, width), lambda k: (0, 0, k)),
        out_shape=jax.ShapeDtypeStruct((count, LANES, chans), BF16),
        compiler_params=ROOMY,
        name="gate",
    )(entering, query, base, states)


def project_kernel(gated, weight, mixed, held, sems):
    planes = gated.shape[0]
    outer = weight.shape[0]
    half = outer // 2
    here = lax.axis_index("seq") // outer

    def copy(plane, part):
        some = pl.ds(part * half, half)
        return pltpu.make_async_copy(weight.at[some, plane], held.at[plane, some], sems.at[plane, part])

    for plane in range(planes):
        for part in range(2):
            copy(plane, part).start()
    depth = gated.shape[2] // 2
    total = jnp.zeros(mixed.shape, F32)
    for plane in range(planes):
        for part in range(2):
            copy(plane, part).wait()
            block = held[plane, part * half : (part + 1) * half].reshape(depth, mixed.shape[1])
            left = gated[lax.rem(here - plane + planes, planes), :, part * depth : (part + 1) * depth]
            total = total + jnp.dot(left, block, preferred_element_type=F32)
    mixed[...] = total.astype(BF16)


def project(gated, weight):
    planes, tokens, _ = gated.shape
    outer, _, rows, width = weight.shape
    return pl.pallas_call(
        project_kernel,
        in_specs=[VMEM, pl.BlockSpec(memory_space=pl.ANY)],
        out_specs=VMEM,
        out_shape=jax.ShapeDtypeStruct((tokens, width), BF16),
        scratch_shapes=[
            pltpu.VMEM((planes, outer, rows, width), BF16),
            pltpu.SemaphoreType.DMA((planes, 2)),
        ],
        compiler_params=ROOMY,
        name="project",
    )(gated, weight)


def shifted(x, axis, by):
    count = lax.axis_size(axis)
    return lax.ppermute(x, axis, [(i, (i + by) % count) for i in range(count)])


PLANES = 4


def on_device(qkv, short_taps, lifetime, residues, skip_gain, segment_starts, out_weight):
    kinds = jnp.transpose(qkv, (1, 0, 2))
    inner = lax.axis_size("seq") // PLANES
    edge, own_rows = lax.optimization_barrier((kinds[:, -(SHORT - 1) :, :], out_weight))
    arrived = [shifted(edge, "seq", 1)] + [shifted(own_rows, "seq", inner * j) for j in range(1, PLANES)]
    rim, *others = lax.optimization_barrier(arrived)
    column = jnp.concatenate([own_rows] + others, axis=0).reshape(PLANES, *out_weight.shape)
    groups = [list(range(x * inner, (x + 1) * inner)) for x in range(PLANES)]
    weight = lax.all_gather(column, "seq", axis=0, tiled=False, axis_index_groups=groups)

    query, base, fresh, entering, decay = local_work(
        segment_starts, lifetime.T, residues.T, kinds, rim, short_taps, skip_gain[None, :]
    )
    all_fresh = lax.all_to_all(fresh, "seq", 0, 0, tiled=True)
    all_states = scan_blocks(segment_starts, all_fresh, decay)
    states = lax.all_to_all(all_states, "seq", 0, 0, tiled=True)
    copies = gate(entering, query, base, states, PLANES)
    gated = lax.all_to_all(copies, "fsdp", 0, 0, tiled=True)
    return project(gated, weight)


def solution(mesh):
    return jax.shard_map(
        on_device,
        mesh=mesh,
        in_specs=(
            P(("dp", "seq"), None, "fsdp"),
            P(None, None, "fsdp"),
            P("fsdp", None),
            P("fsdp", None),
            P("fsdp"),
            P("dp"),
            P("seq", "fsdp"),
        ),
        out_specs=P(("dp", "seq"), "fsdp"),
        check_vma=False,
    )
```

time: 130 us -> 121 us (0.931)
  blocking collectives: 83.5 us -> 69.1 us
  starting transfers between devices: 1.92 us -> 13.3 us
  Pallas kernels: 21.3 us -> 15.8 us
  local copies, waits for them, and re-layouts: 5.12 us -> 0.82 us
  waiting for transfers between devices: 3.67 us -> 6.43 us
  other arithmetic: 0 us -> 1.76 us
    all_to_all x1 -> x0, blocking collectives: 13.7 us -> none  [gather_weight(): lax.all_to_all(copies, 'seq', 0, 0, tiled=True, axis_index_groups=lines)]
    ppermute x1 -> x4, starting transfers between devices: 1.92 us -> 13.3 us  [shifted(): return lax.ppermute(x, axis, [(i, (i + by) % count) for i in range(count)])]
    pallas_call x3, Pallas kernels: 19.6 us -> 14.2 us  [the longest x1 5.83 us: local_work(): pl.pallas_call(local_kernel, grid=(tiles // LOCAL_TILES,), in_specs=[SMEM...]
    unnamed x4 -> x2, local copies, waits for them, and re-layouts: 3.35 us -> 0.01 us
    ppermute x1 -> x4, waiting for transfers between devices: 3.65 us -> 6.41 us  [shifted(): return lax.ppermute(x, axis, [(i, (i + by) % count) for i in range(count)])]
    concatenate x0 -> x1, other arithmetic: none -> 1.76 us  [on_device(): jnp.concatenate([own_rows] + others, axis=0)]
  transfers between devices with their start and end apart: 2 -> 5, of which waited for: 1 -> 1; matrix products, arithmetic and copies ran while one was open for 3% -> 0% of each run, Pallas kernels for 12% -> 8%
where the time goes in v4:
time: 121 us
  blocking collectives  69.1 us (57%)
  Pallas kernels  15.8 us (13%)
  between operations  13.5 us (11%)
  starting transfers between devices  13.3 us (11%)
  waiting for transfers between devices  6.43 us (5%)
  other arithmetic  1.76 us (1%)
    all_to_all x1, blocking collectives, on_device(): gated = lax.all_to_all(copies, 'fsdp', 0, 0, tiled=True)  37.8 us
    all_to_all x1, blocking collectives, on_device(): all_fresh = lax.all_to_all(fresh, 'seq', 0, 0, tiled=True)  15.8 us
    all_to_all x1, blocking collectives, on_device(): states = lax.all_to_all(all_states, 'seq', 0, 0, tiled=True)  15.5 us
    ppermute x4, starting transfers between devices, shifted(): return lax.ppermute(x, axis, [(i, (i + by) % count) for i in range(count)])  13.3 us
    ppermute x4, waiting for transfers between devices, shifted(): return lax.ppermute(x, axis, [(i, (i + by) % count) for i in range(count)])  6.41 us
    pallas_call x1, Pallas kernels, local_work(): pl.pallas_call(local_kernel, grid=(tiles // LOCAL_TILES,), in_specs=[SMEM...  5.83 us
    pallas_call x1, Pallas kernels, project(): pl.pallas_call(project_kernel, in_specs=[VMEM, pl.BlockSpec(memory_space=...  5.72 us
    pallas_call x1, Pallas kernels, gate(): pl.pallas_call(gate_kernel, grid=(chans // width,), in_specs=[pl.BlockSpe...  2.62 us
  transfers between devices with their start and end apart: 5, of which 1 were waited for; matrix products, arithmetic and copies ran while one was open for 0% of the time, Pallas kernels for 8%

profile of v4, /device:TPU:64, one launch (start us, length us, event | category | flops | bytes accessed | tf_op | source)
XLA Modules:
  0.0 120.7 jit_solution(5350433862674748186)
XLA Ops:
  6.5 0.0 all-gather.2.cloned.1.call-start
  6.5 0.8 slice.4
  7.4 3.4 %collective-permute-start.1 = (bf16[64,1024]{1,0:T(8,128)(2,1)}, bf16[64,1024]{1,0:T(8,128)(2,1)S(1)}, u32[]{:S(2)}, u32[]{:S(2)}) collective-permute-start(bf16[64,1024]{1,0:T(8,128)(2,1)} %param.13), channel_id=1, source_target_pairs={{0,128},{8,136},{16,144},{24,152},{32,160},{40,168},{48,176},{56,1... | collective-permute-start | bytes 393224 | tf_op jit(solution)/shard_map/ppermute | solution.py:290
  10.8 4.6 %collective-permute-start.2 = (bf16[64,1024]{1,0:T(8,128)(2,1)}, bf16[64,1024]{1,0:T(8,128)(2,1)S(1)}, u32[]{:S(2)}, u32[]{:S(2)}) collective-permute-start(bf16[64,1024]{1,0:T(8,128)(2,1)} %param.13), channel_id=1, source_target_pairs={{0,256},{8,264},{16,272},{24,280},{32,288},{40,296},{48,304},{56,3... | collective-permute-start | bytes 393224 | tf_op jit(solution)/shard_map/ppermute | solution.py:290
  15.4 3.3 %collective-permute-start.3 = (bf16[64,1024]{1,0:T(8,128)(2,1)}, bf16[64,1024]{1,0:T(8,128)(2,1)S(1)}, u32[]{:S(2)}, u32[]{:S(2)}) collective-permute-start(bf16[64,1024]{1,0:T(8,128)(2,1)} %param.13), channel_id=1, source_target_pairs={{0,384},{8,392},{16,400},{24,408},{32,416},{40,424},{48,432},{56,4... | collective-permute-start | bytes 393224 | tf_op jit(solution)/shard_map/ppermute | solution.py:290
  18.8 1.9 %collective-permute-start = (bf16[3,2,1024]{2,1,0:T(2,128)(2,1)S(1)}, bf16[3,2,1024]{2,1,0:T(2,128)(2,1)S(1)}, u32[]{:S(2)}, u32[]{:S(2)}) collective-permute-start(bf16[3,2,1024]{2,1,0:T(2,128)(2,1)S(1)} %slice.4), channel_id=1, source_target_pairs={{0,8},{8,16},{16,24},{24,32},{32,40},{40,48},{48,56},{56,64},{64,7... | collective-permute-start | bytes 36872 | tf_op jit(solution)/shard_map/ppermute | solution.py:290
  20.7 6.4 %collective-permute-done.rim = bf16[3,2,1024]{2,1,0:T(2,128)(2,1)S(1)} collective-permute-done((bf16[3,2,1024]{2,1,0:T(2,128)(2,1)S(1)}, bf16[3,2,1024]{2,1,0:T(2,128)(2,1)S(1)}, u32[]{:S(2)}, u32[]{:S(2)}) %collective-permute-start) | collective-permute-done | bytes 12320 | tf_op jit(solution)/shard_map/ppermute | solution.py:290
  27.1 0.0 copy-start
  27.1 0.0 collective-permute-done.1
  27.1 0.0 collective-permute-done.2
  27.1 0.0 collective-permute-done.3
  27.1 1.8 %pad_maximum_fusion = bf16[256,1024]{1,0:T(8,128)(2,1)} fusion(bf16[64,1024]{1,0:T(8,128)(2,1)S(1)} %collective-permute-done.3, bf16[64,1024]{1,0:T(8,128)(2,1)S(1)} %collective-permute-done.2, bf16[64,1024]{1,0:T(8,128)(2,1)S(1)} %collective-permute-done.1, bf16[64,1024]{1,0:T(8,128)(2,1)} %param.13), kind=kLoop, calls=%fused_computation | loop fusion | flops 2097152 | bytes 1048576 | tf_op jit(solution)/shard_map/concatenate | solution.py:302
  28.9 0.0 all-gather.2.cloned.1.call-update
  28.9 0.0 copy-done
  28.9 5.8 %local_work.1 = (f32[128,1024]{1,0:T(8,128)}, f32[128,1024]{1,0:T(8,128)}, f32[64,2,128]{2,1,0:T(2,128)}, bf16[8,128,256]{2,1,0:T(8,128)(2,1)}, f32[64,2,128]{2,1,0:T(2,128)}) custom-call(s32[8]{0:T(128)} %starts.3, f32[16,64]{1,0:T(8,128)} %bitcast.8, f32[16,64]{1,0:T(8,128)} %bitcast.9, bf16[3,128,1024]{2,1,0:T(8,128)(2,1)} %bitcast.7, ...), custom_call_target="tpu_custom_call" | custom-call | tf_op jit(solution)/shard_map/local_work/pallas_call | solution.py:159
  34.7 15.8 %all_to_all.15.fresh = f32[64,2,128]{2,1,0:T(2,128)} all-to-all(f32[64,2,128]{2,1,0:T(2,128)} %get-tuple-element.22), channel_id=1, replica_groups=mesh['seq'=64,'fsdp'=4,'dp'=2] {'seq'}, dimensions={0} | all-to-all | bytes 131072 | tf_op jit(solution)/shard_map/all_to_all | solution.py:309
  50.6 1.7 %scan_blocks.1 = f32[64,2,128]{2,1,0:T(2,128)} custom-call(s32[8]{0:T(128)} %starts.3, f32[64,2,128]{2,1,0:T(2,128)} %all_to_all.15.fresh, f32[64,2,128]{2,1,0:T(2,128)} %get-tuple-element.23.decay), custom_call_target="tpu_custom_call" | custom-call | tf_op jit(solution)/shard_map/scan_blocks/pallas_call | solution.py:205
  52.3 15.5 %all_to_all.16.states = f32[64,2,128]{2,1,0:T(2,128)} all-to-all(f32[64,2,128]{2,1,0:T(2,128)} %scan_blocks.1), channel_id=1, replica_groups=mesh['seq'=64,'fsdp'=4,'dp'=2] {'seq'}, dimensions={0} | all-to-all | bytes 131072 | tf_op jit(solution)/shard_map/all_to_all | solution.py:311
  67.7 2.6 %gate.1 = bf16[4,128,1024]{2,1,0:T(8,128)(2,1)} custom-call(bf16[8,128,256]{2,1,0:T(8,128)(2,1)} %get-tuple-element.19.entering, f32[128,1024]{1,0:T(8,128)} %get-tuple-element.20.query, f32[128,1024]{1,0:T(8,128)} %get-tuple-element.21.base, f32[64,2,128]{2,1,0:T(2,128)} %all_to_all.16.states), custom_call_target="tpu_custom_call" | custom-call | tf_op jit(solution)/shard_map/gate/pallas_call | solution.py:236
  70.4 37.8 %all_to_all.17.gated = bf16[4,128,1024]{2,1,0:T(8,128)(2,1)} all-to-all(bf16[4,128,1024]{2,1,0:T(8,128)(2,1)} %gate.1), channel_id=1, replica_groups=mesh['seq'=64,'fsdp'=4,'dp'=2] {'fsdp'}, dimensions={0} | all-to-all | bytes 2097152 | tf_op jit(solution)/shard_map/all_to_all | solution.py:313
  108.2 0.0 all-gather.2.cloned.1.call-done.weight
  108.2 5.7 %project.1 = bf16[128,1024]{1,0:T(8,128)(2,1)} custom-call(bf16[4,128,1024]{2,1,0:T(8,128)(2,1)} %all_to_all.17.gated, bf16[16,4,64,1024]{3,2,1,0:T(8,128)(2,1)} %all-gather.2.cloned.1.call-done.weight), custom_call_target="tpu_custom_call" | custom-call | tf_op jit(solution)/shard_map/project/pallas_call | solution.py:274
Async XLA Ops:
  6.5 101.6 %all-gather.2.cloned.1.call-start = ((), (), s32[]{:S(2)}) async-start(), calls=%async_computation.3 | async-start | bytes 8912896 | tf_op jit(solution)/shard_map/all_gather | solution.py:304
  7.4 19.7 %collective-permute-start.1 = (bf16[64,1024]{1,0:T(8,128)(2,1)}, bf16[64,1024]{1,0:T(8,128)(2,1)S(1)}, u32[]{:S(2)}, u32[]{:S(2)}) collective-permute-start(bf16[64,1024]{1,0:T(8,128)(2,1)} %param.13), channel_id=1, source_target_pairs={{0,128},{8,136},{16,144},{24,152},{32,160},{40,168},{48,176},{56,1... | collective-permute-start | bytes 393224 | tf_op jit(solution)/shard_map/ppermute | solution.py:290
  10.8 16.3 %collective-permute-start.2 = (bf16[64,1024]{1,0:T(8,128)(2,1)}, bf16[64,1024]{1,0:T(8,128)(2,1)S(1)}, u32[]{:S(2)}, u32[]{:S(2)}) collective-permute-start(bf16[64,1024]{1,0:T(8,128)(2,1)} %param.13), channel_id=1, source_target_pairs={{0,256},{8,264},{16,272},{24,280},{32,288},{40,296},{48,304},{56,3... | collective-permute-start | bytes 393224 | tf_op jit(solution)/shard_map/ppermute | solution.py:290
  15.4 11.7 %collective-permute-start.3 = (bf16[64,1024]{1,0:T(8,128)(2,1)}, bf16[64,1024]{1,0:T(8,128)(2,1)S(1)}, u32[]{:S(2)}, u32[]{:S(2)}) collective-permute-start(bf16[64,1024]{1,0:T(8,128)(2,1)} %param.13), channel_id=1, source_target_pairs={{0,384},{8,392},{16,400},{24,408},{32,416},{40,424},{48,432},{56,4... | collective-permute-start | bytes 393224 | tf_op jit(solution)/shard_map/ppermute | solution.py:290
  18.8 8.3 %collective-permute-start = (bf16[3,2,1024]{2,1,0:T(2,128)(2,1)S(1)}, bf16[3,2,1024]{2,1,0:T(2,128)(2,1)S(1)}, u32[]{:S(2)}, u32[]{:S(2)}) collective-permute-start(bf16[3,2,1024]{2,1,0:T(2,128)(2,1)S(1)} %slice.4), channel_id=1, source_target_pairs={{0,8},{8,16},{16,24},{24,32},{32,40},{40,48},{48,56},{56,64},{64,7... | collective-permute-start | bytes 36872 | tf_op jit(solution)/shard_map/ppermute | solution.py:290
  27.1 1.8 %copy-start = (bf16[3,2,1024]{2,1,0:T(2,128)(2,1)}, bf16[3,2,1024]{2,1,0:T(2,128)(2,1)S(1)}, u32[]{:S(2)}) copy-start(bf16[3,2,1024]{2,1,0:T(2,128)(2,1)S(1)} %collective-permute-done.rim) | copy-start | bytes 36868
Sparse Core Ops, SparseCore 0:
  29.0 59.7 all-gather.1

commit v5 on v4

--- a/solution.py
+++ b/solution.py
@@ -1,3 +1,5 @@
+import functools
+
 import jax
 import jax.numpy as jnp
 from jax import lax
@@ -13,6 +15,7 @@
 F32 = jnp.float32
 BF16 = jnp.bfloat16
 ROOMY = pltpu.CompilerParams(vmem_limit_bytes=60 * 1024 * 1024)
+MODEST = pltpu.CompilerParams(vmem_limit_bytes=24 * 1024 * 1024)
 SMEM = pl.BlockSpec(memory_space=pltpu.SMEM)
 VMEM = pl.BlockSpec(memory_space=pltpu.VMEM)
 
@@ -61,16 +64,15 @@
     return jnp.concatenate([wide, jnp.zeros((LANES - x.shape[0], LANES), F32)], axis=0).T
 
 
-LOCAL_TILES = 2
-
-
-def local_kernel(
-    starts, lifetime, residues, qkv, rim, taps, skip, query, base, fresh, entering, decay, rates, weights
+FEATURE_TILES = 2
+
+
+def features_kernel(
+    starts, lifetime, residues, qkv, rim, taps, query, product, fresh, lags, entering, decay, rates, weights
 ):
     step = pl.program_id(0)
     first = lax.axis_index("seq") * LANES
     rows = iota((LANES, LANES), 0)
-    cols = iota((LANES, LANES), 1)
     own = own_group()
 
     @pl.when(step == 0)
@@ -87,11 +89,8 @@
 
     clear = not_start(starts, first + rows)
     clear_before = clear * not_start(starts, first + rows - 1)
-    seg_row = segment_of(starts, first + rows)
-    seg_col = segment_of(starts, first + cols)
-    linked = ((seg_row == seg_col) & (rows >= cols)).astype(F32)
     lane = iota((PER_TILE, LANES), 1)
-    seg_lane = seg_col[:PER_TILE]
+    seg_lane = segment_of(starts, first + lane)
     last = segment_of(starts, jnp.full((PER_TILE, LANES), first + (LANES - 1)))
     before = jnp.where(first > 0, segment_of(starts, jnp.full((PER_TILE, LANES), first - 1)), -1)
     closing = (seg_lane == last).astype(F32)
@@ -99,8 +98,8 @@
     offset = lane.astype(F32)
     apart = jnp.where(lane == 0, 0, LANES - lane).astype(F32)
 
-    for part in range(LOCAL_TILES):
-        tile = step * LOCAL_TILES + part
+    for part in range(FEATURE_TILES):
+        tile = step * FEATURE_TILES + part
         span = slice(part * LANES, (part + 1) * LANES)
         feats = []
         for kind in range(3):
@@ -115,50 +114,43 @@
             )
         query[:, span] = feats[0]
         values = feats[1] * feats[2]
+        product[:, span] = values
 
         group_rows = pl.ds(pl.multiple_of(tile * PER_TILE, PER_TILE), PER_TILE)
         rate = rates[group_rows, :]
         weight = weights[group_rows, :]
-        lags = jnp.zeros((PER_TILE, LANES), F32)
+        total = jnp.zeros((PER_TILE, LANES), F32)
         leave_rows = []
         enter_rows = []
         for mode in range(MODES):
             r = jnp.broadcast_to(rate[:, mode : mode + 1], (PER_TILE, LANES))
             w = jnp.broadcast_to(weight[:, mode : mode + 1], (PER_TILE, LANES))
-            lags = lags + w * jnp.exp(-r * apart)
+            total = total + w * jnp.exp(-r * apart)
             leave_rows.append(jnp.exp(-r * (LANES - 1.0 - offset)) * closing)
             enter_rows.append(w * jnp.exp(-r * (offset + 1.0)) * joined)
             whole = jnp.sum(jnp.exp(-r * LANES) * own, axis=0, keepdims=True)
             decay[4 * mode + tile // 2, pl.ds(tile % 2, 1), :] = whole
-        both = doubled(values)
+        lags[part * PER_TILE : (part + 1) * PER_TILE, :] = total
+        high, low = halves(jnp.concatenate(enter_rows, axis=0).T)
+        entering[part, :, :LANES] = high
+        entering[part, :, LANES:] = low
         high, low = halves(jnp.concatenate(leave_rows, axis=0))
-        states = split_dot(jnp.concatenate([high, low], axis=1), both)
+        states = split_dot(jnp.concatenate([high, low], axis=1), doubled(values))
         for mode in range(MODES):
             some = states[mode * PER_TILE : (mode + 1) * PER_TILE, :] * own
             fresh[4 * mode + tile // 2, pl.ds(tile % 2, 1), :] = jnp.sum(some, axis=0, keepdims=True)
-        high, low = halves(jnp.concatenate(enter_rows, axis=0).T)
-        entering[part, :, :LANES] = high
-        entering[part, :, LANES:] = low
-        total = skip[:, span] * values
-        for group in range(PER_TILE):
-            spread = jnp.broadcast_to(lags[group : group + 1, :], (LANES, LANES))
-            rolled = pltpu.roll(spread, 0, 1, stride=1, stride_axis=0)
-            high, low = halves(rolled * linked)
-            out = split_dot(jnp.concatenate([high, low], axis=1), both)
-            total = total + jnp.where(cols // GROUP == group, out, 0.0)
-        base[:, span] = total
-
-
-def local_work(starts, lifetime, residues, qkv, rim, taps, skip):
+
+
+def features(starts, lifetime, residues, qkv, rim, taps):
     chans = qkv.shape[2]
     tiles = chans // LANES
-    width = LOCAL_TILES * LANES
+    width = FEATURE_TILES * LANES
     flat = pl.BlockSpec((LANES, width), lambda k: (0, k))
     small = pl.BlockSpec(lifetime.shape, lambda k: (0, 0))
     whole = pl.BlockSpec((8 * tiles, 2, LANES), lambda k: (0, 0, 0))
     return pl.pallas_call(
-        local_kernel,
-        grid=(tiles // LOCAL_TILES,),
+        features_kernel,
+        grid=(chans // width,),
         in_specs=[
             SMEM,
             small,
@@ -166,26 +158,74 @@
             pl.BlockSpec((3, LANES, width), lambda k: (0, 0, k)),
             pl.BlockSpec((3, SHORT - 1, width), lambda k: (0, 0, k)),
             pl.BlockSpec((SHORT, 3, width), lambda k: (0, 0, k)),
-            pl.BlockSpec((1, width), lambda k: (0, k)),
         ],
         out_specs=[
             flat,
             flat,
             whole,
-            pl.BlockSpec((LOCAL_TILES, LANES, 2 * LANES), lambda k: (k, 0, 0)),
+            pl.BlockSpec((FEATURE_TILES * PER_TILE, LANES), lambda k: (k, 0)),
+            pl.BlockSpec((FEATURE_TILES, LANES, 2 * LANES), lambda k: (k, 0, 0)),
             whole,
         ],
         out_shape=[
             jax.ShapeDtypeStruct((LANES, chans), F32),
             jax.ShapeDtypeStruct((LANES, chans), F32),
             jax.ShapeDtypeStruct((8 * tiles, 2, LANES), F32),
+            jax.ShapeDtypeStruct((tiles * PER_TILE, LANES), F32),
             jax.ShapeDtypeStruct((tiles, LANES, 2 * LANES), BF16),
             jax.ShapeDtypeStruct((8 * tiles, 2, LANES), F32),
         ],
         scratch_shapes=[pltpu.VMEM((LANES, LANES), F32), pltpu.VMEM((LANES, LANES), F32)],
         compiler_params=ROOMY,
-        name="local_work",
-    )(starts, lifetime, residues, qkv, rim, taps, skip)
+        cost_estimate=pl.CostEstimate(flops=100_000_000, bytes_accessed=3_500_000, transcendentals=600_000),
+        name="features",
+    )(starts, lifetime, residues, qkv, rim, taps)
+
+
+BASE_TILES = 2
+
+
+def base_kernel(starts, lags, product, skip, base):
+    first = lax.axis_index("seq") * LANES
+    rows = iota((LANES, LANES), 0)
+    cols = iota((LANES, LANES), 1)
+    linked = (
+        (segment_of(starts, first + rows) == segment_of(starts, first + cols)) & (rows >= cols)
+    ).astype(F32)
+    for part in range(BASE_TILES):
+        span = slice(part * LANES, (part + 1) * LANES)
+        values = product[:, span]
+        both = doubled(values)
+        total = skip[:, span] * values
+        for group in range(PER_TILE):
+            at = part * PER_TILE + group
+            spread = jnp.broadcast_to(lags[at : at + 1, :], (LANES, LANES))
+            rolled = pltpu.roll(spread, 0, 1, stride=1, stride_axis=0)
+            high, low = halves(rolled * linked)
+            out = split_dot(jnp.concatenate([high, low], axis=1), both)
+            total = total + jnp.where(cols // GROUP == group, out, 0.0)
+        base[:, span] = total
+
+
+def base_work(starts, lags, product, skip):
+    chans = product.shape[1]
+    width = BASE_TILES * LANES
+    flat = pl.BlockSpec((LANES, width), lambda k: (0, k))
+    return pl.pallas_call(
+        base_kernel,
+        grid=(chans // width,),
+        in_specs=[
+            SMEM,
+            pl.BlockSpec((BASE_TILES * PER_TILE, LANES), lambda k: (k, 0)),
+            flat,
+            pl.BlockSpec((1, width), lambda k: (0, k)),
+        ],
+        out_specs=flat,
+        out_shape=jax.ShapeDtypeStruct((LANES, chans), F32),
+        compiler_params=MODEST,
+        cost_estimate=pl.CostEstimate(flops=1_100_000_000, bytes_accessed=1_100_000, transcendentals=0),
+        name="base_work",
+    )(starts, lags, product, skip)
 
 
 def scan_kernel(starts, fresh, decay, entering):
@@ -214,7 +254,7 @@
 GATE_TILES = 4
 
 
-def gate_kernel(entering, query, base, states, copies):
+def gate_kernel(entering, query, base, states, gated):
     own = own_group()
     for part in range(GATE_TILES):
         tile = pl.program_id(0) * GATE_TILES + part
@@ -224,12 +264,10 @@
             state = states[4 * mode + tile // 2, pl.ds(tile % 2, 1), :]
             spread.append(jnp.broadcast_to(state, (PER_TILE, LANES)) * own)
         carried = split_dot(entering[part], doubled(jnp.concatenate(spread, axis=0)))
-        gated = (query[:, span] * (base[:, span] + carried)).astype(BF16)
-        for copy in range(copies.shape[0]):
-            copies[copy, :, span] = gated
-
-
-def gate(entering, query, base, states, count):
+        gated[:, span] = (query[:, span] * (base[:, span] + carried)).astype(BF16)
+
+
+def gate(entering, query, base, states):
     chans = query.shape[1]
     width = GATE_TILES * LANES
     flat = pl.BlockSpec((LANES, width), lambda k: (0, k))
@@ -237,52 +275,62 @@
         gate_kernel,
         grid=(chans // width,),
         in_specs=[pl.BlockSpec((GATE_TILES, LANES, 2 * LANES), lambda k: (k, 0, 0)), flat, flat, VMEM],
-        out_specs=pl.BlockSpec((count, LANES, width), lambda k: (0, 0, k)),
-        out_shape=jax.ShapeDtypeStruct((count, LANES, chans), BF16),
-        compiler_params=ROOMY,
+        out_specs=flat,
+        out_shape=jax.ShapeDtypeStruct((LANES, chans), BF16),
+        compiler_params=MODEST,
         name="gate",
     )(entering, query, base, states)
 
 
-def project_kernel(gated, weight, mixed, held, sems):
-    planes = gated.shape[0]
-    outer = weight.shape[0]
-    half = outer // 2
-    here = lax.axis_index("seq") // outer
-
-    def copy(plane, part):
+def project_kernel(offsets, *refs):
+    count = len(offsets)
+    pieces, weight, rest = refs[:count], refs[count], refs[count + 1 :]
+    held, sems = rest[-2:]
+    mixed = rest[-3]
+    planes = weight.shape[1]
+    half = weight.shape[0] // 2
+    here = lax.axis_index("seq") // weight.shape[0] - lax.axis_index("fsdp") + planes
+
+    def copy(piece, part):
         some = pl.ds(part * half, half)
-        return pltpu.make_async_copy(weight.at[some, plane], held.at[plane, some], sems.at[plane, part])
-
-    for plane in range(planes):
+        plane = lax.rem(here - offsets[piece] + planes, planes)
+        return pltpu.make_async_copy(weight.at[some, plane], held.at[piece, some], sems.at[piece, part])
+
+    for piece in range(count):
         for part in range(2):
-            copy(plane, part).start()
-    depth = gated.shape[2] // 2
-    total = jnp.zeros(mixed.shape, F32)
-    for plane in range(planes):
+            copy(piece, part).start()
+    depth = pieces[0].shape[1] // 2
+    total = rest[0][...] if len(rest) == 4 else jnp.zeros(mixed.shape, F32)
+    for piece in range(count):
         for part in range(2):
-            copy(plane, part).wait()
-            block = held[plane, part * half : (part + 1) * half].reshape(depth, mixed.shape[1])
-            left = gated[lax.rem(here - plane + planes, planes), :, part * depth : (part + 1) * depth]
+            copy(piece, part).wait()
+            block = held[piece, part * half : (part + 1) * half].reshape(depth, mixed.shape[1])
+            left = pieces[piece][:, part * depth : (part + 1) * depth]
             total = total + jnp.dot(left, block, preferred_element_type=F32)
-    mixed[...] = total.astype(BF16)
-
-
-def project(gated, weight):
-    planes, tokens, _ = gated.shape
-    outer, _, rows, width = weight.shape
-    return pl.pallas_call(
-        project_kernel,
-        in_specs=[VMEM, pl.BlockSpec(memory_space=pl.ANY)],
+    mixed[...] = total.astype(mixed.dtype)
+
+
+def project(offsets, pieces, weight, earlier, dtype):
+    outer, planes, rows, width = weight.shape
+    tokens = pieces[0].shape[0]
+    more = [] if earlier is None else [earlier]
+    return pl.pallas_call(
+        functools.partial(project_kernel, offsets),
+        in_specs=[VMEM] * len(pieces) + [pl.BlockSpec(memory_space=pl.ANY)] + [VMEM] * len(more),
         out_specs=VMEM,
-        out_shape=jax.ShapeDtypeStruct((tokens, width), BF16),
+        out_shape=jax.ShapeDtypeStruct((tokens, width), dtype),
         scratch_shapes=[
-            pltpu.VMEM((planes, outer, rows, width), BF16),
-            pltpu.SemaphoreType.DMA((planes, 2)),
-        ],
-        compiler_params=ROOMY,
+            pltpu.VMEM((len(pieces), outer, rows, width), BF16),
+            pltpu.SemaphoreType.DMA((len(pieces), 2)),
+        ],
+        compiler_params=MODEST,
+        cost_estimate=pl.CostEstimate(
+            flops=2 * tokens * outer * rows * width * len(pieces),
+            bytes_accessed=2 * outer * rows * width * len(pieces),
+            transcendentals=0,
+        ),
         name="project",
-    )(gated, weight)
+    )(*pieces, weight, *more)
 
 
 def shifted(x, axis, by):
@@ -303,15 +351,17 @@
     groups = [list(range(x * inner, (x + 1) * inner)) for x in range(PLANES)]
     weight = lax.all_gather(column, "seq", axis=0, tiled=False, axis_index_groups=groups)
 
-    query, base, fresh, entering, decay = local_work(
-        segment_starts, lifetime.T, residues.T, kinds, rim, short_taps, skip_gain[None, :]
+    query, product, fresh, lags, entering, decay = features(
+        segment_starts, lifetime.T, residues.T, kinds, rim, short_taps
     )
     all_fresh = lax.all_to_all(fresh, "seq", 0, 0, tiled=True)
+    base = base_work(segment_starts, lags, product, skip_gain[None, :])
     all_states = scan_blocks(segment_starts, all_fresh, decay)
     states = lax.all_to_all(all_states, "seq", 0, 0, tiled=True)
-    copies = gate(entering, query, base, states, PLANES)
-    gated = lax.all_to_all(copies, "fsdp", 0, 0, tiled=True)
-    return project(gated, weight)
+    gated = gate(entering, query, base, states)
+    behind, ahead, across = (shifted(gated, "fsdp", by) for by in (1, 3, 2))
+    total = project((0, 3, 1), [gated, behind, ahead], weight, None, F32)
+    return project((2,), [across], weight, total, BF16)
 
 
 def solution(mesh):

time: 121 us -> 117 us (0.967)
  the two profiles are of different devices: /device:TPU:64 before, /device:TPU:65 now
where the time goes in v5:
time: 117 us; the launch traced here: 116 us
  starting transfers between devices  36.7 us (31%)
  waiting for transfers between devices  21.6 us (18%)
  blocking collectives  19.9 us (17%)
  between operations  13.5 us (12%)
  Pallas kernels  12.6 us (11%)
  local copies, waits for them, and re-layouts  9.47 us (8%)
  other arithmetic  1.79 us (2%)
    ppermute x7, starting transfers between devices, shifted(): return lax.ppermute(x, axis, [(i, (i + by) % count) for i in range(count)])  32.1 us
    all_to_all x1, blocking collectives, on_device(): all_fresh = lax.all_to_all(fresh, 'seq', 0, 0, tiled=True)  19.9 us
    ppermute x7, waiting for transfers between devices, shifted(): return lax.ppermute(x, axis, [(i, (i + by) % count) for i in range(count)])  17.2 us
    unnamed x18, local copies, waits for them, and re-layouts  8.66 us
    all_to_all x1, starting transfers between devices, on_device(): states = lax.all_to_all(all_states, 'seq', 0, 0, tiled=True)  4.55 us
    all_to_all x1, waiting for transfers between devices, on_device(): states = lax.all_to_all(all_states, 'seq', 0, 0, tiled=True)  4.43 us
    pallas_call x1, Pallas kernels, features(): pl.pallas_call(features_kernel, grid=(chans // width,), in_specs=[SMEM, s...  4.4 us
    pallas_call x2, Pallas kernels, project(): pl.pallas_call(functools.partial(project_kernel, offsets), in_specs=[VMEM...  3.23 us
  transfers between devices with their start and end apart: 9, of which 4 were waited for; matrix products, arithmetic and copies ran while one was open for 0% of the time, Pallas kernels for 10%

profile of v5, /device:TPU:65, one launch (start us, length us, event | category | flops | bytes accessed | tf_op | source)
XLA Modules:
  0.0 115.7 jit_solution(7504241575554231127)
XLA Ops:
  6.5 0.0 all-gather.2.cloned.1.call-start
  6.5 0.8 slice.4
  7.4 3.1 %collective-permute-start.1 = (bf16[64,1024]{1,0:T(8,128)(2,1)}, bf16[64,1024]{1,0:T(8,128)(2,1)S(1)}, u32[]{:S(2)}, u32[]{:S(2)}) collective-permute-start(bf16[64,1024]{1,0:T(8,128)(2,1)} %param.13), channel_id=1, source_target_pairs={{0,128},{8,136},{16,144},{24,152},{32,160},{40,168},{48,176},{56,1... | collective-permute-start | bytes 393224 | tf_op jit(solution)/shard_map/ppermute | solution.py:338
  10.5 4.4 %collective-permute-start.2 = (bf16[64,1024]{1,0:T(8,128)(2,1)}, bf16[64,1024]{1,0:T(8,128)(2,1)S(1)}, u32[]{:S(2)}, u32[]{:S(2)}) collective-permute-start(bf16[64,1024]{1,0:T(8,128)(2,1)} %param.13), channel_id=1, source_target_pairs={{0,256},{8,264},{16,272},{24,280},{32,288},{40,296},{48,304},{56,3... | collective-permute-start | bytes 393224 | tf_op jit(solution)/shard_map/ppermute | solution.py:338
  14.9 3.1 %collective-permute-start.3 = (bf16[64,1024]{1,0:T(8,128)(2,1)}, bf16[64,1024]{1,0:T(8,128)(2,1)S(1)}, u32[]{:S(2)}, u32[]{:S(2)}) collective-permute-start(bf16[64,1024]{1,0:T(8,128)(2,1)} %param.13), channel_id=1, source_target_pairs={{0,384},{8,392},{16,400},{24,408},{32,416},{40,424},{48,432},{56,4... | collective-permute-start | bytes 393224 | tf_op jit(solution)/shard_map/ppermute | solution.py:338
  17.9 4.6 %collective-permute-start = (bf16[3,2,1024]{2,1,0:T(2,128)(2,1)S(1)}, bf16[3,2,1024]{2,1,0:T(2,128)(2,1)S(1)}, u32[]{:S(2)}, u32[]{:S(2)}) collective-permute-start(bf16[3,2,1024]{2,1,0:T(2,128)(2,1)S(1)} %slice.4), channel_id=1, source_target_pairs={{0,8},{8,16},{16,24},{24,32},{32,40},{40,48},{48,56},{56,64},{64,7... | collective-permute-start | bytes 36872 | tf_op jit(solution)/shard_map/ppermute | solution.py:338
  22.5 0.8 collective-permute-done.rim
  23.3 0.0 copy-start.8
  23.3 0.0 collective-permute-done.1
  23.4 0.0 collective-permute-done.2
  23.4 0.0 collective-permute-done.3
  23.4 1.8 %pad_maximum_fusion = bf16[256,1024]{1,0:T(8,128)(2,1)} fusion(bf16[64,1024]{1,0:T(8,128)(2,1)S(1)} %collective-permute-done.3, bf16[64,1024]{1,0:T(8,128)(2,1)S(1)} %collective-permute-done.2, bf16[64,1024]{1,0:T(8,128)(2,1)S(1)} %collective-permute-done.1, bf16[64,1024]{1,0:T(8,128)(2,1)} %param.13), kind=kLoop, calls=%fused_computation | loop fusion | flops 2097152 | bytes 1048576 | tf_op jit(solution)/shard_map/concatenate | solution.py:350
  25.2 0.0 all-gather.2.cloned.1.call-update
  25.2 0.0 copy-done.8
  25.2 4.4 %features.1 = (f32[128,1024]{1,0:T(8,128)}, f32[128,1024]{1,0:T(8,128)}, f32[64,2,128]{2,1,0:T(2,128)}, f32[64,128]{1,0:T(8,128)}, bf16[8,128,256]{2,1,0:T(8,128)(2,1)}, /*index=5*/f32[64,2,128]{2,1,0:T(2,128)}) custom-call(s32[8]{0:T(128)} %starts.5, f32[16,64]{1,0:T(8,128)} %bitcast.9, f32[16,64]{1,0:T(8,128)} %bitcast.10, bf16[3,128,1024]{2,1,0:T(8,128)(2,1)} %bitcast.8, ...), custom_call_target="tpu_custom_call" | custom-call | flops 100000000 | bytes 3500000 | tf_op jit(solution)/shard_map/features/pallas_call | solution.py:151
  29.6 19.9 %all_to_all.10.fresh = f32[64,2,128]{2,1,0:T(2,128)} all-to-all(f32[64,2,128]{2,1,0:T(2,128)} %get-tuple-element.24), channel_id=1, replica_groups=mesh['seq'=64,'fsdp'=4,'dp'=2] {'seq'}, dimensions={0} | all-to-all | bytes 131072 | tf_op jit(solution)/shard_map/all_to_all | solution.py:357
  49.5 1.7 %scan_blocks.1 = f32[64,2,128]{2,1,0:T(2,128)} custom-call(s32[8]{0:T(128)} %starts.5, f32[64,2,128]{2,1,0:T(2,128)} %all_to_all.10.fresh, f32[64,2,128]{2,1,0:T(2,128)} %get-tuple-element.25.decay), custom_call_target="tpu_custom_call" | custom-call | tf_op jit(solution)/shard_map/scan_blocks/pallas_call | solution.py:245
  51.2 4.5 %all-to-all-start.1 = ((f32[64,2,128]{2,1,0:T(2,128)}), f32[64,2,128]{2,1,0:T(2,128)S(1)}, u32[]{:S(2)}, u32[]{:S(2)}) async-start(f32[64,2,128]{2,1,0:T(2,128)} %scan_blocks.1), calls=%async_computation.1 | async-start | bytes 131072 | tf_op jit(solution)/shard_map/all_to_all | solution.py:360
  55.7 0.0 copy-start.4
  55.7 0.6 copy-done.4
  56.4 0.0 copy-start.5
  56.4 0.7 copy-done.5
  57.1 0.0 copy-start.6
  57.1 1.0 copy-done.6
  58.1 0.0 copy-start.7
  58.1 0.8 copy-done.7
  58.9 2.7 %base_work.1.base = f32[128,1024]{1,0:T(8,128)S(1)} custom-call(s32[8]{0:T(128)S(1)} %copy-done.4, f32[64,128]{1,0:T(8,128)S(1)} %copy-done.7, f32[128,1024]{1,0:T(8,128)S(1)} %copy-done.6, f32[1,1024]{1,0:T(1,128)S(1)} %bitcast.5), custom_call_target="tpu_custom_call" | custom-call | flops 1100000000 | bytes 1100000 | tf_op jit(solution)/shard_map/base_work/pallas_call | solution.py:214
  61.6 4.4 %all-to-all-done.1.states = f32[64,2,128]{2,1,0:T(2,128)S(1)} async-done(((f32[64,2,128]{2,1,0:T(2,128)}), f32[64,2,128]{2,1,0:T(2,128)S(1)}, u32[]{:S(2)}, u32[]{:S(2)}) %all-to-all-start.1) | async-done | bytes 65568 | tf_op jit(solution)/shard_map/all_to_all | solution.py:360
  66.0 0.0 copy-start.2
  66.0 1.1 copy-done.2
  67.1 0.0 copy-start.3
  67.1 1.0 copy-done.3
  68.1 0.7 gate.1.refs_0_
  68.8 5.7 %collective-permute-start.5 = (bf16[128,1024]{1,0:T(8,128)(2,1)S(1)}, bf16[128,1024]{1,0:T(8,128)(2,1)S(1)}, u32[]{:S(2)}, u32[]{:S(2)}) collective-permute-start(bf16[128,1024]{1,0:T(8,128)(2,1)S(1)} %gate.1.refs_0_), channel_id=1, source_target_pairs={{0,2},{2,4},{4,6},{6,0},{1,3},{3,5},{5,7},{7,1},{8,10},{10,12},{12... | collective-permute-start | bytes 786440 | tf_op jit(solution)/shard_map/ppermute | solution.py:338
  74.5 6.3 %collective-permute-start.6 = (bf16[128,1024]{1,0:T(8,128)(2,1)S(1)}, bf16[128,1024]{1,0:T(8,128)(2,1)S(1)}, u32[]{:S(2)}, u32[]{:S(2)}) collective-permute-start(bf16[128,1024]{1,0:T(8,128)(2,1)S(1)} %gate.1.refs_0_), channel_id=1, source_target_pairs={{0,6},{2,0},{4,2},{6,4},{1,7},{3,1},{5,3},{7,5},{8,14},{10,8},{12,... | collective-permute-start | bytes 786440 | tf_op jit(solution)/shard_map/ppermute | solution.py:338
  80.7 5.1 %collective-permute-start.4 = (bf16[128,1024]{1,0:T(8,128)(2,1)S(1)}, bf16[128,1024]{1,0:T(8,128)(2,1)S(1)}, u32[]{:S(2)}, u32[]{:S(2)}) collective-permute-start(bf16[128,1024]{1,0:T(8,128)(2,1)S(1)} %gate.1.refs_0_), channel_id=1, source_target_pairs={{0,4},{2,6},{4,0},{6,2},{1,5},{3,7},{5,1},{7,3},{8,12},{10,14},{12... | collective-permute-start | bytes 786440 | tf_op jit(solution)/shard_map/ppermute | solution.py:338
  85.8 5.4 %collective-permute-done.5.refs_1_ = bf16[128,1024]{1,0:T(8,128)(2,1)S(1)} collective-permute-done((bf16[128,1024]{1,0:T(8,128)(2,1)S(1)}, bf16[128,1024]{1,0:T(8,128)(2,1)S(1)}, u32[]{:S(2)}, u32[]{:S(2)}) %collective-permute-start.5) | collective-permute-done | bytes 262176 | tf_op jit(solution)/shard_map/ppermute | solution.py:338
  91.2 0.0 collective-permute-done.6.refs_2_
  91.2 0.0 all-gather.2.cloned.1.call-done.refs_3_.refs_1_
  91.2 0.0 copy-start
  91.2 3.4 %copy-done = bf16[16,4,64,1024]{3,2,1,0:T(8,128)(2,1)S(1)} copy-done((bf16[16,4,64,1024]{3,2,1,0:T(8,128)(2,1)S(1)}, bf16[16,4,64,1024]{3,2,1,0:T(8,128)(2,1)}, u32[]{:S(2)}) %copy-start) | copy-done | bytes 8388632
  94.6 0.0 copy-start.1
  94.6 1.8 %project.2.refs_2_ = f32[128,1024]{1,0:T(8,128)S(1)} custom-call(bf16[128,1024]{1,0:T(8,128)(2,1)S(1)} %gate.1.refs_0_, bf16[128,1024]{1,0:T(8,128)(2,1)S(1)} %collective-permute-done.5.refs_1_, bf16[128,1024]{1,0:T(8,128)(2,1)S(1)} %collective-permute-done.6.refs_2_, bf16[16,4,64,1024]{3,2,1,0:T(8,128)(2,1)S(1)} %copy-done), custom_call_target="tpu_custom_call" | custom-call | flops 805306368 | bytes 6291456 | tf_op jit(solution)/shard_map/project/pallas_call | solution.py:317
  96.4 11.0 %collective-permute-done.4.refs_0_ = bf16[128,1024]{1,0:T(8,128)(2,1)S(1)} collective-permute-done((bf16[128,1024]{1,0:T(8,128)(2,1)S(1)}, bf16[128,1024]{1,0:T(8,128)(2,1)S(1)}, u32[]{:S(2)}, u32[]{:S(2)}) %collective-permute-start.4) | collective-permute-done | bytes 262176 | tf_op jit(solution)/shard_map/ppermute | solution.py:338
  107.4 0.0 copy-done.1
  107.4 1.4 %project.3 = bf16[128,1024]{1,0:T(8,128)(2,1)} custom-call(bf16[128,1024]{1,0:T(8,128)(2,1)S(1)} %collective-permute-done.4.refs_0_, bf16[16,4,64,1024]{3,2,1,0:T(8,128)(2,1)S(1)} %copy-done.1, f32[128,1024]{1,0:T(8,128)S(1)} %project.2.refs_2_), custom_call_target="tpu_custom_call" | custom-call | flops 268435456 | bytes 2097152 | tf_op jit(solution)/shard_map/project/pallas_call | solution.py:317
Async XLA Ops:
  6.5 84.6 %all-gather.2.cloned.1.call-start = ((), (), s32[]{:S(2)}) async-start(), calls=%async_computation.2 | async-start | bytes 8912896 | tf_op jit(solution)/shard_map/all_gather | solution.py:352
  7.4 16.0 %collective-permute-start.1 = (bf16[64,1024]{1,0:T(8,128)(2,1)}, bf16[64,1024]{1,0:T(8,128)(2,1)S(1)}, u32[]{:S(2)}, u32[]{:S(2)}) collective-permute-start(bf16[64,1024]{1,0:T(8,128)(2,1)} %param.13), channel_id=1, source_target_pairs={{0,128},{8,136},{16,144},{24,152},{32,160},{40,168},{48,176},{56,1... | collective-permute-start | bytes 393224 | tf_op jit(solution)/shard_map/ppermute | solution.py:338
  10.5 12.9 %collective-permute-start.2 = (bf16[64,1024]{1,0:T(8,128)(2,1)}, bf16[64,1024]{1,0:T(8,128)(2,1)S(1)}, u32[]{:S(2)}, u32[]{:S(2)}) collective-permute-start(bf16[64,1024]{1,0:T(8,128)(2,1)} %param.13), channel_id=1, source_target_pairs={{0,256},{8,264},{16,272},{24,280},{32,288},{40,296},{48,304},{56,3... | collective-permute-start | bytes 393224 | tf_op jit(solution)/shard_map/ppermute | solution.py:338
  14.9 8.5 %collective-permute-start.3 = (bf16[64,1024]{1,0:T(8,128)(2,1)}, bf16[64,1024]{1,0:T(8,128)(2,1)S(1)}, u32[]{:S(2)}, u32[]{:S(2)}) collective-permute-start(bf16[64,1024]{1,0:T(8,128)(2,1)} %param.13), channel_id=1, source_target_pairs={{0,384},{8,392},{16,400},{24,408},{32,416},{40,424},{48,432},{56,4... | collective-permute-start | bytes 393224 | tf_op jit(solution)/shard_map/ppermute | solution.py:338
  17.9 5.4 %collective-permute-start = (bf16[3,2,1024]{2,1,0:T(2,128)(2,1)S(1)}, bf16[3,2,1024]{2,1,0:T(2,128)(2,1)S(1)}, u32[]{:S(2)}, u32[]{:S(2)}) collective-permute-start(bf16[3,2,1024]{2,1,0:T(2,128)(2,1)S(1)} %slice.4), channel_id=1, source_target_pairs={{0,8},{8,16},{16,24},{24,32},{32,40},{40,48},{48,56},{56,64},{64,7... | collective-permute-start | bytes 36872 | tf_op jit(solution)/shard_map/ppermute | solution.py:338
  23.3 1.8 %copy-start.8 = (bf16[3,2,1024]{2,1,0:T(2,128)(2,1)}, bf16[3,2,1024]{2,1,0:T(2,128)(2,1)S(1)}, u32[]{:S(2)}) copy-start(bf16[3,2,1024]{2,1,0:T(2,128)(2,1)S(1)} %collective-permute-done.rim) | copy-start | bytes 36868
  51.2 14.8 %all-to-all-start.1 = ((f32[64,2,128]{2,1,0:T(2,128)}), f32[64,2,128]{2,1,0:T(2,128)S(1)}, u32[]{:S(2)}, u32[]{:S(2)}) async-start(f32[64,2,128]{2,1,0:T(2,128)} %scan_blocks.1), calls=%async_computation.1 | async-start | bytes 131072 | tf_op jit(solution)/shard_map/all_to_all | solution.py:360
  55.7 0.7 copy-start.4
  56.4 0.7 copy-start.5
  57.1 1.0 copy-start.6
  58.1 0.8 copy-start.7
  66.0 1.1 copy-start.2
  67.1 1.0 copy-start.3
  68.8 22.4 %collective-permute-start.5 = (bf16[128,1024]{1,0:T(8,128)(2,1)S(1)}, bf16[128,1024]{1,0:T(8,128)(2,1)S(1)}, u32[]{:S(2)}, u32[]{:S(2)}) collective-permute-start(bf16[128,1024]{1,0:T(8,128)(2,1)S(1)} %gate.1.refs_0_), channel_id=1, source_target_pairs={{0,2},{2,4},{4,6},{6,0},{1,3},{3,5},{5,7},{7,1},{8,10},{10,12},{12... | collective-permute-start | bytes 786440 | tf_op jit(solution)/shard_map/ppermute | solution.py:338
  74.5 16.7 %collective-permute-start.6 = (bf16[128,1024]{1,0:T(8,128)(2,1)S(1)}, bf16[128,1024]{1,0:T(8,128)(2,1)S(1)}, u32[]{:S(2)}, u32[]{:S(2)}) collective-permute-start(bf16[128,1024]{1,0:T(8,128)(2,1)S(1)} %gate.1.refs_0_), channel_id=1, source_target_pairs={{0,6},{2,0},{4,2},{6,4},{1,7},{3,1},{5,3},{7,5},{8,14},{10,8},{12,... | collective-permute-start | bytes 786440 | tf_op jit(solution)/shard_map/ppermute | solution.py:338
  80.7 26.7 %collective-permute-start.4 = (bf16[128,1024]{1,0:T(8,128)(2,1)S(1)}, bf16[128,1024]{1,0:T(8,128)(2,1)S(1)}, u32[]{:S(2)}, u32[]{:S(2)}) collective-permute-start(bf16[128,1024]{1,0:T(8,128)(2,1)S(1)} %gate.1.refs_0_), channel_id=1, source_target_pairs={{0,4},{2,6},{4,0},{6,2},{1,5},{3,7},{5,1},{7,3},{8,12},{10,14},{12... | collective-permute-start | bytes 786440 | tf_op jit(solution)/shard_map/ppermute | solution.py:338
  91.2 3.4 %copy-start = (bf16[16,4,64,1024]{3,2,1,0:T(8,128)(2,1)S(1)}, bf16[16,4,64,1024]{3,2,1,0:T(8,128)(2,1)}, u32[]{:S(2)}) copy-start(bf16[16,4,64,1024]{3,2,1,0:T(8,128)(2,1)} %all-gather.2.cloned.1.call-done.refs_3_.refs_1_) | copy-start | bytes 25165828
  94.6 12.8 %copy-start.1 = (bf16[16,4,64,1024]{3,2,1,0:T(8,128)(2,1)S(1)}, bf16[16,4,64,1024]{3,2,1,0:T(8,128)(2,1)}, u32[]{:S(2)}) copy-start(bf16[16,4,64,1024]{3,2,1,0:T(8,128)(2,1)} %all-gather.2.cloned.1.call-done.refs_3_.refs_1_) | copy-start | bytes 25165828
Sparse Core Ops, SparseCore 0:
  25.3 63.3 all-gather.1

commit v6 on v5

--- a/solution.py
+++ b/solution.py
@@ -64,11 +64,11 @@
     return jnp.concatenate([wide, jnp.zeros((LANES - x.shape[0], LANES), F32)], axis=0).T
 
 
-FEATURE_TILES = 2
+FEATURE_TILES = 4
 
 
 def features_kernel(
-    starts, lifetime, residues, qkv, rim, taps, query, product, fresh, lags, entering, decay, rates, weights
+    starts, lifetime, qkv, rim, taps, query, product, fresh, decay, rates
 ):
     step = pl.program_id(0)
     first = lax.axis_index("seq") * LANES
@@ -77,26 +77,15 @@
 
     @pl.when(step == 0)
     def _():
-        rate = 1.0 / lifetime[...]
-        double = 2.0 * rate
-        series = double * (
-            1.0
-            - double
-            * (0.5 - double * (1.0 / 6 - double * (1.0 / 24 - double * (1.0 / 120 - double * (1.0 / 720)))))
-        )
-        rates[...] = turned(rate)
-        weights[...] = turned(residues[...] * jnp.sqrt(jnp.where(double < 0.07, series, 1.0 - jnp.exp(-double))))
+        rates[...] = turned(1.0 / lifetime[...])
 
     clear = not_start(starts, first + rows)
     clear_before = clear * not_start(starts, first + rows - 1)
     lane = iota((PER_TILE, LANES), 1)
     seg_lane = segment_of(starts, first + lane)
     last = segment_of(starts, jnp.full((PER_TILE, LANES), first + (LANES - 1)))
-    before = jnp.where(first > 0, segment_of(starts, jnp.full((PER_TILE, LANES), first - 1)), -1)
     closing = (seg_lane == last).astype(F32)
-    joined = (seg_lane == before).astype(F32)
     offset = lane.astype(F32)
-    apart = jnp.where(lane == 0, 0, LANES - lane).astype(F32)
 
     for part in range(FEATURE_TILES):
         tile = step * FEATURE_TILES + part
@@ -118,22 +107,12 @@
 
         group_rows = pl.ds(pl.multiple_of(tile * PER_TILE, PER_TILE), PER_TILE)
         rate = rates[group_rows, :]
-        weight = weights[group_rows, :]
-        total = jnp.zeros((PER_TILE, LANES), F32)
         leave_rows = []
-        enter_rows = []
         for mode in range(MODES):
             r = jnp.broadcast_to(rate[:, mode : mode + 1], (PER_TILE, LANES))
-            w = jnp.broadcast_to(weight[:, mode : mode + 1], (PER_TILE, LANES))
-            total = total + w * jnp.exp(-r * apart)
             leave_rows.append(jnp.exp(-r * (LANES - 1.0 - offset)) * closing)
-            enter_rows.append(w * jnp.exp(-r * (offset + 1.0)) * joined)
             whole = jnp.sum(jnp.exp(-r * LANES) * own, axis=0, keepdims=True)
             decay[4 * mode + tile // 2, pl.ds(tile % 2, 1), :] = whole
-        lags[part * PER_TILE : (part + 1) * PER_TILE, :] = total
-        high, low = halves(jnp.concatenate(enter_rows, axis=0).T)
-        entering[part, :, :LANES] = high
-        entering[part, :, LANES:] = low
         high, low = halves(jnp.concatenate(leave_rows, axis=0))
         states = split_dot(jnp.concatenate([high, low], axis=1), doubled(values))
         for mode in range(MODES):
@@ -141,7 +120,7 @@
             fresh[4 * mode + tile // 2, pl.ds(tile % 2, 1), :] = jnp.sum(some, axis=0, keepdims=True)
 
 
-def features(starts, lifetime, residues, qkv, rim, taps):
+def features(starts, lifetime, qkv, rim, taps):
     chans = qkv.shape[2]
     tiles = chans // LANES
     width = FEATURE_TILES * LANES
@@ -154,7 +133,6 @@
         in_specs=[
             SMEM,
             small,
-            small,
             pl.BlockSpec((3, LANES, width), lambda k: (0, 0, k)),
             pl.BlockSpec((3, SHORT - 1, width), lambda k: (0, 0, k)),
             pl.BlockSpec((SHORT, 3, width), lambda k: (0, 0, k)),
@@ -163,43 +141,72 @@
             flat,
             flat,
             whole,
-            pl.BlockSpec((FEATURE_TILES * PER_TILE, LANES), lambda k: (k, 0)),
-            pl.BlockSpec((FEATURE_TILES, LANES, 2 * LANES), lambda k: (k, 0, 0)),
             whole,
         ],
         out_shape=[
             jax.ShapeDtypeStruct((LANES, chans), F32),
             jax.ShapeDtypeStruct((LANES, chans), F32),
             jax.ShapeDtypeStruct((8 * tiles, 2, LANES), F32),
-            jax.ShapeDtypeStruct((tiles * PER_TILE, LANES), F32),
-            jax.ShapeDtypeStruct((tiles, LANES, 2 * LANES), BF16),
             jax.ShapeDtypeStruct((8 * tiles, 2, LANES), F32),
         ],
-        scratch_shapes=[pltpu.VMEM((LANES, LANES), F32), pltpu.VMEM((LANES, LANES), F32)],
+        scratch_shapes=[pltpu.VMEM((LANES, LANES), F32)],
         compiler_params=ROOMY,
-        cost_estimate=pl.CostEstimate(flops=100_000_000, bytes_accessed=3_500_000, transcendentals=600_000),
+        cost_estimate=pl.CostEstimate(flops=100_000_000, bytes_accessed=2_500_000, transcendentals=200_000),
         name="features",
-    )(starts, lifetime, residues, qkv, rim, taps)
+    )(starts, lifetime, qkv, rim, taps)
 
 
 BASE_TILES = 2
 
 
-def base_kernel(starts, lags, product, skip, base):
+def base_kernel(starts, lifetime, residues, product, skip, base, entering, rates, weights):
+    step = pl.program_id(0)
     first = lax.axis_index("seq") * LANES
     rows = iota((LANES, LANES), 0)
     cols = iota((LANES, LANES), 1)
-    linked = (
-        (segment_of(starts, first + rows) == segment_of(starts, first + cols)) & (rows >= cols)
-    ).astype(F32)
+
+    @pl.when(step == 0)
+    def _():
+        rate = 1.0 / lifetime[...]
+        double = 2.0 * rate
+        series = double * (
+            1.0
+            - double
+            * (0.5 - double * (1.0 / 6 - double * (1.0 / 24 - double * (1.0 / 120 - double * (1.0 / 720)))))
+        )
+        rates[...] = turned(rate)
+        weights[...] = turned(residues[...] * jnp.sqrt(jnp.where(double < 0.07, series, 1.0 - jnp.exp(-double))))
+
+    seg_col = segment_of(starts, first + cols)
+    linked = ((segment_of(starts, first + rows) == seg_col) & (rows >= cols)).astype(F32)
+    before = jnp.where(first > 0, segment_of(starts, jnp.full((PER_TILE, LANES), first - 1)), -1)
+    joined = (seg_col[:PER_TILE] == before).astype(F32)
+    lane = iota((PER_TILE, LANES), 1)
+    offset = lane.astype(F32)
+    apart = jnp.where(lane == 0, 0, LANES - lane).astype(F32)
+
     for part in range(BASE_TILES):
+        tile = step * BASE_TILES + part
+        group_rows = pl.ds(pl.multiple_of(tile * PER_TILE, PER_TILE), PER_TILE)
+        rate = rates[group_rows, :]
+        weight = weights[group_rows, :]
+        lags = jnp.zeros((PER_TILE, LANES), F32)
+        enter_rows = []
+        for mode in range(MODES):
+            r = jnp.broadcast_to(rate[:, mode : mode + 1], (PER_TILE, LANES))
+            w = jnp.broadcast_to(weight[:, mode : mode + 1], (PER_TILE, LANES))
+            lags = lags + w * jnp.exp(-r * apart)
+            enter_rows.append(w * jnp.exp(-r * (offset + 1.0)) * joined)
+        high, low = halves(jnp.concatenate(enter_rows, axis=0).T)
+        entering[part, :, :LANES] = high
+        entering[part, :, LANES:] = low
+
         span = slice(part * LANES, (part + 1) * LANES)
         values = product[:, span]
         both = doubled(values)
         total = skip[:, span] * values
         for group in range(PER_TILE):
-            at = part * PER_TILE + group
-            spread = jnp.broadcast_to(lags[at : at + 1, :], (LANES, LANES))
+            spread = jnp.broadcast_to(lags[group : group + 1, :], (LANES, LANES))
             rolled = pltpu.roll(spread, 0, 1, stride=1, stride_axis=0)
             high, low = halves(rolled * linked)
             out = split_dot(jnp.concatenate([high, low], axis=1), both)
@@ -207,25 +214,26 @@
         base[:, span] = total
 
 
-def base_work(starts, lags, product, skip):
+def base_work(starts, lifetime, residues, product, skip):
     chans = product.shape[1]
+    tiles = chans // LANES
     width = BASE_TILES * LANES
     flat = pl.BlockSpec((LANES, width), lambda k: (0, k))
+    small = pl.BlockSpec(lifetime.shape, lambda k: (0, 0))
     return pl.pallas_call(
         base_kernel,
         grid=(chans // width,),
-        in_specs=[
-            SMEM,
-            pl.BlockSpec((BASE_TILES * PER_TILE, LANES), lambda k: (k, 0)),
-            flat,
-            pl.BlockSpec((1, width), lambda k: (0, k)),
-        ],
-        out_specs=flat,
-        out_shape=jax.ShapeDtypeStruct((LANES, chans), F32),
+        in_specs=[SMEM, small, small, flat, pl.BlockSpec((1, width), lambda k: (0, k))],
+        out_specs=[flat, pl.BlockSpec((BASE_TILES, LANES, 2 * LANES), lambda k: (k, 0, 0))],
+        out_shape=[
+            jax.ShapeDtypeStruct((LANES, chans), F32),
+            jax.ShapeDtypeStruct((tiles, LANES, 2 * LANES), BF16),
+        ],
+        scratch_shapes=[pltpu.VMEM((LANES, LANES), F32), pltpu.VMEM((LANES, LANES), F32)],
         compiler_params=MODEST,
-        cost_estimate=pl.CostEstimate(flops=1_100_000_000, bytes_accessed=1_100_000, transcendentals=0),
+        cost_estimate=pl.CostEstimate(flops=1_100_000_000, bytes_accessed=1_600_000, transcendentals=400_000),
         name="base_work",
-    )(starts, lags, product, skip)
+    )(starts, lifetime, residues, product, skip)
 
 
 def scan_kernel(starts, fresh, decay, entering):
@@ -351,17 +359,15 @@
     groups = [list(range(x * inner, (x + 1) * inner)) for x in range(PLANES)]
     weight = lax.all_gather(column, "seq", axis=0, tiled=False, axis_index_groups=groups)
 
-    query, product, fresh, lags, entering, decay = features(
-        segment_starts, lifetime.T, residues.T, kinds, rim, short_taps
-    )
+    query, product, fresh, decay = features(segment_starts, lifetime.T, kinds, rim, short_taps)
     all_fresh = lax.all_to_all(fresh, "seq", 0, 0, tiled=True)
-    base = base_work(segment_starts, lags, product, skip_gain[None, :])
+    base, entering = base_work(segment_starts, lifetime.T, residues.T, product, skip_gain[None, :])
     all_states = scan_blocks(segment_starts, all_fresh, decay)
     states = lax.all_to_all(all_states, "seq", 0, 0, tiled=True)
     gated = gate(entering, query, base, states)
     behind, ahead, across = (shifted(gated, "fsdp", by) for by in (1, 3, 2))
-    total = project((0, 3, 1), [gated, behind, ahead], weight, None, F32)
-    return project((2,), [across], weight, total, BF16)
+    total = project((0, 2), [gated, across], weight, None, F32)
+    return project((3, 1), [behind, ahead], weight, total, BF16)
 
 
 def solution(mesh):

time: 117 us -> 113 us (0.966)
  the two profiles are of different devices: /device:TPU:65 before, /device:TPU:1 now
where the time goes in v6:
time: 113 us; the launch traced here: 112 us
  starting transfers between devices  36.3 us (32%)
  blocking collectives  20.4 us (18%)
  waiting for transfers between devices  18.1 us (16%)
  between operations  13.5 us (12%)
  Pallas kernels  12.7 us (11%)
  local copies, waits for them, and re-layouts  9.03 us (8%)
  other arithmetic  1.8 us (2%)
    ppermute x7, starting transfers between devices, shifted(): return lax.ppermute(x, axis, [(i, (i + by) % count) for i in range(count)])  31.9 us
    all_to_all x1, blocking collectives, on_device(): all_fresh = lax.all_to_all(fresh, 'seq', 0, 0, tiled=True)  20.4 us
    ppermute x7, waiting for transfers between devices, shifted(): return lax.ppermute(x, axis, [(i, (i + by) % count) for i in range(count)])  10.5 us
    unnamed x18, local copies, waits for them, and re-layouts  8.22 us
    all_gather x1, waiting for transfers between devices, on_device(): lax.all_gather(column, 'seq', axis=0, tiled=False, axis_index_groups=groups)  4.91 us
    all_to_all x1, starting transfers between devices, on_device(): states = lax.all_to_all(all_states, 'seq', 0, 0, tiled=True)  4.45 us
    pallas_call x1, Pallas kernels, base_work(): pl.pallas_call(base_kernel, grid=(chans // width,), in_specs=[SMEM, small...  3.76 us
    pallas_call x1, Pallas kernels, features(): pl.pallas_call(features_kernel, grid=(chans // width,), in_specs=[SMEM, s...  3.36 us
  transfers between devices with their start and end apart: 9, of which 5 were waited for; matrix products, arithmetic and copies ran while one was open for 0% of the time, Pallas kernels for 10%

profile of v6, /device:TPU:1, one launch (start us, length us, event | category | flops | bytes accessed | tf_op | source)
XLA Modules:
  0.0 111.8 jit_solution(2272617930476424871)
XLA Ops:
  6.5 0.0 all-gather.2.cloned.1.call-start
  6.5 0.8 slice.4
  7.4 4.0 %collective-permute-start.1 = (bf16[64,1024]{1,0:T(8,128)(2,1)}, bf16[64,1024]{1,0:T(8,128)(2,1)S(1)}, u32[]{:S(2)}, u32[]{:S(2)}) collective-permute-start(bf16[64,1024]{1,0:T(8,128)(2,1)} %param.13), channel_id=1, source_target_pairs={{0,128},{8,136},{16,144},{24,152},{32,160},{40,168},{48,176},{56,1... | collective-permute-start | bytes 393224 | tf_op jit(solution)/shard_map/ppermute | solution.py:346
  11.3 4.4 %collective-permute-start.2 = (bf16[64,1024]{1,0:T(8,128)(2,1)}, bf16[64,1024]{1,0:T(8,128)(2,1)S(1)}, u32[]{:S(2)}, u32[]{:S(2)}) collective-permute-start(bf16[64,1024]{1,0:T(8,128)(2,1)} %param.13), channel_id=1, source_target_pairs={{0,256},{8,264},{16,272},{24,280},{32,288},{40,296},{48,304},{56,3... | collective-permute-start | bytes 393224 | tf_op jit(solution)/shard_map/ppermute | solution.py:346
  15.7 3.1 %collective-permute-start.3 = (bf16[64,1024]{1,0:T(8,128)(2,1)}, bf16[64,1024]{1,0:T(8,128)(2,1)S(1)}, u32[]{:S(2)}, u32[]{:S(2)}) collective-permute-start(bf16[64,1024]{1,0:T(8,128)(2,1)} %param.13), channel_id=1, source_target_pairs={{0,384},{8,392},{16,400},{24,408},{32,416},{40,424},{48,432},{56,4... | collective-permute-start | bytes 393224 | tf_op jit(solution)/shard_map/ppermute | solution.py:346
  18.8 4.6 %collective-permute-start = (bf16[3,2,1024]{2,1,0:T(2,128)(2,1)S(1)}, bf16[3,2,1024]{2,1,0:T(2,128)(2,1)S(1)}, u32[]{:S(2)}, u32[]{:S(2)}) collective-permute-start(bf16[3,2,1024]{2,1,0:T(2,128)(2,1)S(1)} %slice.4), channel_id=1, source_target_pairs={{0,8},{8,16},{16,24},{24,32},{32,40},{40,48},{48,56},{56,64},{64,7... | collective-permute-start | bytes 36872 | tf_op jit(solution)/shard_map/ppermute | solution.py:346
  23.4 2.4 %collective-permute-done.rim = bf16[3,2,1024]{2,1,0:T(2,128)(2,1)S(1)} collective-permute-done((bf16[3,2,1024]{2,1,0:T(2,128)(2,1)S(1)}, bf16[3,2,1024]{2,1,0:T(2,128)(2,1)S(1)}, u32[]{:S(2)}, u32[]{:S(2)}) %collective-permute-start) | collective-permute-done | bytes 12320 | tf_op jit(solution)/shard_map/ppermute | solution.py:346
  25.8 0.0 copy-start.8
  25.8 0.0 collective-permute-done.1
  25.8 0.0 collective-permute-done.2
  25.8 0.0 collective-permute-done.3
  25.8 1.8 %pad_maximum_fusion = bf16[256,1024]{1,0:T(8,128)(2,1)} fusion(bf16[64,1024]{1,0:T(8,128)(2,1)S(1)} %collective-permute-done.3, bf16[64,1024]{1,0:T(8,128)(2,1)S(1)} %collective-permute-done.2, bf16[64,1024]{1,0:T(8,128)(2,1)S(1)} %collective-permute-done.1, bf16[64,1024]{1,0:T(8,128)(2,1)} %param.13), kind=kLoop, calls=%fused_computation | loop fusion | flops 2097152 | bytes 1048576 | tf_op jit(solution)/shard_map/concatenate | solution.py:358
  27.6 0.0 all-gather.2.cloned.1.call-update
  27.7 0.0 copy-done.8
  27.7 3.4 %features.1 = (f32[128,1024]{1,0:T(8,128)}, f32[128,1024]{1,0:T(8,128)}, f32[64,2,128]{2,1,0:T(2,128)}, f32[64,2,128]{2,1,0:T(2,128)}) custom-call(s32[8]{0:T(128)} %starts.5, f32[16,64]{1,0:T(8,128)} %bitcast.5, bf16[3,128,1024]{2,1,0:T(8,128)(2,1)} %bitcast.11, bf16[3,2,1024]{2,1,0:T(2,128)(2,1)} %copy-done.8, f32[3,3,1024]{2,1,0:T(4,128)} %taps.1), custom_call_target="tpu_custom_call" | custom-call | flops 100000000 | bytes 2500000 | tf_op jit(solution)/shard_map/features/pallas_call | solution.py:130
  31.0 20.4 %all_to_all.10.fresh = f32[64,2,128]{2,1,0:T(2,128)} all-to-all(f32[64,2,128]{2,1,0:T(2,128)} %get-tuple-element.24), channel_id=1, replica_groups=mesh['seq'=64,'fsdp'=4,'dp'=2] {'seq'}, dimensions={0} | all-to-all | bytes 131072 | tf_op jit(solution)/shard_map/all_to_all | solution.py:363
  51.4 1.7 %scan_blocks.1 = f32[64,2,128]{2,1,0:T(2,128)} custom-call(s32[8]{0:T(128)} %starts.5, f32[64,2,128]{2,1,0:T(2,128)} %all_to_all.10.fresh, f32[64,2,128]{2,1,0:T(2,128)} %get-tuple-element.25.decay), custom_call_target="tpu_custom_call" | custom-call | tf_op jit(solution)/shard_map/scan_blocks/pallas_call | solution.py:253
  53.1 4.5 %all-to-all-start.1 = ((f32[64,2,128]{2,1,0:T(2,128)}), f32[64,2,128]{2,1,0:T(2,128)S(1)}, u32[]{:S(2)}, u32[]{:S(2)}) async-start(f32[64,2,128]{2,1,0:T(2,128)} %scan_blocks.1), calls=%async_computation.1 | async-start | bytes 131072 | tf_op jit(solution)/shard_map/all_to_all | solution.py:366
  57.5 0.0 copy-start.3
  57.6 0.7 copy-done.3
  58.2 0.0 copy-start.4
  58.3 0.7 copy-done.4
  58.9 0.0 copy-start.5
  58.9 1.0 copy-done.5
  59.9 0.0 copy-start.6
  60.0 0.7 copy-done.6
  60.6 0.0 copy-start.7
  60.6 0.7 copy-done.7
  61.3 3.8 %base_work.1 = (f32[128,1024]{1,0:T(8,128)S(1)}, bf16[8,128,256]{2,1,0:T(8,128)(2,1)S(1)}) custom-call(s32[8]{0:T(128)S(1)} %copy-done.4, f32[16,64]{1,0:T(8,128)S(1)} %bitcast.6, f32[16,64]{1,0:T(8,128)S(1)} %bitcast.7, f32[128,1024]{1,0:T(8,128)S(1)} %copy-done.5, f32[1,1024]{1,0:T(1,128)S(1)} %bitcast.8), custom_call_target="tpu_custom_call" | custom-call | flops 1100000000 | bytes 1600000 | tf_op jit(solution)/shard_map/base_work/pallas_call | solution.py:223
  65.1 2.7 %all-to-all-done.1.states = f32[64,2,128]{2,1,0:T(2,128)S(1)} async-done(((f32[64,2,128]{2,1,0:T(2,128)}), f32[64,2,128]{2,1,0:T(2,128)S(1)}, u32[]{:S(2)}, u32[]{:S(2)}) %all-to-all-start.1) | async-done | bytes 65568 | tf_op jit(solution)/shard_map/all_to_all | solution.py:366
  67.8 0.0 copy-start.2
  67.8 1.1 copy-done.2
  68.9 0.6 gate.1.refs_0_
  69.5 8.5 %collective-permute-start.6 = (bf16[128,1024]{1,0:T(8,128)(2,1)S(1)}, bf16[128,1024]{1,0:T(8,128)(2,1)S(1)}, u32[]{:S(2)}, u32[]{:S(2)}) collective-permute-start(bf16[128,1024]{1,0:T(8,128)(2,1)S(1)} %gate.1.refs_0_), channel_id=1, source_target_pairs={{0,4},{2,6},{4,0},{6,2},{1,5},{3,7},{5,1},{7,3},{8,12},{10,14},{12... | collective-permute-start | bytes 786440 | tf_op jit(solution)/shard_map/ppermute | solution.py:346
  78.0 4.0 %collective-permute-start.4 = (bf16[128,1024]{1,0:T(8,128)(2,1)S(1)}, bf16[128,1024]{1,0:T(8,128)(2,1)S(1)}, u32[]{:S(2)}, u32[]{:S(2)}) collective-permute-start(bf16[128,1024]{1,0:T(8,128)(2,1)S(1)} %gate.1.refs_0_), channel_id=1, source_target_pairs={{0,2},{2,4},{4,6},{6,0},{1,3},{3,5},{5,7},{7,1},{8,10},{10,12},{12... | collective-permute-start | bytes 786440 | tf_op jit(solution)/shard_map/ppermute | solution.py:346
  82.0 3.4 %collective-permute-start.5 = (bf16[128,1024]{1,0:T(8,128)(2,1)S(1)}, bf16[128,1024]{1,0:T(8,128)(2,1)S(1)}, u32[]{:S(2)}, u32[]{:S(2)}) collective-permute-start(bf16[128,1024]{1,0:T(8,128)(2,1)S(1)} %gate.1.refs_0_), channel_id=1, source_target_pairs={{0,6},{2,0},{4,2},{6,4},{1,7},{3,1},{5,3},{7,5},{8,14},{10,8},{12,... | collective-permute-start | bytes 786440 | tf_op jit(solution)/shard_map/ppermute | solution.py:346
  85.4 0.0 collective-permute-done.6.refs_1_
  85.4 4.9 %all-gather.2.cloned.1.call-done.refs_2_ = bf16[16,4,64,1024]{3,2,1,0:T(8,128)(2,1)} async-done(((bf16[1,4,64,1024]{3,2,1,0:T(8,128)(2,1)}), bf16[16,4,64,1024]{3,2,1,0:T(8,128)(2,1)}) %all-gather.2.cloned.1.call-update) | async-done | bytes 8388624 | tf_op jit(solution)/shard_map/all_gather | solution.py:360
  90.4 0.0 copy-start
  90.4 3.4 %copy-done = bf16[16,4,64,1024]{3,2,1,0:T(8,128)(2,1)S(1)} copy-done((bf16[16,4,64,1024]{3,2,1,0:T(8,128)(2,1)S(1)}, bf16[16,4,64,1024]{3,2,1,0:T(8,128)(2,1)}, u32[]{:S(2)}) %copy-start) | copy-done | bytes 8388632
  93.7 0.0 copy-start.1
  93.7 1.2 %project.2.refs_3_ = f32[128,1024]{1,0:T(8,128)S(1)} custom-call(bf16[128,1024]{1,0:T(8,128)(2,1)S(1)} %gate.1.refs_0_, bf16[128,1024]{1,0:T(8,128)(2,1)S(1)} %collective-permute-done.6.refs_1_, bf16[16,4,64,1024]{3,2,1,0:T(8,128)(2,1)S(1)} %copy-done), custom_call_target="tpu_custom_call" | custom-call | flops 536870912 | bytes 4194304 | tf_op jit(solution)/shard_map/project/pallas_call | solution.py:325
  95.0 1.3 %collective-permute-done.4.refs_0_ = bf16[128,1024]{1,0:T(8,128)(2,1)S(1)} collective-permute-done((bf16[128,1024]{1,0:T(8,128)(2,1)S(1)}, bf16[128,1024]{1,0:T(8,128)(2,1)S(1)}, u32[]{:S(2)}, u32[]{:S(2)}) %collective-permute-start.4) | collective-permute-done | bytes 262176 | tf_op jit(solution)/shard_map/ppermute | solution.py:346
  96.3 6.7 %collective-permute-done.5.refs_1_ = bf16[128,1024]{1,0:T(8,128)(2,1)S(1)} collective-permute-done((bf16[128,1024]{1,0:T(8,128)(2,1)S(1)}, bf16[128,1024]{1,0:T(8,128)(2,1)S(1)}, u32[]{:S(2)}, u32[]{:S(2)}) %collective-permute-start.5) | collective-permute-done | bytes 262176 | tf_op jit(solution)/shard_map/ppermute | solution.py:346
  103.0 0.0 copy-done.1
  103.0 2.0 %project.3 = bf16[128,1024]{1,0:T(8,128)(2,1)} custom-call(bf16[128,1024]{1,0:T(8,128)(2,1)S(1)} %collective-permute-done.4.refs_0_, bf16[128,1024]{1,0:T(8,128)(2,1)S(1)} %collective-permute-done.5.refs_1_, bf16[16,4,64,1024]{3,2,1,0:T(8,128)(2,1)S(1)} %copy-done.1, f32[128,1024]{1,0:T(8,128)S(1)} %project.2.refs_3_), custom_call_target="tpu_custom_call" | custom-call | flops 536870912 | bytes 4194304 | tf_op jit(solution)/shard_map/project/pallas_call | solution.py:325
Async XLA Ops:
  6.5 83.8 %all-gather.2.cloned.1.call-start = ((), (), s32[]{:S(2)}) async-start(), calls=%async_computation.2 | async-start | bytes 8912896 | tf_op jit(solution)/shard_map/all_gather | solution.py:360
  7.4 18.5 %collective-permute-start.1 = (bf16[64,1024]{1,0:T(8,128)(2,1)}, bf16[64,1024]{1,0:T(8,128)(2,1)S(1)}, u32[]{:S(2)}, u32[]{:S(2)}) collective-permute-start(bf16[64,1024]{1,0:T(8,128)(2,1)} %param.13), channel_id=1, source_target_pairs={{0,128},{8,136},{16,144},{24,152},{32,160},{40,168},{48,176},{56,1... | collective-permute-start | bytes 393224 | tf_op jit(solution)/shard_map/ppermute | solution.py:346
  11.3 14.5 %collective-permute-start.2 = (bf16[64,1024]{1,0:T(8,128)(2,1)}, bf16[64,1024]{1,0:T(8,128)(2,1)S(1)}, u32[]{:S(2)}, u32[]{:S(2)}) collective-permute-start(bf16[64,1024]{1,0:T(8,128)(2,1)} %param.13), channel_id=1, source_target_pairs={{0,256},{8,264},{16,272},{24,280},{32,288},{40,296},{48,304},{56,3... | collective-permute-start | bytes 393224 | tf_op jit(solution)/shard_map/ppermute | solution.py:346
  15.7 10.1 %collective-permute-start.3 = (bf16[64,1024]{1,0:T(8,128)(2,1)}, bf16[64,1024]{1,0:T(8,128)(2,1)S(1)}, u32[]{:S(2)}, u32[]{:S(2)}) collective-permute-start(bf16[64,1024]{1,0:T(8,128)(2,1)} %param.13), channel_id=1, source_target_pairs={{0,384},{8,392},{16,400},{24,408},{32,416},{40,424},{48,432},{56,4... | collective-permute-start | bytes 393224 | tf_op jit(solution)/shard_map/ppermute | solution.py:346
  18.8 7.1 %collective-permute-start = (bf16[3,2,1024]{2,1,0:T(2,128)(2,1)S(1)}, bf16[3,2,1024]{2,1,0:T(2,128)(2,1)S(1)}, u32[]{:S(2)}, u32[]{:S(2)}) collective-permute-start(bf16[3,2,1024]{2,1,0:T(2,128)(2,1)S(1)} %slice.4), channel_id=1, source_target_pairs={{0,8},{8,16},{16,24},{24,32},{32,40},{40,48},{48,56},{56,64},{64,7... | collective-permute-start | bytes 36872 | tf_op jit(solution)/shard_map/ppermute | solution.py:346
  25.8 1.8 %copy-start.8 = (bf16[3,2,1024]{2,1,0:T(2,128)(2,1)}, bf16[3,2,1024]{2,1,0:T(2,128)(2,1)S(1)}, u32[]{:S(2)}) copy-start(bf16[3,2,1024]{2,1,0:T(2,128)(2,1)S(1)} %collective-permute-done.rim) | copy-start | bytes 36868
  53.1 14.7 %all-to-all-start.1 = ((f32[64,2,128]{2,1,0:T(2,128)}), f32[64,2,128]{2,1,0:T(2,128)S(1)}, u32[]{:S(2)}, u32[]{:S(2)}) async-start(f32[64,2,128]{2,1,0:T(2,128)} %scan_blocks.1), calls=%async_computation.1 | async-start | bytes 131072 | tf_op jit(solution)/shard_map/all_to_all | solution.py:366
  57.5 0.7 copy-start.3
  58.2 0.7 copy-start.4
  58.9 1.0 copy-start.5
  59.9 0.7 copy-start.6
  60.6 0.7 copy-start.7
  67.8 1.1 copy-start.2
  69.5 15.9 %collective-permute-start.6 = (bf16[128,1024]{1,0:T(8,128)(2,1)S(1)}, bf16[128,1024]{1,0:T(8,128)(2,1)S(1)}, u32[]{:S(2)}, u32[]{:S(2)}) collective-permute-start(bf16[128,1024]{1,0:T(8,128)(2,1)S(1)} %gate.1.refs_0_), channel_id=1, source_target_pairs={{0,4},{2,6},{4,0},{6,2},{1,5},{3,7},{5,1},{7,3},{8,12},{10,14},{12... | collective-permute-start | bytes 786440 | tf_op jit(solution)/shard_map/ppermute | solution.py:346
  78.0 18.3 %collective-permute-start.4 = (bf16[128,1024]{1,0:T(8,128)(2,1)S(1)}, bf16[128,1024]{1,0:T(8,128)(2,1)S(1)}, u32[]{:S(2)}, u32[]{:S(2)}) collective-permute-start(bf16[128,1024]{1,0:T(8,128)(2,1)S(1)} %gate.1.refs_0_), channel_id=1, source_target_pairs={{0,2},{2,4},{4,6},{6,0},{1,3},{3,5},{5,7},{7,1},{8,10},{10,12},{12... | collective-permute-start | bytes 786440 | tf_op jit(solution)/shard_map/ppermute | solution.py:346
  82.0 21.0 %collective-permute-start.5 = (bf16[128,1024]{1,0:T(8,128)(2,1)S(1)}, bf16[128,1024]{1,0:T(8,128)(2,1)S(1)}, u32[]{:S(2)}, u32[]{:S(2)}) collective-permute-start(bf16[128,1024]{1,0:T(8,128)(2,1)S(1)} %gate.1.refs_0_), channel_id=1, source_target_pairs={{0,6},{2,0},{4,2},{6,4},{1,7},{3,1},{5,3},{7,5},{8,14},{10,8},{12,... | collective-permute-start | bytes 786440 | tf_op jit(solution)/shard_map/ppermute | solution.py:346
  90.4 3.4 %copy-start = (bf16[16,4,64,1024]{3,2,1,0:T(8,128)(2,1)S(1)}, bf16[16,4,64,1024]{3,2,1,0:T(8,128)(2,1)}, u32[]{:S(2)}) copy-start(bf16[16,4,64,1024]{3,2,1,0:T(8,128)(2,1)} %all-gather.2.cloned.1.call-done.refs_2_) | copy-start | bytes 25165828
  93.7 9.3 %copy-start.1 = (bf16[16,4,64,1024]{3,2,1,0:T(8,128)(2,1)S(1)}, bf16[16,4,64,1024]{3,2,1,0:T(8,128)(2,1)}, u32[]{:S(2)}) copy-start(bf16[16,4,64,1024]{3,2,1,0:T(8,128)(2,1)} %all-gather.2.cloned.1.call-done.refs_2_) | copy-start | bytes 25165828
Sparse Core Ops, SparseCore 0:
  27.8 62.5 all-gather.1

commit v7 on v6

--- a/solution.py
+++ b/solution.py
@@ -297,11 +297,11 @@
     mixed = rest[-3]
     planes = weight.shape[1]
     half = weight.shape[0] // 2
-    here = lax.axis_index("seq") // weight.shape[0] - lax.axis_index("fsdp") + planes
+    here = lax.axis_index("fsdp")
 
     def copy(piece, part):
         some = pl.ds(part * half, half)
-        plane = lax.rem(here - offsets[piece] + planes, planes)
+        plane = lax.rem(here + offsets[piece], planes)
         return pltpu.make_async_copy(weight.at[some, plane], held.at[piece, some], sems.at[piece, part])
 
     for piece in range(count):
@@ -352,10 +352,10 @@
 def on_device(qkv, short_taps, lifetime, residues, skip_gain, segment_starts, out_weight):
     kinds = jnp.transpose(qkv, (1, 0, 2))
     inner = lax.axis_size("seq") // PLANES
-    edge, own_rows = lax.optimization_barrier((kinds[:, -(SHORT - 1) :, :], out_weight))
-    arrived = [shifted(edge, "seq", 1)] + [shifted(own_rows, "seq", inner * j) for j in range(1, PLANES)]
-    rim, *others = lax.optimization_barrier(arrived)
-    column = jnp.concatenate([own_rows] + others, axis=0).reshape(PLANES, *out_weight.shape)
+    rim = shifted(kinds[:, -(SHORT - 1) :, :], "seq", 1)
+    lines = [list(range(j, lax.axis_size("seq"), inner)) for j in range(inner)]
+    column = lax.all_gather(out_weight, "seq", axis=0, tiled=False, axis_index_groups=lines)
+    rim, column = lax.optimization_barrier((rim, column))
     groups = [list(range(x * inner, (x + 1) * inner)) for x in range(PLANES)]
     weight = lax.all_gather(column, "seq", axis=0, tiled=False, axis_index_groups=groups)
 
@@ -367,7 +367,8 @@
     gated = gate(entering, query, base, states)
     behind, ahead, across = (shifted(gated, "fsdp", by) for by in (1, 3, 2))
     total = project((0, 2), [gated, across], weight, None, F32)
-    return project((3, 1), [behind, ahead], weight, total, BF16)
+    total = project((3,), [behind], weight, total, F32)
+    return project((1,), [ahead], weight, total, BF16)
 
 
 def solution(mesh):

time: 113 us -> 111 us (0.982)
  blocking collectives: 20.4 us -> 32.9 us
  starting transfers between devices: 36.3 us -> 27 us
  waiting for transfers between devices: 18.1 us -> 14.2 us
  other arithmetic: 1.8 us -> 0 us
    all_gather x0 -> x1, blocking collectives: none -> 12.7 us  [on_device(): lax.all_gather(out_weight, 'seq', axis=0, tiled=False, axis_index_groups=...]
    ppermute x7 -> x4, starting transfers between devices: 31.9 us -> 22.6 us  [shifted(): return lax.ppermute(x, axis, [(i, (i + by) % count) for i in range(count)])]
    ppermute x7 -> x4, waiting for transfers between devices: 10.5 us -> 7.43 us  [shifted(): return lax.ppermute(x, axis, [(i, (i + by) % count) for i in range(count)])]
    concatenate x1 -> x0, other arithmetic: 1.8 us -> none  [on_device(): jnp.concatenate([own_rows] + others, axis=0)]
    pallas_call x2 -> x3, Pallas kernels: 3.22 us -> 3.37 us  [project(): pl.pallas_call(functools.partial(project_kernel, offsets), in_specs=[VMEM...]
  transfers between devices with their start and end apart: 9 -> 6, of which waited for: 5 -> 4; matrix products, arithmetic and copies ran while one was open for 0% -> 0% of each run, Pallas kernels for 10% -> 10%
where the time goes in v7:
time: 111 us; the launch traced here: 110 us
  blocking collectives  32.9 us (30%)
  starting transfers between devices  27 us (24%)
  waiting for transfers between devices  14.2 us (13%)
  between operations  13.5 us (12%)
  Pallas kernels  12.8 us (12%)
  local copies, waits for them, and re-layouts  9.95 us (9%)
    ppermute x4, starting transfers between devices, shifted(): return lax.ppermute(x, axis, [(i, (i + by) % count) for i in range(count)])  22.6 us
    all_to_all x1, blocking collectives, on_device(): all_fresh = lax.all_to_all(fresh, 'seq', 0, 0, tiled=True)  20.2 us
    all_gather x1, blocking collectives, on_device(): lax.all_gather(out_weight, 'seq', axis=0, tiled=False, axis_index_groups=...  12.7 us
    unnamed x18, local copies, waits for them, and re-layouts  9.14 us
    ppermute x4, waiting for transfers between devices, shifted(): return lax.ppermute(x, axis, [(i, (i + by) % count) for i in range(count)])  7.43 us
    all_to_all x1, starting transfers between devices, on_device(): states = lax.all_to_all(all_states, 'seq', 0, 0, tiled=True)  4.4 us
    all_gather x1, waiting for transfers between devices, on_device(): lax.all_gather(column, 'seq', axis=0, tiled=False, axis_index_groups=groups)  4.09 us
    pallas_call x1, Pallas kernels, base_work(): pl.pallas_call(base_kernel, grid=(chans // width,), in_specs=[SMEM, small...  3.77 us
  transfers between devices with their start and end apart: 6, of which 4 were waited for; matrix products, arithmetic and copies ran while one was open for 0% of the time, Pallas kernels for 10%

profile of v7, /device:TPU:1, one launch (start us, length us, event | category | flops | bytes accessed | tf_op | source)
XLA Modules:
  0.0 110.5 jit_solution(9330444048284342982)
XLA Ops:
  6.5 0.0 all-gather.4.cloned.1.call-start
  6.5 0.8 slice.4
  7.4 4.6 %collective-permute-start = (bf16[3,2,1024]{2,1,0:T(2,128)(2,1)S(1)}, bf16[3,2,1024]{2,1,0:T(2,128)(2,1)S(1)}, u32[]{:S(2)}, u32[]{:S(2)}) collective-permute-start(bf16[3,2,1024]{2,1,0:T(2,128)(2,1)S(1)} %slice.4), channel_id=1, source_target_pairs={{0,8},{8,16},{16,24},{24,32},{32,40},{40,48},{48,56},{56,64},{64,7... | collective-permute-start | bytes 36872 | tf_op jit(solution)/shard_map/ppermute | solution.py:346
  12.0 12.7 %all-gather = bf16[256,1024]{1,0:T(8,128)(2,1)} all-gather(bf16[64,1024]{1,0:T(8,128)(2,1)} %param.13), channel_id=2, replica_groups={{0,128,256,384},{8,136,264,392},{16,144,272,400},{24,152,280,408},{32,1..., dimensions={0}, use_global_device_ids=true | all-gather | bytes 655360 | tf_op jit(solution)/shard_map/all_gather | solution.py:357
  24.7 0.0 collective-permute-done.rim
  24.7 0.0 copy-start.8
  24.7 0.0 all-gather.4.cloned.1.call-update
  24.7 0.6 copy-done.8
  25.3 3.3 %features.1 = (f32[128,1024]{1,0:T(8,128)}, f32[128,1024]{1,0:T(8,128)}, f32[64,2,128]{2,1,0:T(2,128)}, f32[64,2,128]{2,1,0:T(2,128)}) custom-call(s32[8]{0:T(128)} %starts.5, f32[16,64]{1,0:T(8,128)} %bitcast.9, bf16[3,128,1024]{2,1,0:T(8,128)(2,1)} %bitcast.15, bf16[3,2,1024]{2,1,0:T(2,128)(2,1)} %copy-done.8, f32[3,3,1024]{2,1,0:T(4,128)} %taps.1), custom_call_target="tpu_custom_call" | custom-call | flops 100000000 | bytes 2500000 | tf_op jit(solution)/shard_map/features/pallas_call | solution.py:130
  28.6 20.2 %all_to_all.10.fresh = f32[64,2,128]{2,1,0:T(2,128)} all-to-all(f32[64,2,128]{2,1,0:T(2,128)} %get-tuple-element.18), channel_id=1, replica_groups=mesh['seq'=64,'fsdp'=4,'dp'=2] {'seq'}, dimensions={0} | all-to-all | bytes 131072 | tf_op jit(solution)/shard_map/all_to_all | solution.py:363
  48.8 1.7 %scan_blocks.1 = f32[64,2,128]{2,1,0:T(2,128)} custom-call(s32[8]{0:T(128)} %starts.5, f32[64,2,128]{2,1,0:T(2,128)} %all_to_all.10.fresh, f32[64,2,128]{2,1,0:T(2,128)} %get-tuple-element.19.decay), custom_call_target="tpu_custom_call" | custom-call | tf_op jit(solution)/shard_map/scan_blocks/pallas_call | solution.py:253
  50.5 4.4 %all-to-all-start.1 = ((f32[64,2,128]{2,1,0:T(2,128)}), f32[64,2,128]{2,1,0:T(2,128)S(1)}, u32[]{:S(2)}, u32[]{:S(2)}) async-start(f32[64,2,128]{2,1,0:T(2,128)} %scan_blocks.1), calls=%async_computation.1 | async-start | bytes 131072 | tf_op jit(solution)/shard_map/all_to_all | solution.py:366
  54.9 0.0 copy-start.3
  54.9 0.7 copy-done.3
  55.6 0.0 copy-start.4
  55.6 0.7 copy-done.4
  56.3 0.0 copy-start.5
  56.3 1.0 copy-done.5
  57.3 0.0 copy-start.6
  57.3 0.7 copy-done.6
  58.0 0.0 copy-start.7
  58.0 0.7 copy-done.7
  58.7 3.8 %base_work.1 = (f32[128,1024]{1,0:T(8,128)S(1)}, bf16[8,128,256]{2,1,0:T(8,128)(2,1)S(1)}) custom-call(s32[8]{0:T(128)S(1)} %copy-done.4, f32[16,64]{1,0:T(8,128)S(1)} %bitcast.10, f32[16,64]{1,0:T(8,128)S(1)} %bitcast.11, f32[128,1024]{1,0:T(8,128)S(1)} %copy-done.5, f32[1,1024]{1,0:T(1,128)S(1)} %bitcast.12), custom_call_target="tpu_custom_call" | custom-call | flops 1100000000 | bytes 1600000 | tf_op jit(solution)/shard_map/base_work/pallas_call | solution.py:223
  62.5 2.7 %all-to-all-done.1.states = f32[64,2,128]{2,1,0:T(2,128)S(1)} async-done(((f32[64,2,128]{2,1,0:T(2,128)}), f32[64,2,128]{2,1,0:T(2,128)S(1)}, u32[]{:S(2)}, u32[]{:S(2)}) %all-to-all-start.1) | async-done | bytes 65568 | tf_op jit(solution)/shard_map/all_to_all | solution.py:366
  65.2 0.0 copy-start.2
  65.2 1.1 copy-done.2
  66.2 0.6 gate.1.refs_0_
  66.9 10.6 %collective-permute-start.3 = (bf16[128,1024]{1,0:T(8,128)(2,1)S(1)}, bf16[128,1024]{1,0:T(8,128)(2,1)S(1)}, u32[]{:S(2)}, u32[]{:S(2)}) collective-permute-start(bf16[128,1024]{1,0:T(8,128)(2,1)S(1)} %gate.1.refs_0_), channel_id=1, source_target_pairs={{0,4},{2,6},{4,0},{6,2},{1,5},{3,7},{5,1},{7,3},{8,12},{10,14},{12... | collective-permute-start | bytes 786440 | tf_op jit(solution)/shard_map/ppermute | solution.py:346
  77.5 3.8 %collective-permute-start.2 = (bf16[128,1024]{1,0:T(8,128)(2,1)S(1)}, bf16[128,1024]{1,0:T(8,128)(2,1)S(1)}, u32[]{:S(2)}, u32[]{:S(2)}) collective-permute-start(bf16[128,1024]{1,0:T(8,128)(2,1)S(1)} %gate.1.refs_0_), channel_id=1, source_target_pairs={{0,2},{2,4},{4,6},{6,0},{1,3},{3,5},{5,7},{7,1},{8,10},{10,12},{12... | collective-permute-start | bytes 786440 | tf_op jit(solution)/shard_map/ppermute | solution.py:346
  81.4 3.6 %collective-permute-start.1 = (bf16[128,1024]{1,0:T(8,128)(2,1)S(1)}, bf16[128,1024]{1,0:T(8,128)(2,1)S(1)}, u32[]{:S(2)}, u32[]{:S(2)}) collective-permute-start(bf16[128,1024]{1,0:T(8,128)(2,1)S(1)} %gate.1.refs_0_), channel_id=1, source_target_pairs={{0,6},{2,0},{4,2},{6,4},{1,7},{3,1},{5,3},{7,5},{8,14},{10,8},{12,... | collective-permute-start | bytes 786440 | tf_op jit(solution)/shard_map/ppermute | solution.py:346
  84.9 0.0 collective-permute-done.3.refs_1_
  84.9 4.1 %all-gather.4.cloned.1.call-done = bf16[64,64,1024]{2,1,0:T(8,128)(2,1)} async-done(((bf16[4,64,1024]{2,1,0:T(8,128)(2,1)}), bf16[64,64,1024]{2,1,0:T(8,128)(2,1)}) %all-gather.4.cloned.1.call-update) | async-done | bytes 8388624 | tf_op jit(solution)/shard_map/all_gather | solution.py:360
  89.0 0.0 copy-start
  89.0 3.4 %copy-done = bf16[64,64,1024]{2,1,0:T(8,128)(2,1)S(1)} copy-done((bf16[64,64,1024]{2,1,0:T(8,128)(2,1)S(1)}, bf16[64,64,1024]{2,1,0:T(8,128)(2,1)}, u32[]{:S(2)}) %copy-start) | copy-done | bytes 8388632
  92.4 0.0 copy-start.1
  92.4 1.2 %project.3.refs_2_ = f32[128,1024]{1,0:T(8,128)S(1)} custom-call(bf16[128,1024]{1,0:T(8,128)(2,1)S(1)} %gate.1.refs_0_, bf16[128,1024]{1,0:T(8,128)(2,1)S(1)} %collective-permute-done.3.refs_1_, bf16[16,4,64,1024]{3,2,1,0:T(8,128)(2,1)S(1)} %bitcast.6), custom_call_target="tpu_custom_call" | custom-call | flops 536870912 | bytes 4194304 | tf_op jit(solution)/shard_map/project/pallas_call | solution.py:325
  93.7 1.8 %collective-permute-done.2.refs_0_ = bf16[128,1024]{1,0:T(8,128)(2,1)S(1)} collective-permute-done((bf16[128,1024]{1,0:T(8,128)(2,1)S(1)}, bf16[128,1024]{1,0:T(8,128)(2,1)S(1)}, u32[]{:S(2)}, u32[]{:S(2)}) %collective-permute-start.2) | collective-permute-done | bytes 262176 | tf_op jit(solution)/shard_map/ppermute | solution.py:346
  95.4 0.4 copy-done.1
  95.8 0.7 project.4.refs_2_
  96.5 5.7 %collective-permute-done.1.refs_0_ = bf16[128,1024]{1,0:T(8,128)(2,1)S(1)} collective-permute-done((bf16[128,1024]{1,0:T(8,128)(2,1)S(1)}, bf16[128,1024]{1,0:T(8,128)(2,1)S(1)}, u32[]{:S(2)}, u32[]{:S(2)}) %collective-permute-start.1) | collective-permute-done | bytes 262176 | tf_op jit(solution)/shard_map/ppermute | solution.py:346
  102.2 1.4 %project.5 = bf16[128,1024]{1,0:T(8,128)(2,1)} custom-call(bf16[128,1024]{1,0:T(8,128)(2,1)S(1)} %collective-permute-done.1.refs_0_, bf16[16,4,64,1024]{3,2,1,0:T(8,128)(2,1)S(1)} %bitcast.8, f32[128,1024]{1,0:T(8,128)S(1)} %project.4.refs_2_), custom_call_target="tpu_custom_call" | custom-call | flops 268435456 | bytes 2097152 | tf_op jit(solution)/shard_map/project/pallas_call | solution.py:325
Async XLA Ops:
  6.5 82.5 %all-gather.4.cloned.1.call-start = ((), (), s32[]{:S(2)}) async-start(), calls=%async_computation.2 | async-start | bytes 8912896 | tf_op jit(solution)/shard_map/all_gather | solution.py:360
  7.4 17.3 %collective-permute-start = (bf16[3,2,1024]{2,1,0:T(2,128)(2,1)S(1)}, bf16[3,2,1024]{2,1,0:T(2,128)(2,1)S(1)}, u32[]{:S(2)}, u32[]{:S(2)}) collective-permute-start(bf16[3,2,1024]{2,1,0:T(2,128)(2,1)S(1)} %slice.4), channel_id=1, source_target_pairs={{0,8},{8,16},{16,24},{24,32},{32,40},{40,48},{48,56},{56,64},{64,7... | collective-permute-start | bytes 36872 | tf_op jit(solution)/shard_map/ppermute | solution.py:346
  24.7 0.6 copy-start.8
  50.5 14.7 %all-to-all-start.1 = ((f32[64,2,128]{2,1,0:T(2,128)}), f32[64,2,128]{2,1,0:T(2,128)S(1)}, u32[]{:S(2)}, u32[]{:S(2)}) async-start(f32[64,2,128]{2,1,0:T(2,128)} %scan_blocks.1), calls=%async_computation.1 | async-start | bytes 131072 | tf_op jit(solution)/shard_map/all_to_all | solution.py:366
  54.9 0.7 copy-start.3
  55.6 0.7 copy-start.4
  56.3 1.0 copy-start.5
  57.3 0.7 copy-start.6
  58.0 0.7 copy-start.7
  65.2 1.1 copy-start.2
  66.9 18.1 %collective-permute-start.3 = (bf16[128,1024]{1,0:T(8,128)(2,1)S(1)}, bf16[128,1024]{1,0:T(8,128)(2,1)S(1)}, u32[]{:S(2)}, u32[]{:S(2)}) collective-permute-start(bf16[128,1024]{1,0:T(8,128)(2,1)S(1)} %gate.1.refs_0_), channel_id=1, source_target_pairs={{0,4},{2,6},{4,0},{6,2},{1,5},{3,7},{5,1},{7,3},{8,12},{10,14},{12... | collective-permute-start | bytes 786440 | tf_op jit(solution)/shard_map/ppermute | solution.py:346
  77.5 17.9 %collective-permute-start.2 = (bf16[128,1024]{1,0:T(8,128)(2,1)S(1)}, bf16[128,1024]{1,0:T(8,128)(2,1)S(1)}, u32[]{:S(2)}, u32[]{:S(2)}) collective-permute-start(bf16[128,1024]{1,0:T(8,128)(2,1)S(1)} %gate.1.refs_0_), channel_id=1, source_target_pairs={{0,2},{2,4},{4,6},{6,0},{1,3},{3,5},{5,7},{7,1},{8,10},{10,12},{12... | collective-permute-start | bytes 786440 | tf_op jit(solution)/shard_map/ppermute | solution.py:346
  81.4 20.8 %collective-permute-start.1 = (bf16[128,1024]{1,0:T(8,128)(2,1)S(1)}, bf16[128,1024]{1,0:T(8,128)(2,1)S(1)}, u32[]{:S(2)}, u32[]{:S(2)}) collective-permute-start(bf16[128,1024]{1,0:T(8,128)(2,1)S(1)} %gate.1.refs_0_), channel_id=1, source_target_pairs={{0,6},{2,0},{4,2},{6,4},{1,7},{3,1},{5,3},{7,5},{8,14},{10,8},{12,... | collective-permute-start | bytes 786440 | tf_op jit(solution)/shard_map/ppermute | solution.py:346
  89.0 3.4 %copy-start = (bf16[64,64,1024]{2,1,0:T(8,128)(2,1)S(1)}, bf16[64,64,1024]{2,1,0:T(8,128)(2,1)}, u32[]{:S(2)}) copy-start(bf16[64,64,1024]{2,1,0:T(8,128)(2,1)} %all-gather.4.cloned.1.call-done) | copy-start | bytes 25165828
  92.4 3.4 %copy-start.1 = (bf16[64,64,1024]{2,1,0:T(8,128)(2,1)S(1)}, bf16[64,64,1024]{2,1,0:T(8,128)(2,1)}, u32[]{:S(2)}) copy-start(bf16[64,64,1024]{2,1,0:T(8,128)(2,1)} %all-gather.4.cloned.1.call-done) | copy-start | bytes 25165828
Sparse Core Ops, SparseCore 0:
  24.9 64.1 all-gather.3

commit v8 on v7

--- a/solution.py
+++ b/solution.py
@@ -14,7 +14,7 @@
 PER_TILE = LANES // GROUP
 F32 = jnp.float32
 BF16 = jnp.bfloat16
-ROOMY = pltpu.CompilerParams(vmem_limit_bytes=60 * 1024 * 1024)
+ROOMY = pltpu.CompilerParams(vmem_limit_bytes=59 * 1024 * 1024)
 MODEST = pltpu.CompilerParams(vmem_limit_bytes=24 * 1024 * 1024)
 SMEM = pl.BlockSpec(memory_space=pltpu.SMEM)
 VMEM = pl.BlockSpec(memory_space=pltpu.VMEM)
@@ -68,7 +68,7 @@
 
 
 def features_kernel(
-    starts, lifetime, qkv, rim, taps, query, product, fresh, decay, rates
+    starts, lifetime, residues, skip, qkv, rim, taps, query, product, fresh, decay, aside, rates
 ):
     step = pl.program_id(0)
     first = lax.axis_index("seq") * LANES
@@ -78,6 +78,10 @@
     @pl.when(step == 0)
     def _():
         rates[...] = turned(1.0 / lifetime[...])
+        aside[...] = jnp.zeros(aside.shape, F32)
+        aside[:MODES, : lifetime.shape[1]] = lifetime[...]
+        aside[MODES : 2 * MODES, : residues.shape[1]] = residues[...]
+        aside[2 * MODES :, :] = skip[...]
 
     clear = not_start(starts, first + rows)
     clear_before = clear * not_start(starts, first + rows - 1)
@@ -120,7 +124,7 @@
             fresh[4 * mode + tile // 2, pl.ds(tile % 2, 1), :] = jnp.sum(some, axis=0, keepdims=True)
 
 
-def features(starts, lifetime, qkv, rim, taps):
+def features(starts, lifetime, residues, skip, qkv, rim, taps):
     chans = qkv.shape[2]
     tiles = chans // LANES
     width = FEATURE_TILES * LANES
@@ -133,6 +137,8 @@
         in_specs=[
             SMEM,
             small,
+            small,
+            pl.BlockSpec(skip.shape, lambda k: (0, 0)),
             pl.BlockSpec((3, LANES, width), lambda k: (0, 0, k)),
             pl.BlockSpec((3, SHORT - 1, width), lambda k: (0, 0, k)),
             pl.BlockSpec((SHORT, 3, width), lambda k: (0, 0, k)),
@@ -142,24 +148,26 @@
             flat,
             whole,
             whole,
+            pl.BlockSpec((2 * MODES + tiles, LANES), lambda k: (0, 0)),
         ],
         out_shape=[
             jax.ShapeDtypeStruct((LANES, chans), F32),
             jax.ShapeDtypeStruct((LANES, chans), F32),
             jax.ShapeDtypeStruct((8 * tiles, 2, LANES), F32),
             jax.ShapeDtypeStruct((8 * tiles, 2, LANES), F32),
+            jax.ShapeDtypeStruct((2 * MODES + tiles, LANES), F32),
         ],
         scratch_shapes=[pltpu.VMEM((LANES, LANES), F32)],
         compiler_params=ROOMY,
         cost_estimate=pl.CostEstimate(flops=100_000_000, bytes_accessed=2_500_000, transcendentals=200_000),
         name="features",
-    )(starts, lifetime, qkv, rim, taps)
+    )(starts, lifetime, residues, skip, qkv, rim, taps)
 
 
 BASE_TILES = 2
 
 
-def base_kernel(starts, lifetime, residues, product, skip, base, entering, rates, weights):
+def base_kernel(starts, aside, product, query, base, entering, same_query, rates, weights):
     step = pl.program_id(0)
     first = lax.axis_index("seq") * LANES
     rows = iota((LANES, LANES), 0)
@@ -167,7 +175,8 @@
 
     @pl.when(step == 0)
     def _():
-        rate = 1.0 / lifetime[...]
+        groups = product.shape[1] * pl.num_programs(0) // GROUP
+        rate = 1.0 / aside[:MODES, :groups]
         double = 2.0 * rate
         series = double * (
             1.0
@@ -175,7 +184,7 @@
             * (0.5 - double * (1.0 / 6 - double * (1.0 / 24 - double * (1.0 / 120 - double * (1.0 / 720)))))
         )
         rates[...] = turned(rate)
-        weights[...] = turned(residues[...] * jnp.sqrt(jnp.where(double < 0.07, series, 1.0 - jnp.exp(-double))))
+        weights[...] = turned(aside[MODES : 2 * MODES, :groups] * jnp.sqrt(jnp.where(double < 0.07, series, 1.0 - jnp.exp(-double))))
 
     seg_col = segment_of(starts, first + cols)
     linked = ((segment_of(starts, first + rows) == seg_col) & (rows >= cols)).astype(F32)
@@ -204,7 +213,7 @@
         span = slice(part * LANES, (part + 1) * LANES)
         values = product[:, span]
         both = doubled(values)
-        total = skip[:, span] * values
+        total = aside[pl.ds(2 * MODES + tile, 1), :] * values
         for group in range(PER_TILE):
             spread = jnp.broadcast_to(lags[group : group + 1, :], (LANES, LANES))
             rolled = pltpu.roll(spread, 0, 1, stride=1, stride_axis=0)
@@ -212,28 +221,29 @@
             out = split_dot(jnp.concatenate([high, low], axis=1), both)
             total = total + jnp.where(cols // GROUP == group, out, 0.0)
         base[:, span] = total
-
-
-def base_work(starts, lifetime, residues, product, skip):
+    same_query[...] = query[...]
+
+
+def base_work(starts, aside, product, query):
     chans = product.shape[1]
     tiles = chans // LANES
     width = BASE_TILES * LANES
     flat = pl.BlockSpec((LANES, width), lambda k: (0, k))
-    small = pl.BlockSpec(lifetime.shape, lambda k: (0, 0))
     return pl.pallas_call(
         base_kernel,
         grid=(chans // width,),
-        in_specs=[SMEM, small, small, flat, pl.BlockSpec((1, width), lambda k: (0, k))],
-        out_specs=[flat, pl.BlockSpec((BASE_TILES, LANES, 2 * LANES), lambda k: (k, 0, 0))],
+        in_specs=[SMEM, pl.BlockSpec(aside.shape, lambda k: (0, 0)), flat, flat],
+        out_specs=[flat, pl.BlockSpec((BASE_TILES, LANES, 2 * LANES), lambda k: (k, 0, 0)), flat],
         out_shape=[
             jax.ShapeDtypeStruct((LANES, chans), F32),
             jax.ShapeDtypeStruct((tiles, LANES, 2 * LANES), BF16),
+            jax.ShapeDtypeStruct((LANES, chans), F32),
         ],
         scratch_shapes=[pltpu.VMEM((LANES, LANES), F32), pltpu.VMEM((LANES, LANES), F32)],
         compiler_params=MODEST,
         cost_estimate=pl.CostEstimate(flops=1_100_000_000, bytes_accessed=1_600_000, transcendentals=400_000),
         name="base_work",
-    )(starts, lifetime, residues, product, skip)
+    )(starts, aside, product, query)
 
 
 def scan_kernel(starts, fresh, decay, entering):
@@ -359,9 +369,11 @@
     groups = [list(range(x * inner, (x + 1) * inner)) for x in range(PLANES)]
     weight = lax.all_gather(column, "seq", axis=0, tiled=False, axis_index_groups=groups)
 
-    query, product, fresh, decay = features(segment_starts, lifetime.T, kinds, rim, short_taps)
+    query, product, fresh, decay, aside = features(
+        segment_starts, lifetime.T, residues.T, skip_gain.reshape(-1, LANES), kinds, rim, short_taps
+    )
     all_fresh = lax.all_to_all(fresh, "seq", 0, 0, tiled=True)
-    base, entering = base_work(segment_starts, lifetime.T, residues.T, product, skip_gain[None, :])
+    base, entering, query = base_work(segment_starts, aside, product, query)
     all_states = scan_blocks(segment_starts, all_fresh, decay)
     states = lax.all_to_all(all_states, "seq", 0, 0, tiled=True)
     gated = gate(entering, query, base, states)

time: 111 us -> 110 us (level)
    ppermute x4, waiting for transfers between devices: 7.43 us -> 5.84 us  [shifted(): return lax.ppermute(x, axis, [(i, (i + by) % count) for i in range(count)])]
    unnamed x18 -> x14, local copies, waits for them, and re-layouts: 9.14 us -> 8.47 us
  transfers between devices with their start and end apart: 6 -> 6, of which waited for: 4 -> 4; matrix products, arithmetic and copies ran while one was open for 0% -> 0% of each run, Pallas kernels for 10% -> 11%
where the time goes in v8:
time: 110 us
  blocking collectives  32.9 us (30%)
  starting transfers between devices  27.1 us (25%)
  waiting for transfers between devices  13.7 us (12%)
  between operations  13.5 us (12%)
  Pallas kernels  13 us (12%)
  local copies, waits for them, and re-layouts  9.29 us (8%)
    ppermute x4, starting transfers between devices, shifted(): return lax.ppermute(x, axis, [(i, (i + by) % count) for i in range(count)])  22.7 us
    all_to_all x1, blocking collectives, on_device(): all_fresh = lax.all_to_all(fresh, 'seq', 0, 0, tiled=True)  20.2 us
    all_gather x1, blocking collectives, on_device(): lax.all_gather(out_weight, 'seq', axis=0, tiled=False, axis_index_groups=...  12.7 us
    unnamed x14, local copies, waits for them, and re-layouts  8.47 us
    ppermute x4, waiting for transfers between devices, shifted(): return lax.ppermute(x, axis, [(i, (i + by) % count) for i in range(count)])  5.84 us
    all_gather x1, waiting for transfers between devices, on_device(): lax.all_gather(column, 'seq', axis=0, tiled=False, axis_index_groups=groups)  5 us
    all_to_all x1, starting transfers between devices, on_device(): states = lax.all_to_all(all_states, 'seq', 0, 0, tiled=True)  4.4 us
    pallas_call x1, Pallas kernels, base_work(): pl.pallas_call(base_kernel, grid=(chans // width,), in_specs=[SMEM, pl.Bl...  3.89 us
  transfers between devices with their start and end apart: 6, of which 4 were waited for; matrix products, arithmetic and copies ran while one was open for 0% of the time, Pallas kernels for 11%

profile of v8, /device:TPU:1, one launch (start us, length us, event | category | flops | bytes accessed | tf_op | source)
XLA Modules:
  0.0 109.6 jit_solution(11243900183825898625)
XLA Ops:
  6.5 0.0 all-gather.4.cloned.1.call-start
  6.5 0.8 slice.4
  7.4 4.6 %collective-permute-start = (bf16[3,2,1024]{2,1,0:T(2,128)(2,1)S(1)}, bf16[3,2,1024]{2,1,0:T(2,128)(2,1)S(1)}, u32[]{:S(2)}, u32[]{:S(2)}) collective-permute-start(bf16[3,2,1024]{2,1,0:T(2,128)(2,1)S(1)} %slice.4), channel_id=1, source_target_pairs={{0,8},{8,16},{16,24},{24,32},{32,40},{40,48},{48,56},{56,64},{64,7... | collective-permute-start | bytes 36872 | tf_op jit(solution)/shard_map/ppermute | solution.py:356
  12.0 12.7 %all-gather = bf16[256,1024]{1,0:T(8,128)(2,1)} all-gather(bf16[64,1024]{1,0:T(8,128)(2,1)} %param.13), channel_id=2, replica_groups={{0,128,256,384},{8,136,264,392},{16,144,272,400},{24,152,280,408},{32,1..., dimensions={0}, use_global_device_ids=true | all-gather | bytes 655360 | tf_op jit(solution)/shard_map/all_gather | solution.py:367
  24.7 0.0 collective-permute-done.rim
  24.7 0.0 copy-start.6
  24.7 0.0 all-gather.4.cloned.1.call-update
  24.7 0.6 copy-done.6
  25.3 3.4 %features.1 = (f32[128,1024]{1,0:T(8,128)}, f32[128,1024]{1,0:T(8,128)}, f32[64,2,128]{2,1,0:T(2,128)}, f32[64,2,128]{2,1,0:T(2,128)}, f32[40,128]{1,0:T(8,128)}) custom-call(s32[8]{0:T(128)} %starts.5, f32[16,64]{1,0:T(8,128)} %bitcast.12, f32[16,64]{1,0:T(8,128)} %bitcast.13, f32[8,128]{1,0:T(8,128)} %bitcast.14, bf16[3,128,1024]{2,1,0:T(8,128)(2,1)} %bitcast.11, ...), custom_call_target="tpu_custom_call" | custom-call | flops 100000000 | bytes 2500000 | tf_op jit(solution)/shard_map/features/pallas_call | solution.py:134
  28.7 20.2 %all_to_all.10.fresh = f32[64,2,128]{2,1,0:T(2,128)} all-to-all(f32[64,2,128]{2,1,0:T(2,128)} %get-tuple-element.22), channel_id=1, replica_groups=mesh['seq'=64,'fsdp'=4,'dp'=2] {'seq'}, dimensions={0} | all-to-all | bytes 131072 | tf_op jit(solution)/shard_map/all_to_all | solution.py:375
  48.9 1.7 %scan_blocks.1 = f32[64,2,128]{2,1,0:T(2,128)} custom-call(s32[8]{0:T(128)} %starts.5, f32[64,2,128]{2,1,0:T(2,128)} %all_to_all.10.fresh, f32[64,2,128]{2,1,0:T(2,128)} %get-tuple-element.23.decay), custom_call_target="tpu_custom_call" | custom-call | tf_op jit(solution)/shard_map/scan_blocks/pallas_call | solution.py:263
  50.6 4.4 %all-to-all-start.1 = ((f32[64,2,128]{2,1,0:T(2,128)}), f32[64,2,128]{2,1,0:T(2,128)S(1)}, u32[]{:S(2)}, u32[]{:S(2)}) async-start(f32[64,2,128]{2,1,0:T(2,128)} %scan_blocks.1), calls=%async_computation.1 | async-start | bytes 131072 | tf_op jit(solution)/shard_map/all_to_all | solution.py:378
  55.0 0.0 copy-start.2
  55.0 0.6 copy-done.2
  55.6 0.0 copy-start.3
  55.6 1.0 copy-done.3
  56.7 0.0 copy-start.4
  56.7 1.1 copy-done.4
  57.7 0.0 copy-start.5
  57.7 0.7 copy-done.5
  58.5 3.9 %base_work.1 = (f32[128,1024]{1,0:T(8,128)S(1)}, bf16[8,128,256]{2,1,0:T(8,128)(2,1)S(1)}, f32[128,1024]{1,0:T(8,128)S(1)}) custom-call(s32[8]{0:T(128)S(1)} %copy-done.2, f32[40,128]{1,0:T(8,128)S(1)} %copy-done.5, f32[128,1024]{1,0:T(8,128)S(1)} %copy-done.4, f32[128,1024]{1,0:T(8,128)S(1)} %copy-done.3), custom_call_target="tpu_custom_call" | custom-call | flops 1100000000 | bytes 1600000 | tf_op jit(solution)/shard_map/base_work/pallas_call | solution.py:232
  62.4 2.9 %all-to-all-done.1.states = f32[64,2,128]{2,1,0:T(2,128)S(1)} async-done(((f32[64,2,128]{2,1,0:T(2,128)}), f32[64,2,128]{2,1,0:T(2,128)S(1)}, u32[]{:S(2)}, u32[]{:S(2)}) %all-to-all-start.1) | async-done | bytes 65568 | tf_op jit(solution)/shard_map/all_to_all | solution.py:378
  65.2 0.6 gate.1.refs_0_
  65.9 10.7 %collective-permute-start.3 = (bf16[128,1024]{1,0:T(8,128)(2,1)S(1)}, bf16[128,1024]{1,0:T(8,128)(2,1)S(1)}, u32[]{:S(2)}, u32[]{:S(2)}) collective-permute-start(bf16[128,1024]{1,0:T(8,128)(2,1)S(1)} %gate.1.refs_0_), channel_id=1, source_target_pairs={{0,4},{2,6},{4,0},{6,2},{1,5},{3,7},{5,1},{7,3},{8,12},{10,14},{12... | collective-permute-start | bytes 786440 | tf_op jit(solution)/shard_map/ppermute | solution.py:356
  76.6 4.0 %collective-permute-start.2 = (bf16[128,1024]{1,0:T(8,128)(2,1)S(1)}, bf16[128,1024]{1,0:T(8,128)(2,1)S(1)}, u32[]{:S(2)}, u32[]{:S(2)}) collective-permute-start(bf16[128,1024]{1,0:T(8,128)(2,1)S(1)} %gate.1.refs_0_), channel_id=1, source_target_pairs={{0,2},{2,4},{4,6},{6,0},{1,3},{3,5},{5,7},{7,1},{8,10},{10,12},{12... | collective-permute-start | bytes 786440 | tf_op jit(solution)/shard_map/ppermute | solution.py:356
  80.6 3.4 %collective-permute-start.1 = (bf16[128,1024]{1,0:T(8,128)(2,1)S(1)}, bf16[128,1024]{1,0:T(8,128)(2,1)S(1)}, u32[]{:S(2)}, u32[]{:S(2)}) collective-permute-start(bf16[128,1024]{1,0:T(8,128)(2,1)S(1)} %gate.1.refs_0_), channel_id=1, source_target_pairs={{0,6},{2,0},{4,2},{6,4},{1,7},{3,1},{5,3},{7,5},{8,14},{10,8},{12,... | collective-permute-start | bytes 786440 | tf_op jit(solution)/shard_map/ppermute | solution.py:356
  84.0 0.0 collective-permute-done.3.refs_1_
  84.0 5.0 %all-gather.4.cloned.1.call-done = bf16[64,64,1024]{2,1,0:T(8,128)(2,1)} async-done(((bf16[4,64,1024]{2,1,0:T(8,128)(2,1)}), bf16[64,64,1024]{2,1,0:T(8,128)(2,1)}) %all-gather.4.cloned.1.call-update) | async-done | bytes 8388624 | tf_op jit(solution)/shard_map/all_gather | solution.py:370
  89.0 0.0 copy-start
  89.0 3.4 %copy-done = bf16[64,64,1024]{2,1,0:T(8,128)(2,1)S(1)} copy-done((bf16[64,64,1024]{2,1,0:T(8,128)(2,1)S(1)}, bf16[64,64,1024]{2,1,0:T(8,128)(2,1)}, u32[]{:S(2)}) %copy-start) | copy-done | bytes 8388632
  92.4 0.0 copy-start.1
  92.4 1.2 %project.3.refs_2_ = f32[128,1024]{1,0:T(8,128)S(1)} custom-call(bf16[128,1024]{1,0:T(8,128)(2,1)S(1)} %gate.1.refs_0_, bf16[128,1024]{1,0:T(8,128)(2,1)S(1)} %collective-permute-done.3.refs_1_, bf16[16,4,64,1024]{3,2,1,0:T(8,128)(2,1)S(1)} %bitcast.6), custom_call_target="tpu_custom_call" | custom-call | flops 536870912 | bytes 4194304 | tf_op jit(solution)/shard_map/project/pallas_call | solution.py:335
  93.7 1.1 collective-permute-done.2.refs_0_
  94.8 1.0 copy-done.1
  95.8 0.7 project.4.refs_2_
  96.5 4.8 %collective-permute-done.1.refs_0_ = bf16[128,1024]{1,0:T(8,128)(2,1)S(1)} collective-permute-done((bf16[128,1024]{1,0:T(8,128)(2,1)S(1)}, bf16[128,1024]{1,0:T(8,128)(2,1)S(1)}, u32[]{:S(2)}, u32[]{:S(2)}) %collective-permute-start.1) | collective-permute-done | bytes 262176 | tf_op jit(solution)/shard_map/ppermute | solution.py:356
  101.3 1.4 %project.5 = bf16[128,1024]{1,0:T(8,128)(2,1)} custom-call(bf16[128,1024]{1,0:T(8,128)(2,1)S(1)} %collective-permute-done.1.refs_0_, bf16[16,4,64,1024]{3,2,1,0:T(8,128)(2,1)S(1)} %bitcast.8, f32[128,1024]{1,0:T(8,128)S(1)} %project.4.refs_2_), custom_call_target="tpu_custom_call" | custom-call | flops 268435456 | bytes 2097152 | tf_op jit(solution)/shard_map/project/pallas_call | solution.py:335
Async XLA Ops:
  6.5 82.5 %all-gather.4.cloned.1.call-start = ((), (), s32[]{:S(2)}) async-start(), calls=%async_computation.2 | async-start | bytes 8912896 | tf_op jit(solution)/shard_map/all_gather | solution.py:370
  7.4 17.3 %collective-permute-start = (bf16[3,2,1024]{2,1,0:T(2,128)(2,1)S(1)}, bf16[3,2,1024]{2,1,0:T(2,128)(2,1)S(1)}, u32[]{:S(2)}, u32[]{:S(2)}) collective-permute-start(bf16[3,2,1024]{2,1,0:T(2,128)(2,1)S(1)} %slice.4), channel_id=1, source_target_pairs={{0,8},{8,16},{16,24},{24,32},{32,40},{40,48},{48,56},{56,64},{64,7... | collective-permute-start | bytes 36872 | tf_op jit(solution)/shard_map/ppermute | solution.py:356
  24.7 0.6 copy-start.6
  50.6 14.7 %all-to-all-start.1 = ((f32[64,2,128]{2,1,0:T(2,128)}), f32[64,2,128]{2,1,0:T(2,128)S(1)}, u32[]{:S(2)}, u32[]{:S(2)}) async-start(f32[64,2,128]{2,1,0:T(2,128)} %scan_blocks.1), calls=%async_computation.1 | async-start | bytes 131072 | tf_op jit(solution)/shard_map/all_to_all | solution.py:378
  55.0 0.7 copy-start.2
  55.6 1.1 copy-start.3
  56.7 1.1 copy-start.4
  57.7 0.7 copy-start.5
  65.9 18.2 %collective-permute-start.3 = (bf16[128,1024]{1,0:T(8,128)(2,1)S(1)}, bf16[128,1024]{1,0:T(8,128)(2,1)S(1)}, u32[]{:S(2)}, u32[]{:S(2)}) collective-permute-start(bf16[128,1024]{1,0:T(8,128)(2,1)S(1)} %gate.1.refs_0_), channel_id=1, source_target_pairs={{0,4},{2,6},{4,0},{6,2},{1,5},{3,7},{5,1},{7,3},{8,12},{10,14},{12... | collective-permute-start | bytes 786440 | tf_op jit(solution)/shard_map/ppermute | solution.py:356
  76.6 18.1 %collective-permute-start.2 = (bf16[128,1024]{1,0:T(8,128)(2,1)S(1)}, bf16[128,1024]{1,0:T(8,128)(2,1)S(1)}, u32[]{:S(2)}, u32[]{:S(2)}) collective-permute-start(bf16[128,1024]{1,0:T(8,128)(2,1)S(1)} %gate.1.refs_0_), channel_id=1, source_target_pairs={{0,2},{2,4},{4,6},{6,0},{1,3},{3,5},{5,7},{7,1},{8,10},{10,12},{12... | collective-permute-start | bytes 786440 | tf_op jit(solution)/shard_map/ppermute | solution.py:356
  80.6 20.7 %collective-permute-start.1 = (bf16[128,1024]{1,0:T(8,128)(2,1)S(1)}, bf16[128,1024]{1,0:T(8,128)(2,1)S(1)}, u32[]{:S(2)}, u32[]{:S(2)}) collective-permute-start(bf16[128,1024]{1,0:T(8,128)(2,1)S(1)} %gate.1.refs_0_), channel_id=1, source_target_pairs={{0,6},{2,0},{4,2},{6,4},{1,7},{3,1},{5,3},{7,5},{8,14},{10,8},{12,... | collective-permute-start | bytes 786440 | tf_op jit(solution)/shard_map/ppermute | solution.py:356
  89.0 3.4 %copy-start = (bf16[64,64,1024]{2,1,0:T(8,128)(2,1)S(1)}, bf16[64,64,1024]{2,1,0:T(8,128)(2,1)}, u32[]{:S(2)}) copy-start(bf16[64,64,1024]{2,1,0:T(8,128)(2,1)} %all-gather.4.cloned.1.call-done) | copy-start | bytes 25165828
  92.4 3.4 %copy-start.1 = (bf16[64,64,1024]{2,1,0:T(8,128)(2,1)S(1)}, bf16[64,64,1024]{2,1,0:T(8,128)(2,1)}, u32[]{:S(2)}) copy-start(bf16[64,64,1024]{2,1,0:T(8,128)(2,1)} %all-gather.4.cloned.1.call-done) | copy-start | bytes 25165828
Sparse Core Ops, SparseCore 0:
  24.8 64.1 all-gather.3

commit v9 on v8

--- a/solution.py
+++ b/solution.py
@@ -164,7 +164,7 @@
     )(starts, lifetime, residues, skip, qkv, rim, taps)
 
 
-BASE_TILES = 2
+BASE_TILES = 4
 
 
 def base_kernel(starts, aside, product, query, base, entering, same_query, rates, weights):
@@ -269,7 +269,7 @@
     )(starts, fresh, decay)
 
 
-GATE_TILES = 4
+GATE_TILES = 8
 
 
 def gate_kernel(entering, query, base, states, gated):

time: 110 us -> 110 us (level)
  transfers between devices with their start and end apart: 6 -> 6, of which waited for: 4 -> 4; matrix products, arithmetic and copies ran while one was open for 0% -> 0% of each run, Pallas kernels for 11% -> 10%
where the time goes in v9:
time: 110 us; the launch traced here: 109 us
  blocking collectives  32.9 us (30%)
  starting transfers between devices  27.1 us (25%)
  waiting for transfers between devices  13.8 us (13%)
  between operations  13.5 us (12%)
  Pallas kernels  12.3 us (11%)
  local copies, waits for them, and re-layouts  9.59 us (9%)
    ppermute x4, starting transfers between devices, shifted(): return lax.ppermute(x, axis, [(i, (i + by) % count) for i in range(count)])  22.7 us
    all_to_all x1, blocking collectives, on_device(): all_fresh = lax.all_to_all(fresh, 'seq', 0, 0, tiled=True)  20.2 us
    all_gather x1, blocking collectives, on_device(): lax.all_gather(out_weight, 'seq', axis=0, tiled=False, axis_index_groups=...  12.7 us
    unnamed x14, local copies, waits for them, and re-layouts  8.78 us
    all_gather x1, waiting for transfers between devices, on_device(): lax.all_gather(column, 'seq', axis=0, tiled=False, axis_index_groups=groups)  5.33 us
    ppermute x4, waiting for transfers between devices, shifted(): return lax.ppermute(x, axis, [(i, (i + by) % count) for i in range(count)])  5.21 us
    all_to_all x1, starting transfers between devices, on_device(): states = lax.all_to_all(all_states, 'seq', 0, 0, tiled=True)  4.4 us
    pallas_call x1, Pallas kernels, base_work(): pl.pallas_call(base_kernel, grid=(chans // width,), in_specs=[SMEM, pl.Bl...  3.46 us
  transfers between devices with their start and end apart: 6, of which 4 were waited for; matrix products, arithmetic and copies ran while one was open for 0% of the time, Pallas kernels for 10%

profile of v9, /device:TPU:1, one launch (start us, length us, event | category | flops | bytes accessed | tf_op | source)
XLA Modules:
  0.0 109.2 jit_solution(9758245852251570720)
XLA Ops:
  6.5 0.0 all-gather.4.cloned.1.call-start
  6.5 0.8 slice.4
  7.4 4.6 %collective-permute-start = (bf16[3,2,1024]{2,1,0:T(2,128)(2,1)S(1)}, bf16[3,2,1024]{2,1,0:T(2,128)(2,1)S(1)}, u32[]{:S(2)}, u32[]{:S(2)}) collective-permute-start(bf16[3,2,1024]{2,1,0:T(2,128)(2,1)S(1)} %slice.4), channel_id=1, source_target_pairs={{0,8},{8,16},{16,24},{24,32},{32,40},{40,48},{48,56},{56,64},{64,7... | collective-permute-start | bytes 36872 | tf_op jit(solution)/shard_map/ppermute | solution.py:356
  12.0 12.7 %all-gather = bf16[256,1024]{1,0:T(8,128)(2,1)} all-gather(bf16[64,1024]{1,0:T(8,128)(2,1)} %param.13), channel_id=2, replica_groups={{0,128,256,384},{8,136,264,392},{16,144,272,400},{24,152,280,408},{32,1..., dimensions={0}, use_global_device_ids=true | all-gather | bytes 655360 | tf_op jit(solution)/shard_map/all_gather | solution.py:367
  24.7 0.0 collective-permute-done.rim
  24.7 0.0 copy-start.6
  24.7 0.0 all-gather.4.cloned.1.call-update
  24.7 0.6 copy-done.6
  25.3 3.4 %features.1 = (f32[128,1024]{1,0:T(8,128)}, f32[128,1024]{1,0:T(8,128)}, f32[64,2,128]{2,1,0:T(2,128)}, f32[64,2,128]{2,1,0:T(2,128)}, f32[40,128]{1,0:T(8,128)}) custom-call(s32[8]{0:T(128)} %starts.5, f32[16,64]{1,0:T(8,128)} %bitcast.12, f32[16,64]{1,0:T(8,128)} %bitcast.13, f32[8,128]{1,0:T(8,128)} %bitcast.14, bf16[3,128,1024]{2,1,0:T(8,128)(2,1)} %bitcast.11, ...), custom_call_target="tpu_custom_call" | custom-call | flops 100000000 | bytes 2500000 | tf_op jit(solution)/shard_map/features/pallas_call | solution.py:134
  28.7 20.2 %all_to_all.10.fresh = f32[64,2,128]{2,1,0:T(2,128)} all-to-all(f32[64,2,128]{2,1,0:T(2,128)} %get-tuple-element.22), channel_id=1, replica_groups=mesh['seq'=64,'fsdp'=4,'dp'=2] {'seq'}, dimensions={0} | all-to-all | bytes 131072 | tf_op jit(solution)/shard_map/all_to_all | solution.py:375
  48.9 1.7 %scan_blocks.1 = f32[64,2,128]{2,1,0:T(2,128)} custom-call(s32[8]{0:T(128)} %starts.5, f32[64,2,128]{2,1,0:T(2,128)} %all_to_all.10.fresh, f32[64,2,128]{2,1,0:T(2,128)} %get-tuple-element.23.decay), custom_call_target="tpu_custom_call" | custom-call | tf_op jit(solution)/shard_map/scan_blocks/pallas_call | solution.py:263
  50.6 4.4 %all-to-all-start.1 = ((f32[64,2,128]{2,1,0:T(2,128)}), f32[64,2,128]{2,1,0:T(2,128)S(1)}, u32[]{:S(2)}, u32[]{:S(2)}) async-start(f32[64,2,128]{2,1,0:T(2,128)} %scan_blocks.1), calls=%async_computation.1 | async-start | bytes 131072 | tf_op jit(solution)/shard_map/all_to_all | solution.py:378
  55.0 0.0 copy-start.2
  55.0 0.6 copy-done.2
  55.6 0.0 copy-start.3
  55.6 1.0 copy-done.3
  56.7 0.0 copy-start.4
  56.7 1.1 copy-done.4
  57.7 0.0 copy-start.5
  57.7 0.7 copy-done.5
  58.5 3.5 %base_work.1 = (f32[128,1024]{1,0:T(8,128)S(1)}, bf16[8,128,256]{2,1,0:T(8,128)(2,1)S(1)}, f32[128,1024]{1,0:T(8,128)S(1)}) custom-call(s32[8]{0:T(128)S(1)} %copy-done.2, f32[40,128]{1,0:T(8,128)S(1)} %copy-done.5, f32[128,1024]{1,0:T(8,128)S(1)} %copy-done.4, f32[128,1024]{1,0:T(8,128)S(1)} %copy-done.3), custom_call_target="tpu_custom_call" | custom-call | flops 1100000000 | bytes 1600000 | tf_op jit(solution)/shard_map/base_work/pallas_call | solution.py:232
  61.9 3.3 %all-to-all-done.1.states = f32[64,2,128]{2,1,0:T(2,128)S(1)} async-done(((f32[64,2,128]{2,1,0:T(2,128)}), f32[64,2,128]{2,1,0:T(2,128)S(1)}, u32[]{:S(2)}, u32[]{:S(2)}) %all-to-all-start.1) | async-done | bytes 65568 | tf_op jit(solution)/shard_map/all_to_all | solution.py:378
  65.2 0.3 gate.1.refs_0_
  65.6 10.7 %collective-permute-start.3 = (bf16[128,1024]{1,0:T(8,128)(2,1)S(1)}, bf16[128,1024]{1,0:T(8,128)(2,1)S(1)}, u32[]{:S(2)}, u32[]{:S(2)}) collective-permute-start(bf16[128,1024]{1,0:T(8,128)(2,1)S(1)} %gate.1.refs_0_), channel_id=1, source_target_pairs={{0,4},{2,6},{4,0},{6,2},{1,5},{3,7},{5,1},{7,3},{8,12},{10,14},{12... | collective-permute-start | bytes 786440 | tf_op jit(solution)/shard_map/ppermute | solution.py:356
  76.3 4.0 %collective-permute-start.2 = (bf16[128,1024]{1,0:T(8,128)(2,1)S(1)}, bf16[128,1024]{1,0:T(8,128)(2,1)S(1)}, u32[]{:S(2)}, u32[]{:S(2)}) collective-permute-start(bf16[128,1024]{1,0:T(8,128)(2,1)S(1)} %gate.1.refs_0_), channel_id=1, source_target_pairs={{0,2},{2,4},{4,6},{6,0},{1,3},{3,5},{5,7},{7,1},{8,10},{10,12},{12... | collective-permute-start | bytes 786440 | tf_op jit(solution)/shard_map/ppermute | solution.py:356
  80.3 3.4 %collective-permute-start.1 = (bf16[128,1024]{1,0:T(8,128)(2,1)S(1)}, bf16[128,1024]{1,0:T(8,128)(2,1)S(1)}, u32[]{:S(2)}, u32[]{:S(2)}) collective-permute-start(bf16[128,1024]{1,0:T(8,128)(2,1)S(1)} %gate.1.refs_0_), channel_id=1, source_target_pairs={{0,6},{2,0},{4,2},{6,4},{1,7},{3,1},{5,3},{7,5},{8,14},{10,8},{12,... | collective-permute-start | bytes 786440 | tf_op jit(solution)/shard_map/ppermute | solution.py:356
  83.7 0.0 collective-permute-done.3.refs_1_
  83.7 5.3 %all-gather.4.cloned.1.call-done = bf16[64,64,1024]{2,1,0:T(8,128)(2,1)} async-done(((bf16[4,64,1024]{2,1,0:T(8,128)(2,1)}), bf16[64,64,1024]{2,1,0:T(8,128)(2,1)}) %all-gather.4.cloned.1.call-update) | async-done | bytes 8388624 | tf_op jit(solution)/shard_map/all_gather | solution.py:370
  89.0 0.0 copy-start
  89.0 3.4 %copy-done = bf16[64,64,1024]{2,1,0:T(8,128)(2,1)S(1)} copy-done((bf16[64,64,1024]{2,1,0:T(8,128)(2,1)S(1)}, bf16[64,64,1024]{2,1,0:T(8,128)(2,1)}, u32[]{:S(2)}) %copy-start) | copy-done | bytes 8388632
  92.4 0.0 copy-start.1
  92.4 1.2 %project.3.refs_2_ = f32[128,1024]{1,0:T(8,128)S(1)} custom-call(bf16[128,1024]{1,0:T(8,128)(2,1)S(1)} %gate.1.refs_0_, bf16[128,1024]{1,0:T(8,128)(2,1)S(1)} %collective-permute-done.3.refs_1_, bf16[16,4,64,1024]{3,2,1,0:T(8,128)(2,1)S(1)} %bitcast.6), custom_call_target="tpu_custom_call" | custom-call | flops 536870912 | bytes 4194304 | tf_op jit(solution)/shard_map/project/pallas_call | solution.py:335
  93.7 0.8 collective-permute-done.2.refs_0_
  94.5 1.3 %copy-done.1 = bf16[64,64,1024]{2,1,0:T(8,128)(2,1)S(1)} copy-done((bf16[64,64,1024]{2,1,0:T(8,128)(2,1)S(1)}, bf16[64,64,1024]{2,1,0:T(8,128)(2,1)}, u32[]{:S(2)}) %copy-start.1) | copy-done | bytes 8388632
  95.8 0.7 project.4.refs_2_
  96.5 4.4 %collective-permute-done.1.refs_0_ = bf16[128,1024]{1,0:T(8,128)(2,1)S(1)} collective-permute-done((bf16[128,1024]{1,0:T(8,128)(2,1)S(1)}, bf16[128,1024]{1,0:T(8,128)(2,1)S(1)}, u32[]{:S(2)}, u32[]{:S(2)}) %collective-permute-start.1) | collective-permute-done | bytes 262176 | tf_op jit(solution)/shard_map/ppermute | solution.py:356
  101.0 1.4 %project.5 = bf16[128,1024]{1,0:T(8,128)(2,1)} custom-call(bf16[128,1024]{1,0:T(8,128)(2,1)S(1)} %collective-permute-done.1.refs_0_, bf16[16,4,64,1024]{3,2,1,0:T(8,128)(2,1)S(1)} %bitcast.8, f32[128,1024]{1,0:T(8,128)S(1)} %project.4.refs_2_), custom_call_target="tpu_custom_call" | custom-call | flops 268435456 | bytes 2097152 | tf_op jit(solution)/shard_map/project/pallas_call | solution.py:335
Async XLA Ops:
  6.5 82.5 %all-gather.4.cloned.1.call-start = ((), (), s32[]{:S(2)}) async-start(), calls=%async_computation.2 | async-start | bytes 8912896 | tf_op jit(solution)/shard_map/all_gather | solution.py:370
  7.4 17.3 %collective-permute-start = (bf16[3,2,1024]{2,1,0:T(2,128)(2,1)S(1)}, bf16[3,2,1024]{2,1,0:T(2,128)(2,1)S(1)}, u32[]{:S(2)}, u32[]{:S(2)}) collective-permute-start(bf16[3,2,1024]{2,1,0:T(2,128)(2,1)S(1)} %slice.4), channel_id=1, source_target_pairs={{0,8},{8,16},{16,24},{24,32},{32,40},{40,48},{48,56},{56,64},{64,7... | collective-permute-start | bytes 36872 | tf_op jit(solution)/shard_map/ppermute | solution.py:356
  24.7 0.6 copy-start.6
  50.6 14.7 %all-to-all-start.1 = ((f32[64,2,128]{2,1,0:T(2,128)}), f32[64,2,128]{2,1,0:T(2,128)S(1)}, u32[]{:S(2)}, u32[]{:S(2)}) async-start(f32[64,2,128]{2,1,0:T(2,128)} %scan_blocks.1), calls=%async_computation.1 | async-start | bytes 131072 | tf_op jit(solution)/shard_map/all_to_all | solution.py:378
  55.0 0.7 copy-start.2
  55.6 1.1 copy-start.3
  56.7 1.1 copy-start.4
  57.7 0.7 copy-start.5
  65.6 18.2 %collective-permute-start.3 = (bf16[128,1024]{1,0:T(8,128)(2,1)S(1)}, bf16[128,1024]{1,0:T(8,128)(2,1)S(1)}, u32[]{:S(2)}, u32[]{:S(2)}) collective-permute-start(bf16[128,1024]{1,0:T(8,128)(2,1)S(1)} %gate.1.refs_0_), channel_id=1, source_target_pairs={{0,4},{2,6},{4,0},{6,2},{1,5},{3,7},{5,1},{7,3},{8,12},{10,14},{12... | collective-permute-start | bytes 786440 | tf_op jit(solution)/shard_map/ppermute | solution.py:356
  76.3 18.2 %collective-permute-start.2 = (bf16[128,1024]{1,0:T(8,128)(2,1)S(1)}, bf16[128,1024]{1,0:T(8,128)(2,1)S(1)}, u32[]{:S(2)}, u32[]{:S(2)}) collective-permute-start(bf16[128,1024]{1,0:T(8,128)(2,1)S(1)} %gate.1.refs_0_), channel_id=1, source_target_pairs={{0,2},{2,4},{4,6},{6,0},{1,3},{3,5},{5,7},{7,1},{8,10},{10,12},{12... | collective-permute-start | bytes 786440 | tf_op jit(solution)/shard_map/ppermute | solution.py:356
  80.3 20.7 %collective-permute-start.1 = (bf16[128,1024]{1,0:T(8,128)(2,1)S(1)}, bf16[128,1024]{1,0:T(8,128)(2,1)S(1)}, u32[]{:S(2)}, u32[]{:S(2)}) collective-permute-start(bf16[128,1024]{1,0:T(8,128)(2,1)S(1)} %gate.1.refs_0_), channel_id=1, source_target_pairs={{0,6},{2,0},{4,2},{6,4},{1,7},{3,1},{5,3},{7,5},{8,14},{10,8},{12,... | collective-permute-start | bytes 786440 | tf_op jit(solution)/shard_map/ppermute | solution.py:356
  89.0 3.4 %copy-start = (bf16[64,64,1024]{2,1,0:T(8,128)(2,1)S(1)}, bf16[64,64,1024]{2,1,0:T(8,128)(2,1)}, u32[]{:S(2)}) copy-start(bf16[64,64,1024]{2,1,0:T(8,128)(2,1)} %all-gather.4.cloned.1.call-done) | copy-start | bytes 25165828
  92.4 3.4 %copy-start.1 = (bf16[64,64,1024]{2,1,0:T(8,128)(2,1)S(1)}, bf16[64,64,1024]{2,1,0:T(8,128)(2,1)}, u32[]{:S(2)}) copy-start(bf16[64,64,1024]{2,1,0:T(8,128)(2,1)} %all-gather.4.cloned.1.call-done) | copy-start | bytes 25165828
Sparse Core Ops, SparseCore 0:
  24.8 64.1 all-gather.3
